TPU v7x, 32 devices: a whole 2x2x4 slice. The times are simulated.
32 devices in a mesh: dp: 4 (over x, core), row: 2 (over y), col: 4 (over z).
Axes of the slice: x: 2, y: 2, z: 4, core: 2. Of those that a mesh axis runs over, the one named last changes fastest.
Arguments:
- inputs: bfloat16 [8192, 1536], P(('dp', 'col'), 'row'), may hold values from -6 to 6
- norm_gain: float32 [1536], P('row'), may hold values from 0.25 to 1.75
- query_weight: bfloat16 [1536, 1536], P('row', 'col'), may hold values from -0.15625 to 0.15625
- key_value_matrix: bfloat16 [1536, 512], P('row', 'col'), may hold values from -0.15625 to 0.15625
- output_weight: bfloat16 [1536, 1536], P('col', 'row'), may hold values from -0.625 to 0.625
- mixer_gain: float32 [1536], P('row'), may hold values from 0.25 to 1.75
- gate_weight: bfloat16 [8, 1536, 768], P(None, 'row', 'col'), may hold values from -0.15625 to 0.15625
- up_weight: bfloat16 [8, 1536, 768], P(None, 'row', 'col'), may hold values from -0.15625 to 0.15625
- down_weight: bfloat16 [8, 768, 1536], P(None, 'col', 'row'), may hold values from -0.4375 to 0.4375
- lengths: int32 [8, 4], P(('dp', 'row')), may hold values from 1 to 512, 1024 in all within a row
- routes: int32 [8192, 4], P('dp'), may hold values from 0 to 7, all different within a row; in each aligned block of 2048 rows (0 to 2047, 2048 to 4095, ...) at most 1536 rows name the same one
- route_gates: float32 [8192, 4], P('dp'), may hold values from 0.1 to 1
- cotangent: bfloat16 [8192, 1536], P(('dp', 'col'), 'row'), may hold values from -6 to 6
Outputs:
- outputs: bfloat16 [8192, 1536], P(('dp', 'col'), 'row')
- input_grad: bfloat16 [8192, 1536], P(('dp', 'col'), 'row')
- norm_gain_grad: float32 [1536], P('row')
- query_weight_grad: float32 [1536, 1536], P('row', 'col')
- key_value_weight_grad: float32 [1536, 512], P('row', 'col')
- output_weight_grad: float32 [1536, 1536], P('col', 'row')
- mixer_gain_grad: float32 [1536], P('row')
- gate_weight_grad: float32 [8, 1536, 768], P(None, 'row', 'col')
- up_weight_grad: float32 [8, 1536, 768], P(None, 'row', 'col')
- down_weight_grad: float32 [8, 768, 1536], P(None, 'col', 'row')
Inputs may be any that keep to these rules, and one draw needn't show every extreme that they name: Each row holds the lengths of the 4 sequences of one block in order; they sum to 1024 and the longest is exactly 512. `routes`: A token's 4 experts differ. Within the rows of one data index (aligned blocks of 2048 rows) no expert is named more than 1536 times, a bound that some block reaches.
All inputs are finite; a program needn't handle non-finite values.
Results may differ from a plain program's by a relative error of at most 0.025.
Values may be sent and summed in bfloat16 or wider, within the bound.
A program may use at most 320 MiB of HBM per device.

v0:
```python
import math

import jax
import jax.numpy as jnp
from jax import lax
from jax.sharding import PartitionSpec as P

MODEL_DIM = 1536
HEAD_SIZE = 128


epsilon = 1e-06
rope_base = 1000000.0


def partner_2(block, axis, apart):
    count = lax.axis_size(axis)
    route = []
    for low in range(count):
        high = low | 1 << apart
        if high != low and high < count:
            route += [(low, high), (high, low)]
    return lax.ppermute(block, axis, route)


def row_stat(partial_value):
    return lax.psum(partial_value, "row")


def col_rows(matrix):
    return lax.all_gather(matrix, "col", axis=0, tiled=True)


def col_sums(matrix):
    return lax.psum_scatter(
        matrix.astype(jnp.bfloat16), "col", scatter_dimension=0, tiled=True
    ).astype(jnp.float32)


def row_sums(matrix):
    return lax.psum_scatter(matrix, "row", scatter_dimension=0, tiled=True)


def row_rows(matrix):
    return lax.all_gather(matrix, "row", axis=0, tiled=True)


def norm_forward(matrix, gain_part, model_width):
    square_sum = row_stat(jnp.sum(matrix * matrix, axis=1, keepdims=True))
    row_scale = lax.rsqrt(square_sum / model_width + epsilon)
    return (row_scale, (matrix * row_scale * gain_part).astype(jnp.bfloat16))


def norm_backward(upstream, matrix, row_scale, gain_part, model_width):
    weighted = gain_part * upstream
    inner_sum = row_stat(jnp.sum(weighted * matrix, axis=1, keepdims=True))
    grad_rows = (
        row_scale * weighted
        - matrix * (row_scale * row_scale * row_scale) * inner_sum / model_width
    )
    gain_partial = jnp.sum(upstream * matrix * row_scale, axis=0)
    return (grad_rows, gain_partial)


def frequencies(head_dim):
    return rope_base ** (-jnp.arange(0, head_dim, 2, dtype=jnp.float32) / head_dim)


def rotate(matrix, cosine, sine_rows):
    half_dim = matrix.shape[-1] // 2
    first_half = matrix[..., :half_dim]
    second = matrix[..., half_dim:]
    return jnp.concatenate(
        [first_half * cosine - second * sine_rows, second * cosine + first_half * sine_rows],
        axis=-1,
    )


def positions(lengths_row, per_half_columns):
    seq_ends = jnp.cumsum(lengths_row)
    token_index = jnp.arange(per_half_columns, dtype=jnp.int32)
    segment = jnp.sum((token_index[:, None] >= seq_ends[None, :]).astype(jnp.int32), axis=1)
    starts = seq_ends - lengths_row
    picked = segment[:, None] == jnp.arange(lengths_row.shape[0], dtype=jnp.int32)[None, :]
    seq_begin = jnp.sum(jnp.where(picked, starts[None, :], 0), axis=1)
    return (segment, token_index - seq_begin)


def block_scores(queries, key_rows, segment, position, number, block_rows):
    first_row = number * block_rows
    query_block = lax.dynamic_slice_in_dim(queries, first_row, block_rows, 0)
    seg_block = lax.dynamic_slice_in_dim(segment, first_row, block_rows, 0)
    pos_block = lax.dynamic_slice_in_dim(position, first_row, block_rows, 0)
    raw_scores = jnp.einsum(
        "qhd,kd->hqk", query_block, key_rows, preferred_element_type=jnp.float32
    )
    allowed = (seg_block[:, None] == segment[None, :]) & (position[None, :] <= pos_block[:, None])
    scores = jnp.where(allowed[None], raw_scores * queries.shape[2] ** (-0.5), -1e30)
    return (query_block, scores)


def attention_forward(queries, key_rows, value_rows, segment, position, block_rows):
    blocks = queries.shape[0] // block_rows

    def one_block(number):
        query_block, scores = block_scores(queries, key_rows, segment, position, number, block_rows)
        row_max = jnp.max(scores, axis=2, keepdims=True)
        exponent = jnp.exp(scores - row_max)
        totals = jnp.sum(exponent, axis=2, keepdims=True)
        weights = (exponent / totals).astype(jnp.bfloat16)
        mixed_rows = jnp.einsum(
            "hqk,kd->qhd", weights, value_rows, preferred_element_type=jnp.float32
        )
        return (mixed_rows, (row_max + jnp.log(totals))[:, :, 0])

    mixed_rows, logsum = lax.map(one_block, jnp.arange(blocks, dtype=jnp.int32))
    return (mixed_rows.reshape(queries.shape[0], -1), logsum)


def attention_backward(
    queries, key_rows, value_rows, segment, position, logsum, grad_out, block_rows
):
    blocks = queries.shape[0] // block_rows
    score_scale = queries.shape[2] ** (-0.5)

    def one_block(running, number):
        key_grad, value_grad = running
        query_block, scores = block_scores(queries, key_rows, segment, position, number, block_rows)
        probs = jnp.exp(scores - logsum[number][:, :, None])
        grad_block = lax.dynamic_slice_in_dim(grad_out, number * block_rows, block_rows, 0)
        prob_grad = jnp.einsum(
            "qhd,kd->hqk", grad_block, value_rows, preferred_element_type=jnp.float32
        )
        inner_sum = jnp.sum(probs * prob_grad, axis=2, keepdims=True)
        score_grad = (probs * (prob_grad - inner_sum) * score_scale).astype(jnp.bfloat16)
        query_grad = jnp.einsum(
            "hqk,kd->qhd", score_grad, key_rows, preferred_element_type=jnp.float32
        )
        key_grad = key_grad + jnp.einsum(
            "hqk,qhd->kd", score_grad, query_block, preferred_element_type=jnp.float32
        )
        value_grad = value_grad + jnp.einsum(
            "hqk,qhd->kd",
            probs.astype(jnp.bfloat16),
            grad_block,
            preferred_element_type=jnp.float32,
        )
        return ((key_grad, value_grad), query_grad)

    zeros_rows = jnp.zeros(key_rows.shape, jnp.float32)
    totals, query_grads = lax.scan(
        one_block, (zeros_rows, zeros_rows), jnp.arange(blocks, dtype=jnp.int32)
    )
    return (query_grads.reshape(queries.shape), totals[0], totals[1])


def slotted_product(left, stack, form, experts):
    shaped = left.reshape(-1, experts, left.shape[1])
    result = jax.vmap(
        lambda piece, weight: jnp.einsum(form, piece, weight, preferred_element_type=jnp.float32),
        in_axes=(1, 0),
        out_axes=1,
    )(shaped, stack)
    return result.reshape(left.shape[0], -1)


def slotted_grad(left, right, form, experts):
    shaped_left = left.reshape(-1, experts, left.shape[1])
    shaped_right = right.reshape(-1, experts, right.shape[1])
    return jax.vmap(
        lambda first, second: jnp.einsum(form, first, second, preferred_element_type=jnp.float32),
        in_axes=(1, 1),
        out_axes=0,
    )(shaped_left, shaped_right)


def shards(
    inputs,
    norm_gain,
    query_weight,
    key_value_matrix,
    output_weight,
    mixer_gain,
    gate_weight,
    up_weight,
    down_weight,
    lengths,
    routes,
    route_gates,
    cotangent,
):
    model_width = MODEL_DIM
    head_dim = HEAD_SIZE
    query_cols = query_weight.shape[1]
    experts = gate_weight.shape[0]
    group_rows = routes.shape[0]
    top_count = routes.shape[1]
    capacity = 3 * group_rows * top_count // (2 * experts)
    even_col = lax.axis_index("col") % 2 == 0
    input_rows = inputs.astype(jnp.float32)
    first_scale, first_normed = norm_forward(input_rows, norm_gain, model_width)
    normed_all = col_rows(first_normed)
    joint_weight = jnp.concatenate([query_weight, key_value_matrix], axis=1)
    projected = row_sums(jnp.dot(normed_all, joint_weight, preferred_element_type=jnp.float32))
    per_half_columns = projected.shape[0]
    segment, position = positions(lengths[0], per_half_columns)
    angles = position.astype(jnp.float32)[:, None] * frequencies(head_dim)[None, :]
    cosine = jnp.cos(angles)[:, None, :]
    sine_rows = jnp.sin(angles)[:, None, :]
    queries = rotate(
        projected[:, :query_cols].reshape(per_half_columns, -1, head_dim), cosine, sine_rows
    ).astype(jnp.bfloat16)
    own_block = projected[:, query_cols:].reshape(per_half_columns, 1, head_dim)
    own_rounded = (
        jnp.where(even_col, rotate(own_block, cosine, sine_rows), own_block)
        .reshape(per_half_columns, head_dim)
        .astype(jnp.bfloat16)
    )
    partner = partner_2(own_rounded, "col", 0)
    key_rows = jnp.where(even_col, own_rounded, partner)
    value_rows = jnp.where(even_col, partner, own_rounded)
    block_rows = math.gcd(per_half_columns, 512)
    attended, logsum = attention_forward(
        queries, key_rows, value_rows, segment, position, block_rows
    )
    attended = attended.astype(jnp.bfloat16)
    attended_all = row_rows(attended)
    branch = col_sums(jnp.dot(attended_all, output_weight, preferred_element_type=jnp.float32))
    middle = input_rows + branch
    second_scale, second_normed = norm_forward(middle, mixer_gain, model_width)
    expert_in = col_rows(second_normed)
    flat_routes = routes.reshape(-1)
    onehot = (flat_routes[:, None] == jnp.arange(experts, dtype=jnp.int32)[None, :]).astype(
        jnp.int32
    )
    slot_index = jnp.sum((jnp.cumsum(onehot, axis=0) - 1) * onehot, axis=1)
    slot_rows = capacity * experts
    target = slot_index * experts + flat_routes

    def expert_product(left, stack, form):
        return slotted_product(left, stack, form, experts)

    def expert_grad(left, right, form):
        return slotted_grad(left, right, form, experts)

    source = jnp.arange(flat_routes.shape[0], dtype=jnp.int32) // top_count
    feature_cols = expert_in.shape[1]
    buffer = jnp.zeros((slot_rows, feature_cols), jnp.bfloat16).at[target].set(expert_in[source])
    unit_cols = gate_weight.shape[2]
    joint_expert = jnp.concatenate([gate_weight, up_weight], axis=2)
    joint_part = expert_product(buffer, joint_expert, "td,df->tf")
    shares = row_sums(joint_part)
    split_at = shares.shape[1] // 2
    gate_share = shares[:, :split_at]
    up_share = shares[:, split_at:]
    sigmoid_gate = jax.nn.sigmoid(gate_share)
    silu_gate = gate_share * sigmoid_gate
    hidden_share = (silu_gate * up_share).astype(jnp.bfloat16)
    hidden_all = row_rows(hidden_share)
    down_part = expert_product(hidden_all, down_weight, "tf,fd->td")
    routed = down_part[target].reshape(group_rows, top_count, -1)
    combined = jnp.sum(routed * route_gates[:, :, None], axis=1)
    experts_out = col_sums(combined)
    outputs = (middle + experts_out).astype(jnp.bfloat16)
    cot_rows = cotangent.astype(jnp.float32)
    cot_all = col_rows(cotangent)
    route_grad = (
        (route_gates[:, :, None] * cot_all[:, None, :].astype(jnp.float32))
        .astype(jnp.bfloat16)
        .reshape(group_rows * top_count, -1)
    )
    grad_buffer = jnp.zeros((slot_rows, feature_cols), jnp.bfloat16).at[target].set(route_grad)
    down_grad = expert_grad(hidden_all, grad_buffer, "tf,td->fd")
    hidden_part = expert_product(grad_buffer, down_weight, "td,fd->tf")
    hidden_grad = row_sums(hidden_part)
    gate_grad_share = (
        hidden_grad * up_share * (sigmoid_gate * (1.0 + gate_share * (1.0 - sigmoid_gate)))
    )
    up_grad_share = hidden_grad * silu_gate
    joint_grad_share = jnp.concatenate(
        [gate_grad_share.astype(jnp.bfloat16), up_grad_share.astype(jnp.bfloat16)], axis=1
    )
    joint_grad = row_rows(joint_grad_share)
    joint_expert_grad = expert_grad(buffer, joint_grad, "td,tf->df")
    gate_grad = joint_expert_grad[:, :, :unit_cols]
    up_grad = joint_expert_grad[:, :, unit_cols:]
    in_part = expert_product(joint_grad, joint_expert, "tf,df->td")
    in_routed = jnp.sum(in_part[target].reshape(group_rows, top_count, -1), axis=1)
    second_grad = col_sums(in_routed)
    mixer_rows, mixer_partial = norm_backward(
        second_grad, middle, second_scale, mixer_gain, model_width
    )
    middle_grad = cot_rows + mixer_rows
    branch_grad_all = col_rows(middle_grad.astype(jnp.bfloat16))
    output_grad = jnp.einsum(
        "tq,td->qd", attended_all, branch_grad_all, preferred_element_type=jnp.float32
    )
    attended_grad = row_sums(
        jnp.einsum("td,qd->tq", branch_grad_all, output_weight, preferred_element_type=jnp.float32)
    ).astype(jnp.bfloat16)
    query_grad, key_grad, value_grad = attention_backward(
        queries,
        key_rows,
        value_rows,
        segment,
        position,
        logsum,
        attended_grad.reshape(per_half_columns, -1, head_dim),
        block_rows,
    )
    query_pre = (
        rotate(query_grad, cosine, -sine_rows).reshape(per_half_columns, -1).astype(jnp.bfloat16)
    )
    own_grad = jnp.where(even_col, key_grad, value_grad)
    other_grad = jnp.where(even_col, value_grad, key_grad)
    returned = partner_2(other_grad.astype(jnp.bfloat16), "col", 0).astype(other_grad.dtype)
    own_total = own_grad + returned
    own_pre = jnp.where(
        even_col, rotate(own_total[:, None, :], cosine, -sine_rows)[:, 0, :], own_total
    ).astype(jnp.bfloat16)
    joint_grad_rows = row_rows(jnp.concatenate([query_pre, own_pre], axis=1))
    joint_weight_grad = jnp.einsum(
        "td,tf->df", normed_all, joint_grad_rows, preferred_element_type=jnp.float32
    )
    first_grad = col_sums(
        jnp.einsum("tf,df->td", joint_grad_rows, joint_weight, preferred_element_type=jnp.float32)
    )
    first_rows, norm_partial = norm_backward(
        first_grad, input_rows, first_scale, norm_gain, model_width
    )
    input_grad = (middle_grad + first_rows).astype(jnp.bfloat16)
    query_part = joint_weight_grad[:, :query_cols]
    keyval_part = joint_weight_grad[:, query_cols:]
    (
        query_total,
        keyval_total,
        output_total,
        norm_total,
        mixer_total,
        gate_total,
        up_total,
        down_total,
    ) = (
        lax.psum(query_part.astype(jnp.bfloat16), "dp").astype(jnp.float32),
        lax.psum(keyval_part.astype(jnp.bfloat16), "dp").astype(jnp.float32),
        lax.psum(output_grad.astype(jnp.bfloat16), "dp").astype(jnp.float32),
        lax.psum(norm_partial.astype(jnp.bfloat16), "dp").astype(jnp.float32),
        lax.psum(mixer_partial.astype(jnp.bfloat16), "dp").astype(jnp.float32),
        lax.psum(gate_grad.astype(jnp.bfloat16), "dp").astype(jnp.float32),
        lax.psum(up_grad.astype(jnp.bfloat16), "dp").astype(jnp.float32),
        lax.psum(down_grad.astype(jnp.bfloat16), "dp").astype(jnp.float32),
    )
    norm_total, mixer_total = lax.psum((norm_total, mixer_total), "col")
    return (
        outputs,
        input_grad,
        norm_total,
        query_total,
        keyval_total,
        output_total,
        mixer_total,
        gate_total,
        up_total,
        down_total,
    )


def solution(mesh):
    return jax.shard_map(
        shards,
        mesh=mesh,
        in_specs=(
            P(("dp", "col"), "row"),
            P("row"),
            P("row", "col"),
            P("row", "col"),
            P("col", "row"),
            P("row"),
            P(None, "row", "col"),
            P(None, "row", "col"),
            P(None, "col", "row"),
            P(("dp", "row"), None),
            P("dp", None),
            P("dp", None),
            P(("dp", "col"), "row"),
        ),
        out_specs=(
            P(("dp", "col"), "row"),
            P(("dp", "col"), "row"),
            P("row"),
            P("row", "col"),
            P("row", "col"),
            P("col", "row"),
            P("row"),
            P(None, "row", "col"),
            P(None, "row", "col"),
            P(None, "col", "row"),
        ),
        check_vma=False,
    )
```

profile of v0, /device:TPU:17, one launch (start us, length us, event | category | flops | bytes accessed | tf_op | source)
XLA Modules:
  0.0 1890.4 jit_solution(17957822765934526680)
XLA Ops:
  18.2 62.4 %all-gather.9.cloned.1.call-done = bf16[2048,768]{1,0:T(8,128)(2,1)} async-done(((bf16[512,768]{1,0:T(8,128)(2,1)}), bf16[2048,768]{1,0:T(8,128)(2,1)}) %all-gather.9.cloned.1.call-update) | async-done | bytes 3145744 | tf_op jit(solution)/shard_map/all_gather | solution.py:31
  88.5 52.2 %reduce-scatter.9.cloned.1.call-done = f32[1024,512]{1,0:T(8,128)} async-done(((f32[2048,512]{1,0:T(8,128)}), f32[1024,512]{1,0:T(8,128)}) %reduce-scatter.9.cloned.1.call-update) | async-done | bytes 2097168 | tf_op jit(solution)/shard_map/reduce_scatter | solution.py:41
  183.6 28.2 %all-gather.11.cloned.1.call-done = bf16[2048,384]{0,1:T(8,128)(2,1)} async-done(((bf16[1024,384]{0,1:T(8,128)(2,1)}), bf16[2048,384]{0,1:T(8,128)(2,1)}) %all-gather.11.cloned.1.call-update) | async-done | bytes 1572880 | tf_op jit(solution)/shard_map/all_gather | solution.py:45
  226.7 50.6 %reduce-scatter.11.cloned.1.call-done = bf16[512,768]{1,0:T(8,128)(2,1)} async-done(((bf16[2048,768]{1,0:T(8,128)(2,1)}), bf16[512,768]{1,0:T(8,128)(2,1)}) %reduce-scatter.11.cloned.1.call-update) | async-done | bytes 786448 | tf_op jit(solution)/shard_map/reduce_scatter | solution.py:35
  292.7 48.3 %all-gather.17.cloned.1.call-done = bf16[2048,768]{1,0:T(8,128)(2,1)} async-done(((bf16[512,768]{1,0:T(8,128)(2,1)}), bf16[2048,768]{1,0:T(8,128)(2,1)}) %all-gather.17.cloned.1.call-update) | async-done | bytes 3145744 | tf_op jit(solution)/shard_map/all_gather | solution.py:31
  353.9 29.1 %mul.403 = f32[8192,768]{1,0:T(8,128)} reshape(f32[2048,4,768]{2,1,0:T(4,128)} %mul.402) | data formatting | bytes 50331648 | tf_op jit(solution)/shard_map/mul | solution.py:268
  382.9 58.4 %scatter_custom_fusion.1 = bf16[12288,768]{1,0:T(8,128)(2,1)} fusion(s32[8192]{0:T(1024)S(1)} %bitcast.267, f32[8192,768]{1,0:T(8,128)} %mul.403, f32[8192]{0:T(1024)S(1)} %mul.400, bf16[]{:T(256)} %constant.109.clone.1), kind=kCustom, calls=%fused_computation.79 | custom fusion | flops 12582912 | bytes 44072960 | tf_op jit(solution)/shard_map/scatter | solution.py:272
  482.9 111.2 %scatter_custom_fusion = bf16[12288,768]{1,0:T(8,128)(2,1)} fusion(s32[8192]{0:T(1024)S(1)} %bitcast.268, bf16[2048,768]{1,0:T(8,128)(2,1)} %all-gather.13.cloned.1.call-done, s32[8192]{0:T(1024)S(1)} %broadcast_clamp_fusion.1, bf16[]{:T(256)} %constant.109.clone.1), kind=kCustom, calls=%fused_computation.80 | custom fusion | bytes 18874880 | tf_op jit(solution)/shard_map/scatter | solution.py:248
  617.2 24.8 %copy.133 = f32[1536,8,384]{2,1,0:T(8,128)} copy(f32[1536,8,384]{2,0,1:T(8,128)} %fusion.69) | data formatting | bytes 37748736 | tf_op jit(solution)/shard_map/vmap()/transpose | solution.py:159
  642.6 211.3 %reduce-scatter.13.cloned.1.call-done = f32[6144,384]{1,0:T(8,128)} async-done(((f32[12288,384]{1,0:T(8,128)}), f32[6144,384]{1,0:T(8,128)}) %reduce-scatter.13.cloned.1.call-update) | async-done | bytes 9437200 | tf_op jit(solution)/shard_map/reduce_scatter | solution.py:41
  867.6 118.1 %all-gather.19.cloned.1.call-done = bf16[12288,384]{1,0:T(8,128)(2,1)} async-done(((bf16[6144,384]{1,0:T(8,128)(2,1)}), bf16[12288,384]{1,0:T(8,128)(2,1)}) %all-gather.19.cloned.1.call-update) | async-done | bytes 9437200 | tf_op jit(solution)/shard_map/all_gather | solution.py:45
  1020.6 35.6 %copy.131 = f32[1536,8,768]{2,1,0:T(8,128)} copy(f32[1536,8,768]{2,0,1:T(8,128)} %convolution_bitcast_fusion.3) | data formatting | bytes 75497472 | tf_op jit(solution)/shard_map/vmap()/transpose | solution.py:159
  1056.1 51.2 %gather_fusion.1 = f32[8192,768]{1,0:T(8,128)} fusion(f32[12288,768]{1,0:T(8,128)} %bitcast.252, s32[8192]{0:T(1024)S(1)} %broadcast_clamp_fusion), kind=kCustom, calls=%fused_computation.2 | custom fusion | bytes 50364416 | tf_op jit(solution)/shard_map/gather | solution.py:288
  1107.3 28.6 %reshape.492 = f32[2048,4,768]{2,1,0:T(4,128)} reshape(f32[8192,768]{1,0:T(8,128)} %gather_fusion.1) | data formatting | bytes 50331648 | tf_op jit(solution)/shard_map/reshape | solution.py:288
  1136.0 36.3 %reduce_sum.123 = bf16[2048,768]{1,0:T(8,128)(2,1)} reduce(f32[2048,4,768]{2,1,0:T(4,128)} %reshape.492, f32[]{:T(128)} %constant.100.clone.1), dimensions={1}, to_apply=%region_22.23 | reduce | flops 4718592 | bytes 28311556 | tf_op jit(solution)/shard_map/reduce_sum | solution.py:288
  1172.4 60.5 %reduce-scatter.19.cloned.1.call-done = bf16[512,768]{1,0:T(8,128)(2,1)} async-done(((bf16[2048,768]{1,0:T(8,128)(2,1)}), bf16[512,768]{1,0:T(8,128)(2,1)}) %reduce-scatter.19.cloned.1.call-update) | async-done | bytes 786448 | tf_op jit(solution)/shard_map/reduce_scatter | solution.py:35
  1243.1 62.8 %all-gather.21.cloned.1.call-done = bf16[2048,768]{1,0:T(8,128)(2,1)} async-done(((bf16[512,768]{1,0:T(8,128)(2,1)}), bf16[2048,768]{1,0:T(8,128)(2,1)}) %all-gather.21.cloned.1.call-update) | async-done | bytes 3145744 | tf_op jit(solution)/shard_map/all_gather | solution.py:31
  1311.5 76.3 %all-gather.15.cloned.1.call-done = bf16[12288,192]{1,0:T(8,128)(2,1)} async-done(((bf16[6144,192]{1,0:T(8,128)(2,1)}), bf16[12288,192]{1,0:T(8,128)(2,1)}) %all-gather.15.cloned.1.call-update) | async-done | bytes 4718608 | tf_op jit(solution)/shard_map/all_gather | solution.py:45
  1438.7 98.2 %while.28 = (s32[]{:T(128)}, f32[1024,128]{1,0:T(8,128)}, f32[1024,128]{1,0:T(8,128)}, f32[2,512,3,128]{3,1,0,2:T(8,128)}, s32[2]{0:T(128)S(1)}, /*index=5*/s32[...) while((s32[]{:T(128)}, f32[1024,128]{1,0:T(8,128)}, ...), condition=%wide.region_29.30_spmd.clone, body=%wide.region_27.29_spmd.clone.sunk | while | flops 2056262656 | bytes 109126048 | solution.py:151
  1621.2 36.0 %copy.132 = f32[1536,8,768]{2,1,0:T(8,128)} copy(f32[1536,8,768]{2,0,1:T(8,128)} %convolution_bitcast_fusion.2) | data formatting | bytes 75497472 | tf_op jit(solution)/shard_map/vmap()/transpose | solution.py:159
  1657.2 51.4 %gather_fusion = f32[8192,768]{1,0:T(8,128)} fusion(f32[12288,768]{1,0:T(8,128)} %bitcast.251, s32[8192]{0:T(1024)S(1)} %copy-done.30), kind=kCustom, calls=%fused_computation.1 | custom fusion | bytes 50364416 | tf_op jit(solution)/shard_map/gather | solution.py:261
  1708.6 28.9 %reshape.487 = f32[2048,4,768]{2,1,0:T(4,128)} reshape(f32[8192,768]{1,0:T(8,128)} %gather_fusion) | data formatting | bytes 50331648 | tf_op jit(solution)/shard_map/reshape | solution.py:261
  1772.2 44.5 %reduce-scatter.23.cloned.1.call-done = bf16[512,768]{1,0:T(8,128)(2,1)} async-done(((bf16[2048,768]{1,0:T(8,128)(2,1)}), bf16[512,768]{1,0:T(8,128)(2,1)}) %reduce-scatter.23.cloned.1.call-update) | async-done | bytes 786448 | tf_op jit(solution)/shard_map/reduce_scatter | solution.py:35
  1836.7 43.0 %reduce-scatter.15.cloned.1.call-done = bf16[512,768]{1,0:T(8,128)(2,1)} async-done(((bf16[2048,768]{1,0:T(8,128)(2,1)}), bf16[512,768]{1,0:T(8,128)(2,1)}) %reduce-scatter.15.cloned.1.call-update) | async-done | bytes 786448 | tf_op jit(solution)/shard_map/reduce_scatter | solution.py:35
  (311 shorter events, 535.6 us)
Async XLA Ops:
  7.2 434.2 %copy-start = (bf16[8,192,768]{2,1,0:T(8,128)(2,1)S(1)}, bf16[8,192,768]{2,1,0:T(8,128)(2,1)}, u32[]{:S(2)}) copy-start(bf16[8,192,768]{2,1,0:T(8,128)(2,1)} %param.25) | copy-start | bytes 7077892
  7.2 73.4 %all-gather.9.cloned.1.call-start = ((), (), s32[]{:S(2)}) async-start(), calls=%async_computation.8 | async-start | bytes 3932160 | tf_op jit(solution)/shard_map/all_gather | solution.py:31
  16.0 124.7 %reduce-scatter.9.cloned.1.call-start = ((), (), s32[]{:S(2)}) async-start(), calls=%async_computation.9 | async-start | bytes 6291456 | tf_op jit(solution)/shard_map/reduce_scatter | solution.py:41
  86.3 125.5 %all-gather.11.cloned.1.call-start = ((), (), s32[]{:S(2)}) async-start(), calls=%async_computation.10 | async-start | bytes 2359296 | tf_op jit(solution)/shard_map/all_gather | solution.py:45
  151.8 7.5 collective-permute-start
  183.5 93.8 %reduce-scatter.11.cloned.1.call-start = ((), (), s32[]{:S(2)}) async-start(), calls=%async_computation.11 | async-start | bytes 3932160 | tf_op jit(solution)/shard_map/reduce_scatter | solution.py:35
  216.9 124.1 %all-gather.17.cloned.1.call-start = ((), (), s32[]{:S(2)}) async-start(), calls=%async_computation.16 | async-start | bytes 3932160 | tf_op jit(solution)/shard_map/all_gather | solution.py:31
  217.4 265.4 %all-gather.13.cloned.1.call-start = ((), (), s32[]{:S(2)}) async-start(), calls=%async_computation.12 | async-start | bytes 3932160 | tf_op jit(solution)/shard_map/all_gather | solution.py:31
  285.5 357.0 %reduce-scatter.17.cloned.1.call-start = ((), (), s32[]{:S(2)}) async-start(), calls=%async_computation.17 | async-start | bytes 18874368 | tf_op jit(solution)/shard_map/reduce_scatter | solution.py:41
  473.3 380.6 %reduce-scatter.13.cloned.1.call-start = ((), (), s32[]{:S(2)}) async-start(), calls=%async_computation.13 | async-start | bytes 28311552 | tf_op jit(solution)/shard_map/reduce_scatter | solution.py:41
  642.1 343.6 %all-gather.19.cloned.1.call-start = ((), (), s32[]{:S(2)}) async-start(), calls=%async_computation.18 | async-start | bytes 14155776 | tf_op jit(solution)/shard_map/all_gather | solution.py:45
  867.5 365.4 %reduce-scatter.19.cloned.1.call-start = ((), (), s32[]{:S(2)}) async-start(), calls=%async_computation.19 | async-start | bytes 3932160 | tf_op jit(solution)/shard_map/reduce_scatter | solution.py:35
  867.6 188.6 %copy-start.29 = (s32[8192]{0:T(1024)}, s32[8192]{0:T(1024)S(1)}, u32[]{:S(2)}) copy-start(s32[8192]{0:T(1024)S(1)} %broadcast_clamp_fusion) | copy-start | bytes 98308
  1172.3 133.5 %all-gather.21.cloned.1.call-start = ((), (), s32[]{:S(2)}) async-start(), calls=%async_computation.20 | async-start | bytes 3932160 | tf_op jit(solution)/shard_map/all_gather | solution.py:31
  1242.5 145.3 %all-gather.15.cloned.1.call-start = ((), (), s32[]{:S(2)}) async-start(), calls=%async_computation.14 | async-start | bytes 9437184 | tf_op jit(solution)/shard_map/all_gather | solution.py:45
  1243.0 191.0 %reduce-scatter.21.cloned.1.call-start = ((), (), s32[]{:S(2)}) async-start(), calls=%async_computation.21 | async-start | bytes 4718592 | tf_op jit(solution)/shard_map/reduce_scatter | solution.py:41
  1311.4 280.8 %all-gather.23.cloned.1.call-start = ((), (), s32[]{:S(2)}) async-start(), calls=%async_computation.22 | async-start | bytes 3145728 | tf_op jit(solution)/shard_map/all_gather | solution.py:45
  1538.7 13.5 collective-permute-start.1
  1557.5 200.4 %all-reduce.5.cloned.1.call-start = ((), (), s32[]{:S(2)}) async-start(), calls=%async_computation.24 | async-start | bytes 16908288 | tf_op jit(solution)/shard_map/psum | solution.py:344
  1598.2 218.6 %reduce-scatter.23.cloned.1.call-start = ((), (), s32[]{:S(2)}) async-start(), calls=%async_computation.23 | async-start | bytes 3932160 | tf_op jit(solution)/shard_map/reduce_scatter | solution.py:35
  1603.7 276.0 %reduce-scatter.15.cloned.1.call-start = ((), (), s32[]{:S(2)}) async-start(), calls=%async_computation.15 | async-start | bytes 3932160 | tf_op jit(solution)/shard_map/reduce_scatter | solution.py:35
  1769.5 110.2 %copy-start.37 = (f32[768]{0:T(1024)S(1)}, f32[768]{0:T(1024)}, u32[]{:S(2)}) copy-start(f32[768]{0:T(1024)} %param.22) | copy-start | bytes 9220
  1769.5 110.2 %copy-start.40 = (f32[512,1]{0,1:T(1,128)S(1)}, f32[512,1]{0,1:T(1,128)}, u32[]{:S(2)}) copy-start(f32[512,1]{0,1:T(1,128)} %copy-done.38) | copy-start | bytes 6148
  1769.6 110.2 %copy-start.47 = (f32[512,1]{0,1:T(1,128)S(1)}, f32[512,1]{0,1:T(1,128)}, u32[]{:S(2)}) copy-start(f32[512,1]{0,1:T(1,128)} %get-tuple-element.278) | copy-start | bytes 6148
  (59 other events, 2023.1 us)
Sparse Core Ops, SparseCore 0:
  16.1 64.3 all-gather.8
  86.4 54.2 reduce-scatter.8
  183.6 28.0 all-gather.10
  217.0 60.2 reduce-scatter.10
  278.8 62.1 all-gather.16
  343.1 62.1 all-gather.12
  473.4 144.4 reduce-scatter.16
  642.2 211.6 reduce-scatter.12
  867.6 118.0 all-gather.18
  1172.4 60.3 reduce-scatter.18
  1242.6 63.2 all-gather.20
  1307.3 80.3 all-gather.14
  1390.6 43.3 reduce-scatter.20
  1557.6 34.5 all-gather.22
  1598.3 155.5 all-reduce.4
  1756.0 60.6 reduce-scatter.22
  1818.9 60.7 reduce-scatter.14
where the time goes:
time: 1910 us; the launch traced here: 1890 us
  waiting for transfers between devices  888 us (46%)
  local copies, waits for them, and re-layouts  502 us (26%)
  matrix products  246 us (13%)
  other arithmetic  199 us (10%)
  blocking collectives  29.4 us (2%)
    reduce_scatter x4, waiting for transfers between devices, row_sums(): return lax.psum_scatter(matrix, 'row', scatter_dimension=0, tiled=True)  285 us
    all_gather x4, waiting for transfers between devices, row_rows(): return lax.all_gather(matrix, 'row', axis=0, tiled=True)  228 us
    reduce_scatter x4, waiting for transfers between devices, col_sums(): lax.psum_scatter(matrix.astype(jnp.bfloat16), 'col', scatter_dimension=0,...  199 us
    all_gather x4, waiting for transfers between devices, col_rows(): return lax.all_gather(matrix, 'col', axis=0, tiled=True)  173 us
    scatter x1, local copies, waits for them, and re-layouts, shards(): jnp.zeros((slot_rows, feature_cols), jnp.bfloat16).at[target]  111 us
    transpose x4, local copies, waits for them, and re-layouts, slotted_product(): jax.vmap(lambda piece, weight: jnp.einsum(form, piece, weight, preferred_...  109 us
    dot_general x4, matrix products, slotted_product(): jnp.einsum(form, piece, weight, preferred_element_type=jnp.float32)  81.5 us
    scatter x1, other arithmetic, shards(): jnp.zeros((slot_rows, feature_cols), jnp.bfloat16).at[target]  58.4 us
  transfers between devices with their start and end apart: 19, of which 15 were waited for; matrix products, arithmetic and copies ran while one was open for 31% of the time, Pallas kernels for 0%

commit v1 on v0

v1 whole, which is shorter than its diff:
```python
import functools

import jax
import jax.numpy as jnp
from jax import lax
from jax.experimental import pallas as pl
from jax.experimental.pallas import tpu as pltpu
from jax.sharding import PartitionSpec as P

epsilon = 1e-06
rope_base = 1000000.0
head_dim = 128
low = jnp.bfloat16
full = jnp.float32


def swap(block, axis, bit):
    count = lax.axis_size(axis)
    return lax.ppermute(block, axis, [(i, i ^ bit) for i in range(count)])


def pair(bit, own, other, axis):
    first = jnp.where(bit == 0, own, other)
    second = jnp.where(bit == 0, other, own)
    return jnp.concatenate([first, second], axis=axis)


def dot(left, right, left_dim=1, right_dim=0):
    return lax.dot_general(
        left, right, (((left_dim,), (right_dim,)), ((), ())), preferred_element_type=full
    )


def gather_col(block, col):
    count = lax.axis_size("col")
    from_left, from_right = [block], [block]
    for step in range(1, count):
        from_left.append(
            lax.ppermute(from_left[-1], "col", [(i, i + 1) for i in range(step - 1, count - 1)])
        )
        from_right.append(
            lax.ppermute(from_right[-1], "col", [(i + 1, i) for i in range(count - step)])
        )
    slots = [block]
    for k in range(1, count):
        chosen = None
        for at in range(count):
            there = at ^ k
            value = from_right[there - at] if there > at else from_left[at - there]
            chosen = value if chosen is None else jnp.where(col == at, value, chosen)
        slots.append(chosen)
    return slots


def scatter_col(stack, col):
    count = lax.axis_size("col")

    def term(block):
        return lax.dynamic_index_in_dim(stack, col ^ jnp.clip(block, 0, count - 1), 0, False)

    right, left = None, None
    for step in range(1, count):
        to_right = term(col + count - step)
        to_left = term(col - count + step)
        if right is not None:
            to_right = (to_right.astype(full) + right.astype(full)).astype(low)
            to_left = (to_left.astype(full) + left.astype(full)).astype(low)
        right = lax.ppermute(to_right, "col", [(i, i + 1) for i in range(min(step, count - 1))])
        left = lax.ppermute(
            to_left, "col", [(i, i - 1) for i in range(count - 1, count - 1 - step, -1)]
        )
    return stack[0].astype(full) + right.astype(full) + left.astype(full)


def halves_sum(parts, core, axis):
    size = parts.shape[axis] // 2
    mine = lax.dynamic_slice_in_dim(parts, core * size, size, axis)
    theirs = lax.dynamic_slice_in_dim(parts, (1 - core) * size, size, axis)
    return (mine.astype(full) + swap(theirs, "dp", 1).astype(full)).astype(low)


def others_sum(block):
    bit = 2
    while bit < lax.axis_size("dp"):
        block = (block.astype(full) + swap(block, "dp", bit).astype(full)).astype(low)
        bit *= 2
    return block


def quarter_of(block, quarter):
    size = block.shape[0] // 4
    return lax.dynamic_slice_in_dim(block, quarter * size, size, 0)


def quarters_all(block, core, side):
    across = swap(block, "dp", 2)
    two = [jnp.where(side == 0, block, across), jnp.where(side == 0, across, block)]
    both = jnp.stack(two)
    near = swap(both, "dp", 1)
    result = []
    for at in range(2):
        result.append(jnp.where(core == 0, both[at], near[at]))
        result.append(jnp.where(core == 0, near[at], both[at]))
    return result


def attention_forward_kernel(
    pre_ref, cosine_ref, sine_ref, key_ref, value_ref, start_ref, out_ref, rot_ref, *, window, tile
):
    rows = pre_ref.shape[0]
    pre = pre_ref[...]
    rot = (pre * cosine_ref[...] + pltpu.roll(pre, head_dim // 2, 1) * sine_ref[...]).astype(low)
    rot_ref[...] = rot
    for at in range(rows // tile):
        first = at * tile
        keys = key_ref[first : first + window, :]
        values = value_ref[first : first + window, :]
        scores = dot(rot[first : first + tile], keys, 1, 1) * head_dim ** (-0.5)
        place = lax.broadcasted_iota(jnp.int32, scores.shape, 1) + first
        query = lax.broadcasted_iota(jnp.int32, scores.shape, 0) + (first + rows)
        allowed = (place <= query) & (place >= start_ref[first : first + tile, :])
        scores = jnp.where(allowed, scores, -1e30)
        exponent = jnp.exp(scores - jnp.max(scores, axis=1, keepdims=True))
        weights = exponent / jnp.sum(exponent, axis=1, keepdims=True)
        out_ref[first : first + tile, :] = dot(weights.astype(low), values).astype(low)


def attention_backward_kernel(
    rot_ref,
    cosine_ref,
    sine_ref,
    key_ref,
    value_ref,
    start_ref,
    grad_ref,
    query_grad_ref,
    key_grad_ref,
    value_grad_ref,
    *,
    window,
    tile,
):
    rows = rot_ref.shape[0]

    @pl.when(pl.program_id(0) == 0)
    def _():
        key_grad_ref[...] = jnp.zeros_like(key_grad_ref)
        value_grad_ref[...] = jnp.zeros_like(value_grad_ref)

    for at in range(rows // tile):
        first = at * tile
        rot = rot_ref[first : first + tile, :]
        grad = grad_ref[first : first + tile, :]
        keys = key_ref[first : first + window, :]
        values = value_ref[first : first + window, :]
        scores = dot(rot, keys, 1, 1) * head_dim ** (-0.5)
        place = lax.broadcasted_iota(jnp.int32, scores.shape, 1) + first
        query = lax.broadcasted_iota(jnp.int32, scores.shape, 0) + (first + rows)
        allowed = (place <= query) & (place >= start_ref[first : first + tile, :])
        scores = jnp.where(allowed, scores, -1e30)
        exponent = jnp.exp(scores - jnp.max(scores, axis=1, keepdims=True))
        probs = exponent / jnp.sum(exponent, axis=1, keepdims=True)
        prob_grad = dot(grad, values, 1, 1)
        inner = jnp.sum(probs * prob_grad, axis=1, keepdims=True)
        score_grad = (probs * (prob_grad - inner) * head_dim ** (-0.5)).astype(low)
        rot_grad = dot(score_grad, keys)
        cosine = cosine_ref[first : first + tile, :]
        sine = sine_ref[first : first + tile, :]
        query_grad_ref[first : first + tile, :] = (
            rot_grad * cosine - pltpu.roll(rot_grad, head_dim // 2, 1) * sine
        ).astype(low)
        key_grad_ref[first : first + window, :] += dot(score_grad, rot, 0, 0)
        value_grad_ref[first : first + window, :] += dot(probs.astype(low), grad, 0, 0)


def attention_forward(pre, cosine, sine, keys, values, start, heads):
    rows, reach = pre.shape[0], keys.shape[0]
    whole = lambda shape: pl.BlockSpec(shape, lambda h: (0, 0))
    head = pl.BlockSpec((rows, head_dim), lambda h: (0, h))
    shape = jax.ShapeDtypeStruct((rows, heads * head_dim), low)
    per_half = heads // 2
    return pl.pallas_call(
        functools.partial(attention_forward_kernel, window=reach - rows // 2, tile=rows // 2),
        grid=(heads,),
        in_specs=[
            pl.BlockSpec((rows, head_dim), lambda h: (0, h + h // per_half)),
            whole((rows, head_dim)),
            whole((rows, head_dim)),
            whole((reach, head_dim)),
            whole((reach, head_dim)),
            whole((rows, 1)),
        ],
        out_specs=[head, head],
        out_shape=[shape, shape],
        compiler_params=pltpu.CompilerParams(vmem_limit_bytes=32 * 2**20),
        cost_estimate=pl.CostEstimate(
            flops=heads * rows * reach * 3 * head_dim,
            bytes_accessed=heads * rows * head_dim * 8,
            transcendentals=heads * rows * reach,
        ),
    )(pre, cosine, sine, keys, values, start)


def attention_backward(rot, cosine, sine, keys, values, start, grad, heads):
    rows, reach = rot.shape[0], keys.shape[0]
    whole = lambda shape: pl.BlockSpec(shape, lambda h: (0, 0))
    head = pl.BlockSpec((rows, head_dim), lambda h: (0, h))
    return pl.pallas_call(
        functools.partial(attention_backward_kernel, window=reach - rows // 2, tile=rows // 2),
        grid=(heads,),
        in_specs=[
            head,
            whole((rows, head_dim)),
            whole((rows, head_dim)),
            whole((reach, head_dim)),
            whole((reach, head_dim)),
            whole((rows, 1)),
            head,
        ],
        out_specs=[head, whole((reach, head_dim)), whole((reach, head_dim))],
        out_shape=[
            jax.ShapeDtypeStruct((rows, heads * head_dim), low),
            jax.ShapeDtypeStruct((reach, head_dim), full),
            jax.ShapeDtypeStruct((reach, head_dim), full),
        ],
        compiler_params=pltpu.CompilerParams(vmem_limit_bytes=32 * 2**20),
        cost_estimate=pl.CostEstimate(
            flops=heads * rows * reach * 8 * head_dim,
            bytes_accessed=heads * rows * head_dim * 8,
            transcendentals=heads * rows * reach,
        ),
    )(rot, cosine, sine, keys, values, start, grad)


def rotate(matrix, cosine, sine):
    return matrix * cosine + jnp.roll(matrix, head_dim // 2, axis=1) * sine


def shards(
    inputs,
    norm_gain,
    query_weight,
    key_value_matrix,
    output_weight,
    mixer_gain,
    gate_weight,
    up_weight,
    down_weight,
    lengths,
    routes,
    route_gates,
    cotangent,
):
    row, col, dp = lax.axis_index("row"), lax.axis_index("col"), lax.axis_index("dp")
    core, side, quarter = dp % 2, (dp // 2) % 2, dp % 4
    cols = lax.axis_size("col")
    tokens, part_width = inputs.shape
    width = 2 * part_width
    own_tokens = tokens // 2
    experts, _, units = gate_weight.shape
    hidden_width = experts * units
    query_block, keyval_block = query_weight.shape[1], key_value_matrix.shape[1]
    heads = 2 * query_block // head_dim

    inputs_all = pair(row, inputs, swap(inputs, "row", 1), 1)
    gains = jnp.stack([norm_gain, mixer_gain])
    gains = pair(row, gains, swap(gains, "row", 1), 1)
    norm_all, mixer_all = gains[0], gains[1]
    lengths_all = pair(row, lengths, swap(lengths, "row", 1), 0)
    lengths_row = jnp.where(col < cols // 2, lengths_all[0], lengths_all[1])

    blocks = 2 * cols
    joint = jnp.concatenate([query_weight, key_value_matrix], axis=1)
    joint_part = quarter_of(joint, quarter)
    output_part = quarter_of(output_weight, quarter)

    def spread(part):
        arrived = []
        for k in range(cols):
            route = []
            for index in range(blocks):
                from_row, from_col = index // cols, index % cols
                to_row, to_col = from_col // 2, (2 * from_row + from_col % 2) ^ k
                route.append((index, to_row * cols + to_col))
            arrived.append(lax.ppermute(part, ("row", "col"), route))
        for bit in (1, 2):
            arrived = [
                jnp.where(col & bit == 0, arrived[k], arrived[k ^ bit]) for k in range(cols)
            ]
        return jnp.stack(arrived)

    joint_quarters = quarters_all(spread(joint_part), core, side)
    output_quarters = quarters_all(spread(output_part), core, side)
    joint_weight = jnp.concatenate(
        [
            jnp.concatenate(
                [piece[2 * r + b] for r in range(2) for piece in joint_quarters], axis=0
            )
            for b in range(2)
        ],
        axis=1,
    )
    head_output = jnp.concatenate(
        [
            jnp.concatenate(
                [piece[2 * r + b] for b in range(2) for piece in output_quarters], axis=0
            )
            for r in range(2)
        ],
        axis=1,
    )

    def flat_units(weight):
        return weight.transpose(1, 0, 2).reshape(part_width, hidden_width)

    gate_flat, up_flat = flat_units(gate_weight), flat_units(up_weight)
    down_flat = down_weight.reshape(hidden_width, part_width)

    def partner_of(flat):
        part = swap(quarter_of(flat, quarter), "row", 1)
        return jnp.concatenate(quarters_all(part, core, side), axis=0)

    gate_all = pair(row, gate_flat, partner_of(gate_flat), 0)
    up_all = pair(row, up_flat, partner_of(up_flat), 0)
    down_all = pair(row, down_flat, partner_of(down_flat), 1)

    kept = lax.dynamic_slice_in_dim(cotangent, row * own_tokens, own_tokens, 0)
    sent = lax.dynamic_slice_in_dim(cotangent, (1 - row) * own_tokens, own_tokens, 0)
    cot_own = pair(row, kept, swap(sent, "row", 1), 1)
    cot_all = jnp.concatenate(gather_col(cot_own, col), axis=0)

    chosen = routes[:, :, None] == jnp.arange(experts, dtype=jnp.int32)[None, None, :]
    table = jnp.sum(jnp.where(chosen, route_gates[:, :, None], 0.0), axis=1)
    slot_tables = [
        lax.dynamic_slice_in_dim(table, (col ^ k) * tokens + row * own_tokens, own_tokens, 0)
        for k in range(cols)
    ]
    widen = jnp.repeat(jnp.eye(experts, dtype=full), units, axis=1)
    gates = jnp.dot(
        jnp.concatenate(slot_tables, axis=0), widen, precision=lax.Precision.HIGHEST
    )

    inputs_full = inputs_all.astype(full)
    first_scale = lax.rsqrt(jnp.mean(inputs_full * inputs_full, axis=1, keepdims=True) + epsilon)
    normed = (inputs_full * first_scale * norm_all[None, :]).astype(low)
    projected = dot(normed, joint_weight)
    ends = jnp.cumsum(lengths_row)
    starts = ends - lengths_row
    odd = col % 2
    place = odd * tokens + jnp.arange(tokens, dtype=jnp.int32)
    begin = jnp.max(jnp.where(starts[None, :] <= place[:, None], starts[None, :], 0), axis=1)
    position = place - begin
    start = (begin + (1 - odd) * tokens)[:, None]
    theta = rope_base ** (-jnp.arange(0, head_dim, 2, dtype=full) / head_dim)
    angles = position.astype(full)[:, None] * theta[None, :]
    cosine, sine = jnp.cos(angles), jnp.sin(angles)
    cosine = jnp.concatenate([cosine, cosine], axis=1)
    sine = jnp.concatenate([-sine, sine], axis=1)
    key_at = query_block
    value_at = 2 * query_block + keyval_block
    key_own = rotate(projected[:, key_at : key_at + head_dim], cosine, sine).astype(low)
    value_own = projected[:, value_at : value_at + head_dim].astype(low)
    own_pair = jnp.concatenate([key_own, value_own], axis=1)
    before = lax.ppermute(own_pair, "col", [(i, i + 1) for i in range(0, cols, 2)])
    pairs = jnp.concatenate([before, own_pair], axis=0)
    keys, values = pairs[:, :head_dim], pairs[:, head_dim:]
    attended, rot = attention_forward(projected, cosine, sine, keys, values, start, heads)

    branch_part = dot(attended, head_output).astype(low)
    kept = lax.dynamic_slice_in_dim(branch_part, row * own_tokens, own_tokens, 0)
    sent = lax.dynamic_slice_in_dim(branch_part, (1 - row) * own_tokens, own_tokens, 0)
    branch = kept.astype(full) + swap(sent, "row", 1).astype(full)
    inputs_own = lax.dynamic_slice_in_dim(inputs_all, row * own_tokens, own_tokens, 0)
    middle = inputs_own.astype(full) + branch
    second_scale = lax.rsqrt(jnp.mean(middle * middle, axis=1, keepdims=True) + epsilon)
    expert_own = (middle * second_scale * mixer_all[None, :]).astype(low)
    expert_in = jnp.concatenate(gather_col(expert_own, col), axis=0)

    gate = dot(expert_in, gate_all)
    up = dot(expert_in, up_all)
    hidden_grad = dot(cot_all, down_all, 1, 1) * gates
    sigmoid = jax.nn.sigmoid(gate)
    silu = gate * sigmoid
    hidden = (silu * up * gates).astype(low)
    gate_grad = (hidden_grad * up * (sigmoid * (1.0 + gate * (1.0 - sigmoid)))).astype(low)
    up_grad = (hidden_grad * silu).astype(low)
    in_part = (dot(gate_grad, gate_all, 1, 1) + dot(up_grad, up_all, 1, 1)).astype(low)
    second_grad = scatter_col(in_part.reshape(cols, own_tokens, width), col)
    out_part = dot(hidden, down_all).astype(low)
    experts_out = scatter_col(out_part.reshape(cols, own_tokens, width), col)
    outputs_own = (middle + experts_out).astype(low)
    theirs = lax.dynamic_slice_in_dim(outputs_own, (1 - row) * part_width, part_width, 1)
    mine = lax.dynamic_slice_in_dim(outputs_own, row * part_width, part_width, 1)
    outputs = pair(row, mine, swap(theirs, "row", 1), 0)

    gate_part = dot(expert_in, gate_grad, 0, 0).astype(low)
    up_part = dot(expert_in, up_grad, 0, 0).astype(low)
    down_part = dot(hidden, cot_all, 0, 0).astype(low)

    def expert_total(part, hidden_axis):
        half = halves_sum(part, core, hidden_axis)
        axis = 1 - hidden_axis
        mine = lax.dynamic_slice_in_dim(half, row * part_width, part_width, axis)
        theirs = lax.dynamic_slice_in_dim(half, (1 - row) * part_width, part_width, axis)
        block = (mine.astype(full) + swap(theirs, "row", 1).astype(full)).astype(low)
        block = others_sum(block)
        return pair(core, block, swap(block, "dp", 1), hidden_axis).astype(full)

    def by_expert(flat):
        return flat.reshape(part_width, experts, units).transpose(1, 0, 2)

    gate_total = by_expert(expert_total(gate_part, 1))
    up_total = by_expert(expert_total(up_part, 1))
    down_total = expert_total(down_part, 0).reshape(experts, units, part_width)

    weighted = mixer_all[None, :] * second_grad
    inner = jnp.sum(weighted * middle, axis=1, keepdims=True)
    cube = second_scale * second_scale * second_scale
    middle_grad = cot_own.astype(full) + second_scale * weighted - middle * cube * inner / width
    mixer_partial = jnp.sum(second_grad * middle * second_scale, axis=0)
    branch_own = middle_grad.astype(low)
    branch_grad = pair(row, branch_own, swap(branch_own, "row", 1), 0)

    attended_grad = dot(branch_grad, head_output, 1, 1).astype(low)
    output_part_grad = dot(attended, branch_grad, 0, 0).astype(low)
    query_grad, key_grad, value_grad = attention_backward(
        rot, cosine, sine, keys, values, start, attended_grad, heads
    )
    pair_grad = jnp.concatenate([key_grad, value_grad], axis=1)
    returned = lax.ppermute(
        pair_grad[:tokens].astype(low), "col", [(i + 1, i) for i in range(0, cols, 2)]
    )
    pair_grad = pair_grad[tokens:] + returned.astype(full)
    key_pre = rotate(pair_grad[:, :head_dim], cosine, -sine).astype(low)
    value_pre = pair_grad[:, head_dim:].astype(low)
    joint_grad = jnp.concatenate(
        [query_grad[:, :query_block], key_pre, query_grad[:, query_block:], value_pre], axis=1
    )
    normed_part = dot(joint_grad, joint_weight, 1, 1).astype(low)
    mine = lax.dynamic_slice_in_dim(normed_part, row * part_width, part_width, 1)
    theirs = lax.dynamic_slice_in_dim(normed_part, (1 - row) * part_width, part_width, 1)
    normed_grad = mine.astype(full) + swap(theirs, "row", 1).astype(full)
    weighted = norm_gain[None, :] * normed_grad
    inputs_part = inputs.astype(full)
    inner = jnp.sum(weighted * inputs_part, axis=1)
    inner = (inner + swap(inner, "row", 1))[:, None]
    cube = first_scale * first_scale * first_scale
    middle_part = lax.dynamic_slice_in_dim(branch_grad, row * part_width, part_width, 1)
    input_grad = (
        middle_part.astype(full) + first_scale * weighted - inputs_part * cube * inner / width
    ).astype(low)
    norm_partial = jnp.sum(normed_grad * inputs_part * first_scale, axis=0)

    joint_weight_grad = dot(normed, joint_grad, 0, 0).astype(low)

    def block_total(part, block_axis):
        half = halves_sum(part, core, 2 + block_axis)
        mine = lax.dynamic_index_in_dim(half, row, 0, False)
        theirs = swap(lax.dynamic_index_in_dim(half, 1 - row, 0, False), "row", 1)
        by_col = pair(row, mine, theirs, 0)
        stack = jnp.stack(
            [lax.dynamic_index_in_dim(by_col, col ^ k, 0, False) for k in range(cols)]
        )
        block = others_sum(scatter_col(stack, col).astype(low))
        return pair(core, block, swap(block, "dp", 1), block_axis).astype(full)

    both = query_block + keyval_block
    joint_total = block_total(
        joint_weight_grad.reshape(2, part_width, 2, both).transpose(0, 2, 1, 3), 0
    )
    output_total = block_total(
        output_part_grad.reshape(2, query_block, 2, part_width).transpose(2, 0, 1, 3), 0
    )
    query_total, keyval_total = joint_total[:, :query_block], joint_total[:, query_block:]

    norm_total = lax.psum(norm_partial, ("dp", "col"))
    mixer_sum = lax.psum(mixer_partial, ("dp", "row", "col"))
    mixer_total = lax.dynamic_slice_in_dim(mixer_sum, row * part_width, part_width, 0)
    return (
        outputs,
        input_grad,
        norm_total,
        query_total,
        keyval_total,
        output_total,
        mixer_total,
        gate_total,
        up_total,
        down_total,
    )


def solution(mesh):
    return jax.shard_map(
        shards,
        mesh=mesh,
        in_specs=(
            P(("dp", "col"), "row"),
            P("row"),
            P("row", "col"),
            P("row", "col"),
            P("col", "row"),
            P("row"),
            P(None, "row", "col"),
            P(None, "row", "col"),
            P(None, "col", "row"),
            P(("dp", "row"), None),
            P("dp", None),
            P("dp", None),
            P(("dp", "col"), "row"),
        ),
        out_specs=(
            P(("dp", "col"), "row"),
            P(("dp", "col"), "row"),
            P("row"),
            P("row", "col"),
            P("row", "col"),
            P("col", "row"),
            P("row"),
            P(None, "row", "col"),
            P(None, "row", "col"),
            P(None, "col", "row"),
        ),
        check_vma=False,
    )
```

time: 1910 us -> 889 us (0.47)
  waiting for transfers between devices: 888 us -> 228 us
  local copies, waits for them, and re-layouts: 502 us -> 84.4 us
  starting transfers between devices: 4.37 us -> 205 us
  matrix products: 246 us -> 104 us
  blocking collectives: 29.4 us -> 122 us
  other arithmetic: 199 us -> 107 us
  Pallas kernels: 0 us -> 21.4 us
    reduce_scatter x8 -> x0, waiting for transfers between devices: 483 us -> none  [the longest x4 285 us: row_sums(): return lax.psum_scatter(matrix, 'row', scatter_dimension=0, tiled=True)]
    all_gather x8 -> x0, waiting for transfers between devices: 401 us -> none  [the longest x4 228 us: row_rows(): return lax.all_gather(matrix, 'row', axis=0, tiled=True)]
    ppermute x2 -> x88, waiting for transfers between devices: 2.23 us -> 228 us  [the longest x42 88.8 us: swap(): return lax.ppermute(block, axis, [(i, i ^ bit) for i in range(count)])]
    ppermute x2 -> x88, starting transfers between devices: 2.4 us -> 205 us  [the longest x42 60 us: swap(): return lax.ppermute(block, axis, [(i, i ^ bit) for i in range(count)])]
    dot_general x26 -> x16, matrix products: 246 us -> 104 us  [the longest x15 96.5 us: dot(): lax.dot_general(left, right, (((left_dim,), (right_dim,)), ((), ())), pre...]
    scatter x1 -> x0, local copies, waits for them, and re-layouts: 111 us -> none  [shards(): jnp.zeros((slot_rows, feature_cols), jnp.bfloat16).at[target]]
    transpose x4 -> x0, local copies, waits for them, and re-layouts: 109 us -> none  [slotted_product(): jax.vmap(lambda piece, weight: jnp.einsum(form, piece, weight, preferred_...]
    gather x2 -> x0, local copies, waits for them, and re-layouts: 103 us -> none  [the longest x1 51.4 us: shards(): routed = down_part[target].reshape(group_rows, top_count, -1)]
  transfers between devices with their start and end apart: 19 -> 88, of which waited for: 15 -> 25; matrix products, arithmetic and copies ran while one was open for 31% -> 24% of each run, Pallas kernels for 0% -> 2%
where the time goes in v1:
time: 889 us; the launch traced here: 876 us
  waiting for transfers between devices  228 us (26%)
  starting transfers between devices  205 us (23%)
  blocking collectives  122 us (14%)
  other arithmetic  107 us (12%)
  matrix products  104 us (12%)
  local copies, waits for them, and re-layouts  84.4 us (9%)
  Pallas kernels  21.4 us (2%)
    dot_general x15, matrix products, dot(): lax.dot_general(left, right, (((left_dim,), (right_dim,)), ((), ())), pre...  96.5 us
    psum x1, blocking collectives, shards(): mixer_sum = lax.psum(mixer_partial, ('dp', 'row', 'col'))  89.5 us
    ppermute x42, waiting for transfers between devices, swap(): return lax.ppermute(block, axis, [(i, i ^ bit) for i in range(count)])  88.8 us
    ppermute x42, starting transfers between devices, swap(): return lax.ppermute(block, axis, [(i, i ^ bit) for i in range(count)])  60 us
    ppermute x12, waiting for transfers between devices, scatter_col(): lax.ppermute(to_right, 'col', [(i, i + 1) for i in range(min(step, count...  54.1 us
    ppermute x12, waiting for transfers between devices, scatter_col(): lax.ppermute(to_left, 'col', [(i, i - 1) for i in range(count - 1, count...  45.7 us
    ppermute x12, starting transfers between devices, scatter_col(): lax.ppermute(to_left, 'col', [(i, i - 1) for i in range(count - 1, count...  38.2 us
    ppermute x8, starting transfers between devices, spread(): arrived.append(lax.ppermute(part, ('row', 'col'), route))  37.6 us
  transfers between devices with their start and end apart: 88, of which 25 were waited for; matrix products, arithmetic and copies ran while one was open for 24% of the time, Pallas kernels for 2%

profile of v1, /device:TPU:17, one launch (start us, length us, event | category | flops | bytes accessed | tf_op | source)
XLA Modules:
  0.0 875.6 jit_solution(10880584984502458508)
XLA Ops:
  73.2 42.3 %collective-permute-done.39 = bf16[256,768]{1,0:T(8,128)(2,1)S(1)} collective-permute-done((bf16[256,768]{1,0:T(8,128)(2,1)}, bf16[256,768]{1,0:T(8,128)(2,1)S(1)}, u32[]{:S(2)}, u32[]{:S(2)}) %collective-permute-start.39) | collective-permute-done | bytes 393248 | tf_op jit(solution)/shard_map/ppermute | solution.py:19
  143.3 8.0 collective-permute-done.24
  192.8 11.4 %collective-permute-done.42 = bf16[256,1536]{1,0:T(8,128)(2,1)} collective-permute-done((bf16[256,1536]{1,0:T(8,128)(2,1)}, bf16[256,1536]{1,0:T(8,128)(2,1)}, u32[]{:S(2)}, u32[]{:S(2)}) %collective-permute-start.42) | collective-permute-done | bytes 786464 | tf_op jit(solution)/shard_map/ppermute | solution.py:39
  237.7 8.9 %shard_map.204 = (bf16[512,768]{1,0:T(8,128)(2,1)S(1)}, bf16[512,768]{1,0:T(8,128)(2,1)S(1)}) custom-call(f32[512,1024]{1,0:T(8,128)S(1)} %fusion.9.pre_ref, f32[512,128]{1,0:T(8,128)S(1)} %get-tuple-element.193.cosine_ref, f32[512,128]{1,0:T(8,128)S(1)} %get-tuple-element.39.sine_ref, bf16[1024,128]{1,0:T(8,128)(2,1)S(1)} %get-tuple-element.192.key_ref, ...), custom_call_target="tpu_custom_call" | custom-call | flops 1207959552 | bytes 3145728 | tf_op jit(solution)/shard_map/pallas_call | solution.py:182
  258.4 10.3 %collective-permute-done.16 = bf16[256,1536]{1,0:T(8,128)(2,1)} collective-permute-done((bf16[256,1536]{1,0:T(8,128)(2,1)}, bf16[256,1536]{1,0:T(8,128)(2,1)}, u32[]{:S(2)}, u32[]{:S(2)}) %collective-permute-start.16) | collective-permute-done | bytes 786464 | tf_op jit(solution)/shard_map/ppermute | solution.py:19
  279.8 10.5 %collective-permute-done.17 = bf16[256,1536]{1,0:T(8,128)(2,1)S(1)} collective-permute-done((bf16[256,1536]{1,0:T(8,128)(2,1)S(1)}, bf16[256,1536]{1,0:T(8,128)(2,1)S(1)}, u32[]{:S(2)}, u32[]{:S(2)}) %collective-permute-start.17) | collective-permute-done | bytes 786464 | tf_op jit(solution)/shard_map/ppermute | solution.py:39
  300.0 8.4 collective-permute-done.19
  312.6 12.7 %collective-permute-start.22 = (bf16[256,1536]{1,0:T(8,128)(2,1)S(1)}, bf16[256,1536]{1,0:T(8,128)(2,1)S(1)}, u32[]{:S(2)}, u32[]{:S(2)}) collective-permute-start(bf16[256,1536]{1,0:T(8,128)(2,1)S(1)} %collective-permute-done.20), channel_id=1, source_target_pairs={{1,0},{5,4},{9,8},{13,12},{17,16},{21,20},{25,24},{29,28}} | collective-permute-start | bytes 2359304 | tf_op jit(solution)/shard_map/ppermute | solution.py:42
  328.5 7.7 fusion.5
  336.3 7.7 fusion.7
  344.0 17.7 %multiply_convert_fusion = (bf16[1024,1536]{1,0:T(8,128)(2,1)}, bf16[1024,1536]{1,0:T(8,128)(2,1)}, bf16[1024,1536]{1,0:T(8,128)(2,1)}) fusion(f32[1024,1536]{1,0:T(8,128)} %fusion.7, f32[1024,1536]{1,0:T(8,128)} %fusion.5, f32[1024,1536]{1,0:T(8,128)} %fusion.90, bf16[1536,768]{1,0:T(8,128)(2,1)} %get-tuple-element.48, ...), kind=kOutput, calls=%fused_computation.4 | convolution fusion | flops 4883742720 | bytes 36175872 | tf_op jit(solution)/shard_map/dot_general | solution.py:29
  361.7 10.1 %convolution_convert_fusion = bf16[1536,1536]{0,1:T(8,128)(2,1)S(1)} fusion(bf16[1024,1536]{1,0:T(8,128)(2,1)} %get-tuple-element.42, bf16[256,1536]{1,0:T(8,128)(2,1)} %get-tuple-element.98, bf16[256,1536]{1,0:T(8,128)(2,1)} %select_select_fusion, bf16[256,1536]{1,0:T(8,128)(2,1)} %get-tuple-element.97, bf16[256,768]{1,0:T(8,128)(2,1)S(1)} %copy-done.48, ...), kind=kOutput, calls=%fused_computation | convolution fusion | flops 4849926144 | bytes 11010048 | tf_op jit(solution)/shard_map/dot_general | solution.py:29
  379.5 7.9 convolution_convert_fusion.2
  387.4 9.2 %fusion.6 = f32[1024,1536]{1,0:T(8,128)} fusion(bf16[1024,1536]{1,0:T(8,128)(2,1)} %get-tuple-element.41, bf16[768,1536]{0,1:T(8,128)(2,1)S(1)} %copy-done.71, bf16[768,1536]{0,1:T(8,128)(2,1)S(1)} %copy-done.69), kind=kOutput, calls=%fused_computation.32 | convolution fusion | flops 4841275392 | bytes 14155776 | tf_op jit(solution)/shard_map/dot_general | solution.py:29
  412.4 8.3 add_convert_fusion
  427.6 14.9 %collective-permute-done.35 = bf16[256,1536]{1,0:T(8,128)(2,1)S(1)} collective-permute-done((bf16[256,1536]{1,0:T(8,128)(2,1)S(1)}, bf16[256,1536]{1,0:T(8,128)(2,1)S(1)}, u32[]{:S(2)}, u32[]{:S(2)}) %collective-permute-start.35) | collective-permute-done | bytes 786464 | tf_op jit(solution)/shard_map/ppermute | solution.py:69
  444.0 35.1 %collective-permute-done.33 = bf16[256,1536]{1,0:T(8,128)(2,1)S(1)} collective-permute-done((bf16[256,1536]{1,0:T(8,128)(2,1)S(1)}, bf16[256,1536]{1,0:T(8,128)(2,1)S(1)}, u32[]{:S(2)}, u32[]{:S(2)}) %collective-permute-start.33) | collective-permute-done | bytes 786464 | tf_op jit(solution)/shard_map/ppermute | solution.py:68
  486.1 10.0 %collective-permute-done.47 = bf16[256,1536]{1,0:T(8,128)(2,1)S(1)} collective-permute-done((bf16[256,1536]{1,0:T(8,128)(2,1)S(1)}, bf16[256,1536]{1,0:T(8,128)(2,1)S(1)}, u32[]{:S(2)}, u32[]{:S(2)}) %collective-permute-start.47) | collective-permute-done | bytes 786464 | tf_op jit(solution)/shard_map/ppermute | solution.py:68
  533.6 21.6 %collective-permute-done.51 = bf16[256,1536]{1,0:T(8,128)(2,1)S(1)} collective-permute-done((bf16[256,1536]{1,0:T(8,128)(2,1)S(1)}, bf16[256,1536]{1,0:T(8,128)(2,1)S(1)}, u32[]{:S(2)}, u32[]{:S(2)}) %collective-permute-start.51) | collective-permute-done | bytes 786464 | tf_op jit(solution)/shard_map/ppermute | solution.py:69
  561.1 89.5 %psum.15 = f32[1536]{0:T(1024)S(1)} all-reduce(f32[1536]{0:T(1024)S(1)} %get-tuple-element.30), channel_id=1, replica_groups=mesh['dp'=4,'row'=2,'col'=4] {'dp','row','col'}, use_global_device_ids=true, to_apply=%region_10.11 | all-reduce | flops 1536 | bytes 12288 | tf_op jit(solution)/shard_map/psum | solution.py:477
  676.1 12.5 %shard_map.205 = (bf16[512,768]{1,0:T(8,128)(2,1)S(1)}, f32[1024,128]{1,0:T(8,128)S(1)}, f32[1024,128]{1,0:T(8,128)S(1)}) custom-call(bf16[512,768]{1,0:T(8,128)(2,1)S(1)} %copy-done.9, f32[512,128]{1,0:T(8,128)S(1)} %get-tuple-element.193.cosine_ref, f32[512,128]{1,0:T(8,128)S(1)} %get-tuple-element.39.sine_ref, bf16[1024,128]{1,0:T(8,128)(2,1)S(1)} %copy-done.5, ...), custom_call_target="tpu_custom_call" | custom-call | flops 3221225472 | bytes 3145728 | tf_op jit(solution)/shard_map/pallas_call | solution.py:208
  733.5 32.6 %psum.14 = f32[768]{0:T(1024)} all-reduce(f32[768]{0:T(1024)S(1)} %get-tuple-element.32), channel_id=1, replica_groups=mesh['dp'=4,'row'=2,'col'=4] {'dp','col'}, use_global_device_ids=true, to_apply=%region_8.9 | all-reduce | flops 768 | bytes 6144 | tf_op jit(solution)/shard_map/psum | solution.py:476
  788.5 12.3 %collective-permute-done.57 = bf16[2,384,512]{2,1,0:T(8,128)(2,1)S(1)} collective-permute-done((bf16[2,384,512]{2,1,0:T(8,128)(2,1)S(1)}, bf16[2,384,512]{2,1,0:T(8,128)(2,1)S(1)}, u32[]{:S(2)}, u32[]{:S(2)}) %collective-permute-start.57) | collective-permute-done | bytes 786464 | tf_op jit(solution)/shard_map/ppermute | solution.py:19
  815.2 10.1 %collective-permute-start.72 = (bf16[192,768]{1,0:T(8,128)(2,1)S(1)}, bf16[192,768]{1,0:T(8,128)(2,1)S(1)}, u32[]{:S(2)}, u32[]{:S(2)}) collective-permute-start(bf16[192,768]{1,0:T(8,128)(2,1)S(1)} %get-tuple-element.120), channel_id=1, source_target_pairs={{3,2},{2,1},{7,6},{6,5},{11,10},{10,9},{15,14},{14,13},{19,18},{18... | collective-permute-start | bytes 884744 | tf_op jit(solution)/shard_map/ppermute | solution.py:69
  (590 shorter events, 452.3 us)
Async XLA Ops:
  59.2 60.2 %collective-permute-start.23 = (bf16[192,1536]{1,0:T(8,128)(2,1)}, bf16[192,1536]{1,0:T(8,128)(2,1)S(1)}, u32[]{:S(2)}, u32[]{:S(2)}) collective-permute-start(bf16[192,1536]{1,0:T(8,128)(2,1)} %copy.78), channel_id=1, source_target_pairs={{0,4},{4,0},{1,5},{5,1},{2,6},{6,2},{3,7},{7,3},{8,12},{12,8},{9,1... | collective-permute-start | bytes 1769480 | tf_op jit(solution)/shard_map/ppermute | solution.py:19
  61.4 62.3 %collective-permute-start.26 = (bf16[192,1536]{1,0:T(8,128)(2,1)}, bf16[192,1536]{1,0:T(8,128)(2,1)}, u32[]{:S(2)}, u32[]{:S(2)}) collective-permute-start(bf16[192,1536]{1,0:T(8,128)(2,1)} %copy.86), channel_id=1, source_target_pairs={{0,4},{4,0},{1,5},{5,1},{2,6},{6,2},{3,7},{7,3},{8,12},{12,8},{9,1... | collective-permute-start | bytes 1769480 | tf_op jit(solution)/shard_map/ppermute | solution.py:19
  64.8 66.6 %collective-permute-start = (bf16[512,768]{1,0:T(8,128)(2,1)S(1)}, bf16[512,768]{1,0:T(8,128)(2,1)}, u32[]{:S(2)}, u32[]{:S(2)}) collective-permute-start(bf16[512,768]{1,0:T(8,128)(2,1)S(1)} %copy-done.17), channel_id=1, source_target_pairs={{0,4},{4,0},{1,5},{5,1},{2,6},{6,2},{3,7},{7,3},{8,12},{12,8},{9,1... | collective-permute-start | bytes 2359304 | tf_op jit(solution)/shard_map/ppermute | solution.py:19
  123.7 58.6 %collective-permute-start.40 = (bf16[256,1536]{1,0:T(8,128)(2,1)}, bf16[256,1536]{1,0:T(8,128)(2,1)}, u32[]{:S(2)}, u32[]{:S(2)}) collective-permute-start(bf16[256,1536]{1,0:T(8,128)(2,1)} %pad_maximum_fusion.36), channel_id=1, source_target_pairs={{0,1},{1,2},{2,3},{4,5},{5,6},{6,7},{8,9},{9,10},{10,11},{12,13},{... | collective-permute-start | bytes 2359304 | tf_op jit(solution)/shard_map/ppermute | solution.py:39
  163.9 57.7 %collective-permute-start.7 = (bf16[2,4,192,512]{3,2,1,0:T(8,128)(2,1)}, bf16[2,4,192,512]{3,2,1,0:T(8,128)(2,1)}, u32[]{:S(2)}, u32[]{:S(2)}) collective-permute-start(bf16[2,4,192,512]{3,2,1,0:T(8,128)(2,1)} %pad_maximum_fusion.20), channel_id=1, source_target_pairs={{0,8},{8,0},{16,24},{24,16},{1,9},{9,1},{17,25},{25,17},{2,10},{10... | collective-permute-start | bytes 4718600 | tf_op jit(solution)/shard_map/ppermute | solution.py:19
  204.2 91.4 %collective-permute-start.31 = (bf16[2,384,768]{2,1,0:T(8,128)(2,1)}, bf16[2,384,768]{2,1,0:T(8,128)(2,1)}, u32[]{:S(2)}, u32[]{:S(2)}) collective-permute-start(bf16[2,384,768]{2,1,0:T(8,128)(2,1)} %pad_maximum_fusion.29), channel_id=1, source_target_pairs={{0,8},{8,0},{16,24},{24,16},{1,9},{9,1},{17,25},{25,17},{2,10},{10... | collective-permute-start | bytes 3538952 | tf_op jit(solution)/shard_map/ppermute | solution.py:19
  205.9 119.3 %collective-permute-start.44 = (bf16[256,1536]{1,0:T(8,128)(2,1)}, bf16[256,1536]{1,0:T(8,128)(2,1)}, u32[]{:S(2)}, u32[]{:S(2)}) collective-permute-start(bf16[256,1536]{1,0:T(8,128)(2,1)} %collective-permute-done.42), channel_id=1, source_target_pairs={{2,3},{6,7},{10,11},{14,15},{18,19},{22,23},{26,27},{30,31}} | collective-permute-start | bytes 2359304 | tf_op jit(solution)/shard_map/ppermute | solution.py:39
  211.6 113.7 %collective-permute-start.45 = (bf16[256,1536]{1,0:T(8,128)(2,1)}, bf16[256,1536]{1,0:T(8,128)(2,1)}, u32[]{:S(2)}, u32[]{:S(2)}) collective-permute-start(bf16[256,1536]{1,0:T(8,128)(2,1)} %collective-permute-done.43), channel_id=1, source_target_pairs={{1,0},{5,4},{9,8},{13,12},{17,16},{21,20},{25,24},{29,28}} | collective-permute-start | bytes 2359304 | tf_op jit(solution)/shard_map/ppermute | solution.py:42
  398.2 101.0 %collective-permute-start.84 = (bf16[768,1536]{0,1:T(8,128)(2,1)}, bf16[768,1536]{0,1:T(8,128)(2,1)}, u32[]{:S(2)}, u32[]{:S(2)}) collective-permute-start(bf16[768,1536]{0,1:T(8,128)(2,1)} %constant_dynamic-slice_fusion.1), channel_id=1, source_target_pairs={{0,8},{8,0},{16,24},{24,16},{1,9},{9,1},{17,25},{25,17},{2,10},{10... | collective-permute-start | bytes 7077896 | tf_op jit(solution)/shard_map/ppermute | solution.py:19
  421.9 82.9 %collective-permute-start.80 = (bf16[1536,768]{0,1:T(8,128)(2,1)S(1)}, bf16[1536,768]{0,1:T(8,128)(2,1)S(1)}, u32[]{:S(2)}, u32[]{:S(2)}) collective-permute-start(bf16[1536,768]{0,1:T(8,128)(2,1)S(1)} %constant_dynamic-slice_fusion.3), channel_id=1, source_target_pairs={{0,8},{8,0},{16,24},{24,16},{1,9},{9,1},{17,25},{25,17},{2,10},{10... | collective-permute-start | bytes 7077896 | tf_op jit(solution)/shard_map/ppermute | solution.py:19
  423.3 59.1 %collective-permute-start.49 = (bf16[256,1536]{1,0:T(8,128)(2,1)S(1)}, bf16[256,1536]{1,0:T(8,128)(2,1)S(1)}, u32[]{:S(2)}, u32[]{:S(2)}) collective-permute-start(bf16[256,1536]{1,0:T(8,128)(2,1)S(1)} %get-tuple-element.52), channel_id=1, source_target_pairs={{3,2},{7,6},{11,10},{15,14},{19,18},{23,22},{27,26},{31,30}} | collective-permute-start | bytes 2359304 | tf_op jit(solution)/shard_map/ppermute | solution.py:69
  496.0 60.9 %collective-permute-start.34 = (bf16[256,1536]{1,0:T(8,128)(2,1)S(1)}, bf16[256,1536]{1,0:T(8,128)(2,1)S(1)}, u32[]{:S(2)}, u32[]{:S(2)}) collective-permute-start(bf16[256,1536]{1,0:T(8,128)(2,1)S(1)} %get-tuple-element.53), channel_id=1, source_target_pairs={{0,1},{1,2},{2,3},{4,5},{5,6},{6,7},{8,9},{9,10},{10,11},{12,13},{... | collective-permute-start | bytes 2359304 | tf_op jit(solution)/shard_map/ppermute | solution.py:68
  509.7 141.7 %collective-permute-start.85 = (bf16[768,768]{0,1:T(8,128)(2,1)}, bf16[768,768]{0,1:T(8,128)(2,1)}, u32[]{:S(2)}, u32[]{:S(2)}) collective-permute-start(bf16[768,768]{0,1:T(8,128)(2,1)} %constant_dynamic-slice_fusion), channel_id=1, source_target_pairs={{0,4},{4,0},{1,5},{5,1},{2,6},{6,2},{3,7},{7,3},{8,12},{12,8},{9,1... | collective-permute-start | bytes 3538952 | tf_op jit(solution)/shard_map/ppermute | solution.py:19
  532.8 122.6 %collective-permute-start.81 = (bf16[768,768]{0,1:T(8,128)(2,1)}, bf16[768,768]{0,1:T(8,128)(2,1)}, u32[]{:S(2)}, u32[]{:S(2)}) collective-permute-start(bf16[768,768]{0,1:T(8,128)(2,1)} %constant_dynamic-slice_fusion.2), channel_id=1, source_target_pairs={{0,4},{4,0},{1,5},{5,1},{2,6},{6,2},{3,7},{7,3},{8,12},{12,8},{9,1... | collective-permute-start | bytes 3538952 | tf_op jit(solution)/shard_map/ppermute | solution.py:19
  555.2 103.4 %collective-permute-start.77 = (bf16[768,768]{0,1:T(8,128)(2,1)}, bf16[768,768]{0,1:T(8,128)(2,1)}, u32[]{:S(2)}, u32[]{:S(2)}) collective-permute-start(bf16[768,768]{0,1:T(8,128)(2,1)} %constant_dynamic-slice_fusion.4), channel_id=1, source_target_pairs={{0,4},{4,0},{1,5},{5,1},{2,6},{6,2},{3,7},{7,3},{8,12},{12,8},{9,1... | collective-permute-start | bytes 3538952 | tf_op jit(solution)/shard_map/ppermute | solution.py:19
  558.9 105.3 %collective-permute-start.52 = (bf16[256,1536]{1,0:T(8,128)(2,1)}, bf16[256,1536]{1,0:T(8,128)(2,1)}, u32[]{:S(2)}, u32[]{:S(2)}) collective-permute-start(bf16[256,1536]{1,0:T(8,128)(2,1)} %get-tuple-element.95), channel_id=1, source_target_pairs={{0,4},{4,0},{1,5},{5,1},{2,6},{6,2},{3,7},{7,3},{8,12},{12,8},{9,1... | collective-permute-start | bytes 2359304 | tf_op jit(solution)/shard_map/ppermute | solution.py:19
  560.5 101.6 %collective-permute-start.38 = (bf16[256,768]{1,0:T(8,128)(2,1)}, bf16[256,768]{1,0:T(8,128)(2,1)}, u32[]{:S(2)}, u32[]{:S(2)}) collective-permute-start(bf16[256,768]{1,0:T(8,128)(2,1)} %constant_dynamic-slice_fusion.12), channel_id=1, source_target_pairs={{0,4},{4,0},{1,5},{5,1},{2,6},{6,2},{3,7},{7,3},{8,12},{12,8},{9,1... | collective-permute-start | bytes 1179656 | tf_op jit(solution)/shard_map/ppermute | solution.py:19
  654.3 61.9 %collective-permute-start.86 = (bf16[768,768]{0,1:T(8,128)(2,1)}, bf16[768,768]{0,1:T(8,128)(2,1)}, u32[]{:S(2)}, u32[]{:S(2)}) collective-permute-start(bf16[768,768]{0,1:T(8,128)(2,1)} %add_convert_fusion.5), channel_id=1, source_target_pairs={{0,16},{8,24},{16,0},{24,8},{1,17},{9,25},{17,1},{25,9},{2,18},{10... | collective-permute-start | bytes 3538952 | tf_op jit(solution)/shard_map/ppermute | solution.py:19
  658.0 62.8 %collective-permute-start.82 = (bf16[768,768]{0,1:T(8,128)(2,1)}, bf16[768,768]{0,1:T(8,128)(2,1)}, u32[]{:S(2)}, u32[]{:S(2)}) collective-permute-start(bf16[768,768]{0,1:T(8,128)(2,1)} %add_convert_fusion.7), channel_id=1, source_target_pairs={{0,16},{8,24},{16,0},{24,8},{1,17},{9,25},{17,1},{25,9},{2,18},{10... | collective-permute-start | bytes 3538952 | tf_op jit(solution)/shard_map/ppermute | solution.py:19
  661.2 69.7 %collective-permute-start.78 = (bf16[768,768]{0,1:T(8,128)(2,1)}, bf16[768,768]{0,1:T(8,128)(2,1)}, u32[]{:S(2)}, u32[]{:S(2)}) collective-permute-start(bf16[768,768]{0,1:T(8,128)(2,1)} %add_convert_fusion.9), channel_id=1, source_target_pairs={{0,16},{8,24},{16,0},{24,8},{1,17},{9,25},{17,1},{25,9},{2,18},{10... | collective-permute-start | bytes 3538952 | tf_op jit(solution)/shard_map/ppermute | solution.py:19
  694.3 72.6 %collective-permute-start.66 = (bf16[2,2,192,768]{3,2,1,0:T(8,128)(2,1)}, bf16[2,2,192,768]{3,2,1,0:T(8,128)(2,1)}, u32[]{:S(2)}, u32[]{:S(2)}) collective-permute-start(bf16[2,2,192,768]{3,2,1,0:T(8,128)(2,1)} %bitcast.330), channel_id=1, source_target_pairs={{0,8},{8,0},{16,24},{24,16},{1,9},{9,1},{17,25},{25,17},{2,10},{10... | collective-permute-start | bytes 3538952 | tf_op jit(solution)/shard_map/ppermute | solution.py:19
  720.8 64.6 %collective-permute-start.87 = (bf16[768,768]{0,1:T(8,128)(2,1)}, bf16[768,768]{0,1:T(8,128)(2,1)}, u32[]{:S(2)}, u32[]{:S(2)}) collective-permute-start(bf16[768,768]{0,1:T(8,128)(2,1)} %add_convert_fusion.4), channel_id=1, source_target_pairs={{0,8},{8,0},{16,24},{24,16},{1,9},{9,1},{17,25},{25,17},{2,10},{10... | collective-permute-start | bytes 3538952 | tf_op jit(solution)/shard_map/ppermute | solution.py:19
  728.1 97.2 %collective-permute-start.83 = (bf16[768,768]{0,1:T(8,128)(2,1)}, bf16[768,768]{0,1:T(8,128)(2,1)}, u32[]{:S(2)}, u32[]{:S(2)}) collective-permute-start(bf16[768,768]{0,1:T(8,128)(2,1)} %add_convert_fusion.6), channel_id=1, source_target_pairs={{0,8},{8,0},{16,24},{24,16},{1,9},{9,1},{17,25},{25,17},{2,10},{10... | collective-permute-start | bytes 3538952 | tf_op jit(solution)/shard_map/ppermute | solution.py:19
  766.1 69.7 %collective-permute-start.79 = (bf16[768,768]{0,1:T(8,128)(2,1)S(1)}, bf16[768,768]{0,1:T(8,128)(2,1)S(1)}, u32[]{:S(2)}, u32[]{:S(2)}) collective-permute-start(bf16[768,768]{0,1:T(8,128)(2,1)S(1)} %add_convert_fusion.8), channel_id=1, source_target_pairs={{0,8},{8,0},{16,24},{24,16},{1,9},{9,1},{17,25},{25,17},{2,10},{10... | collective-permute-start | bytes 3538952 | tf_op jit(solution)/shard_map/ppermute | solution.py:19
  (183 other events, 2939.5 us)

commit v2 on v1

--- a/solution.py
+++ b/solution.py
@@ -232,6 +232,319 @@
     )(rot, cosine, sine, keys, values, start, grad)
 
 
+def experts_kernel(
+    own_ref,
+    cot_ref,
+    table_ref,
+    gate_ref,
+    up_ref,
+    down_ref,
+    sum_ref,
+    out_part_ref,
+    mine_ref,
+    theirs_ref,
+    mine_down_ref,
+    theirs_down_ref,
+    expert_in,
+    gate_grad,
+    up_grad,
+    hidden,
+    send_stage,
+    arrived,
+    stage,
+    stage_down,
+    ag_recv,
+    ag_right,
+    ag_left,
+    rs_recv,
+    rs_send,
+    local_sem,
+    core_send,
+    core_recv,
+    down_local,
+    down_send,
+    down_recv,
+):
+    col, dp = lax.axis_index("col"), lax.axis_index("dp")
+    core = dp % 2
+    last = cot_ref.shape[0] - 1
+    rows, width = own_ref.shape
+    half = width // 2
+    inner = (col > 0) & (col < last)
+
+    barrier = pltpu.get_barrier_semaphore()
+
+    def greet(device):
+        pl.semaphore_signal(barrier, inc=1, device_id=device, device_id_type=pl.DeviceIdType.MESH)
+
+    greet({"dp": dp + 1 - 2 * core})
+    pl.when(col > 0)(lambda: greet({"col": col - 1}))
+    pl.when(col < last)(lambda: greet({"col": col + 1}))
+    expert_in[col] = own_ref[...]
+    pl.when(inner)(lambda: pl.semaphore_wait(barrier, 3))
+    pl.when(jnp.logical_not(inner))(lambda: pl.semaphore_wait(barrier, 2))
+
+    def ag_copy(block, right):
+        return pltpu.make_async_remote_copy(
+            src_ref=expert_in.at[block],
+            dst_ref=expert_in.at[block],
+            send_sem=(ag_right if right else ag_left).at[block],
+            recv_sem=ag_recv.at[block],
+            device_id={"col": col + 1 if right else col - 1},
+            device_id_type=pl.DeviceIdType.MESH,
+        )
+
+    def rs_copy(block, part, right):
+        neighbour = col + 1 if right else col - 1
+        slot = block if right else jnp.where(block == neighbour, last + 1, block)
+        return pltpu.make_async_remote_copy(
+            src_ref=send_stage.at[block, part],
+            dst_ref=arrived.at[slot, part],
+            send_sem=rs_send.at[block, part],
+            recv_sem=rs_recv.at[slot, part],
+            device_id={"col": neighbour},
+            device_id_type=pl.DeviceIdType.MESH,
+        )
+
+    def rs_wait(slot, part):
+        pltpu.make_async_remote_copy(
+            src_ref=arrived.at[slot, part],
+            dst_ref=arrived.at[slot, part],
+            send_sem=rs_send.at[0, part],
+            recv_sem=rs_recv.at[slot, part],
+            device_id={"col": jnp.where(col > 0, col - 1, col + 1)},
+            device_id_type=pl.DeviceIdType.MESH,
+        ).wait_recv()
+
+    pl.when(col < last)(lambda: ag_copy(col, True).start())
+    pl.when(col > 0)(lambda: ag_copy(col, False).start())
+
+    def compute(block):
+        tokens = expert_in[block]
+        grads = cot_ref[block]
+        table = table_ref[block]
+        experts = table.shape[1]
+        units = width // experts
+        for g in range(2):
+            cols = slice(g * half, (g + 1) * half)
+            gate = dot(tokens, gate_ref[:, cols])
+            up = dot(tokens, up_ref[:, cols])
+            grad = dot(grads, down_ref[cols, :], 1, 1)
+            lane = lax.broadcasted_iota(jnp.int32, gate.shape, 1)
+            first = g * experts // 2
+            chosen = jnp.broadcast_to(table[:, first : first + 1], gate.shape)
+            for e in range(1, experts // 2):
+                chosen = jnp.where(lane >= e * units, table[:, first + e : first + e + 1], chosen)
+            sigmoid = 1.0 / (1.0 + jnp.exp(-gate))
+            silu = gate * sigmoid
+            grad = grad * chosen
+            hidden[block, :, cols] = (silu * up * chosen).astype(low)
+            gate_grad[block, :, cols] = (
+                grad * up * (sigmoid * (1.0 + gate * (1.0 - sigmoid)))
+            ).astype(low)
+            up_grad[block, :, cols] = (grad * silu).astype(low)
+        gates_now, ups_now = gate_grad[block], up_grad[block]
+        for part in range(2):
+            cols = slice(part * half, (part + 1) * half)
+            total = dot(gates_now, gate_ref[cols, :], 1, 1) + dot(ups_now, up_ref[cols, :], 1, 1)
+            send_stage[block, part] = total.astype(low)
+            pl.when((col == 0) & (block != col))(lambda: rs_copy(block, part, True).start())
+            pl.when((col == last) & (block != col))(lambda: rs_copy(block, part, False).start())
+        out_part_ref[block] = dot(hidden[block], down_ref[...]).astype(low)
+
+    def step(i, carry):
+        apart = (i + 1) // 2
+        from_left = i % 2 == 1
+
+        @pl.when(from_left & (col - apart >= 0))
+        def _():
+            block = col - apart
+            ag_copy(block, True).wait_recv()
+            pl.when(col < last)(lambda: ag_copy(block, True).start())
+
+        @pl.when(from_left & (col + apart <= last))
+        def _():
+            block = col + apart
+            ag_copy(block, False).wait_recv()
+            pl.when(col > 0)(lambda: ag_copy(block, False).start())
+
+        block = jnp.where(from_left, col - apart, col + apart)
+        pl.when((block >= 0) & (block <= last))(lambda: compute(block))
+        return carry
+
+    lax.fori_loop(0, 2 * last + 1, step, 0)
+
+    def forward(block, right):
+        for part in range(2):
+            rs_wait(block, part)
+            send_stage[block, part] = (
+                send_stage[block, part].astype(full) + arrived[block, part].astype(full)
+            ).astype(low)
+            rs_copy(block, part, right).start()
+
+    def event(number):
+        blocks = ((2, 1), (3, 0), (0, 3))[number]
+        pl.when(col == 1)(lambda: forward(blocks[0], number < 2))
+        pl.when(col == 2)(lambda: forward(blocks[1], number == 2))
+
+    def to_partner(source, target, send_sem, recv_sem):
+        return pltpu.make_async_remote_copy(
+            src_ref=source,
+            dst_ref=target,
+            send_sem=send_sem,
+            recv_sem=recv_sem,
+            device_id={"dp": dp + 1 - 2 * core},
+            device_id_type=pl.DeviceIdType.MESH,
+        )
+
+    size = stage.shape[1]
+    tiles = width // size
+    flat_in = expert_in[...].reshape((last + 1) * rows, width)
+
+    def weight_copies(which, tile):
+        at = which * tiles + tile
+        slot = at % 2
+        target = pl.ds(tile * size, size)
+        return (
+            to_partner(
+                stage.at[2 * slot], theirs_ref.at[which, target], core_send.at[at], core_recv.at[at]
+            ),
+            pltpu.make_async_copy(
+                stage.at[2 * slot + 1], mine_ref.at[which, target], local_sem.at[at]
+            ),
+        )
+
+    def weight_tile(which, tile):
+        right = (gate_grad, up_grad)[which]
+        at = which * tiles + tile
+        if at >= 2:
+            before = weight_copies((at - 2) // tiles, (at - 2) % tiles)
+            before[0].wait_send()
+            before[1].wait()
+        left = expert_in[:, :, tile * size : (tile + 1) * size].reshape(-1, size)
+        for order in range(2):
+            which_half = 1 - core if order == 0 else core
+            cols = pl.ds(pl.multiple_of(which_half * half, half), half)
+            stage[2 * (at % 2) + order] = dot(
+                left, right[:, :, cols].reshape(-1, half), 0, 0
+            ).astype(low)
+        for copy in weight_copies(which, tile):
+            copy.start()
+
+    size_down = stage_down.shape[1]
+    tiles_down = half // size_down
+
+    def down_copy(order, tile):
+        at = order * tiles_down + tile
+        target = pl.ds(tile * size_down, size_down)
+        if order == 0:
+            return to_partner(
+                stage_down.at[at], theirs_down_ref.at[target], down_send.at[tile], down_recv.at[tile]
+            )
+        return pltpu.make_async_copy(
+            stage_down.at[at], mine_down_ref.at[target], down_local.at[tile]
+        )
+
+    def down_tile(order, tile):
+        which_half = 1 - core if order == 0 else core
+        first = pl.multiple_of(which_half * half + tile * size_down, 128)
+        left = hidden[:, :, pl.ds(first, size_down)].reshape(-1, size_down)
+        stage_down[order * tiles_down + tile] = dot(
+            left, cot_ref[...].reshape(-1, width), 0, 0
+        ).astype(low)
+        down_copy(order, tile).start()
+
+    for tile in range(tiles):
+        weight_tile(0, tile)
+    event(0)
+    for tile in range(tiles):
+        weight_tile(1, tile)
+    for tile in range(tiles_down):
+        down_tile(0, tile)
+    event(1)
+    for tile in range(tiles_down):
+        down_tile(1, tile)
+    event(2)
+
+    for part in range(2):
+        cols = slice(part * half, (part + 1) * half)
+        sum_ref[:, cols] = send_stage[col, part].astype(full)
+
+        @pl.when(col > 0)
+        def _():
+            rs_wait(col, part)
+            sum_ref[:, cols] += arrived[col, part].astype(full)
+
+        @pl.when(col < last)
+        def _():
+            rs_wait(last + 1, part)
+            sum_ref[:, cols] += arrived[last + 1, part].astype(full)
+
+    for block in range(last + 1):
+        pl.when((block <= col) & (col < last))(lambda: ag_copy(block, True).wait_send())
+        pl.when((block >= col) & (col > 0))(lambda: ag_copy(block, False).wait_send())
+        for part in range(2):
+            pl.when(block > col)(lambda: rs_copy(block, part, True).wait_send())
+            pl.when(block < col)(lambda: rs_copy(block, part, False).wait_send())
+    for at in range(2 * tiles):
+        remote, local = weight_copies(at // tiles, at % tiles)
+        remote.wait_recv()
+        if at >= 2 * tiles - 2:
+            remote.wait_send()
+            local.wait()
+    for tile in range(tiles_down):
+        down_copy(0, tile).wait()
+        down_copy(1, tile).wait()
+
+
+def experts_call(own, cot, table, gate_all, up_all, down_all):
+    rows, width = own.shape
+    blocks, half = cot.shape[0], width // 2
+    vmem = pl.BlockSpec(memory_space=pltpu.VMEM)
+    anywhere = pl.BlockSpec(memory_space=pl.ANY)
+    dma = pltpu.SemaphoreType.DMA
+    size, size_down = width // 3, half // 2
+    return pl.pallas_call(
+        experts_kernel,
+        in_specs=[vmem] * 6,
+        out_specs=[vmem, vmem] + [anywhere] * 4,
+        out_shape=[
+            jax.ShapeDtypeStruct((rows, width), full),
+            jax.ShapeDtypeStruct((blocks, rows, width), low),
+            jax.ShapeDtypeStruct((2, width, half), low),
+            jax.ShapeDtypeStruct((2, width, half), low),
+            jax.ShapeDtypeStruct((half, width), low),
+            jax.ShapeDtypeStruct((half, width), low),
+        ],
+        scratch_shapes=[pltpu.VMEM((blocks, rows, width), low)] * 4
+        + [
+            pltpu.VMEM((blocks, 2, rows, half), low),
+            pltpu.VMEM((blocks + 1, 2, rows, half), low),
+            pltpu.VMEM((4, size, half), low),
+            pltpu.VMEM((4, size_down, width), low),
+            dma((blocks,)),
+            dma((blocks,)),
+            dma((blocks,)),
+            dma((blocks + 1, 2)),
+            dma((blocks, 2)),
+            dma((6,)),
+            dma((6,)),
+            dma((6,)),
+            dma((2,)),
+            dma((2,)),
+            dma((2,)),
+        ],
+        compiler_params=pltpu.CompilerParams(
+            collective_id=1, has_side_effects=True, vmem_limit_bytes=60 * 2**20
+        ),
+        cost_estimate=pl.CostEstimate(
+            flops=9 * 2 * blocks * rows * width * width,
+            bytes_accessed=12 * width * width,
+            transcendentals=blocks * rows * width,
+        ),
+    )(own, cot, table, gate_all, up_all, down_all)
+
+
 def rotate(matrix, cosine, sine):
     return matrix * cosine + jnp.roll(matrix, head_dim // 2, axis=1) * sine
 
@@ -327,17 +640,17 @@
     kept = lax.dynamic_slice_in_dim(cotangent, row * own_tokens, own_tokens, 0)
     sent = lax.dynamic_slice_in_dim(cotangent, (1 - row) * own_tokens, own_tokens, 0)
     cot_own = pair(row, kept, swap(sent, "row", 1), 1)
-    cot_all = jnp.concatenate(gather_col(cot_own, col), axis=0)
+    cot_slots = gather_col(cot_own, col)
+    for bit in (1, 2):
+        cot_slots = [
+            jnp.where(col & bit == 0, cot_slots[k], cot_slots[k ^ bit]) for k in range(cols)
+        ]
+    cot_all = jnp.stack(cot_slots)
 
     chosen = routes[:, :, None] == jnp.arange(experts, dtype=jnp.int32)[None, None, :]
     table = jnp.sum(jnp.where(chosen, route_gates[:, :, None], 0.0), axis=1)
-    slot_tables = [
-        lax.dynamic_slice_in_dim(table, (col ^ k) * tokens + row * own_tokens, own_tokens, 0)
-        for k in range(cols)
-    ]
-    widen = jnp.repeat(jnp.eye(experts, dtype=full), units, axis=1)
-    gates = jnp.dot(
-        jnp.concatenate(slot_tables, axis=0), widen, precision=lax.Precision.HIGHEST
+    tables = lax.dynamic_index_in_dim(
+        table.reshape(cols, 2, own_tokens, experts), row, 1, False
     )
 
     inputs_full = inputs_all.astype(full)
@@ -374,31 +687,26 @@
     middle = inputs_own.astype(full) + branch
     second_scale = lax.rsqrt(jnp.mean(middle * middle, axis=1, keepdims=True) + epsilon)
     expert_own = (middle * second_scale * mixer_all[None, :]).astype(low)
-    expert_in = jnp.concatenate(gather_col(expert_own, col), axis=0)
-
-    gate = dot(expert_in, gate_all)
-    up = dot(expert_in, up_all)
-    hidden_grad = dot(cot_all, down_all, 1, 1) * gates
-    sigmoid = jax.nn.sigmoid(gate)
-    silu = gate * sigmoid
-    hidden = (silu * up * gates).astype(low)
-    gate_grad = (hidden_grad * up * (sigmoid * (1.0 + gate * (1.0 - sigmoid)))).astype(low)
-    up_grad = (hidden_grad * silu).astype(low)
-    in_part = (dot(gate_grad, gate_all, 1, 1) + dot(up_grad, up_all, 1, 1)).astype(low)
-    second_grad = scatter_col(in_part.reshape(cols, own_tokens, width), col)
-    out_part = dot(hidden, down_all).astype(low)
-    experts_out = scatter_col(out_part.reshape(cols, own_tokens, width), col)
+    (
+        second_grad,
+        out_part,
+        mine_parts,
+        their_parts,
+        mine_down,
+        their_down,
+    ) = experts_call(expert_own, cot_all, tables, gate_all, up_all, down_all)
+    by_slot = jnp.stack(
+        [lax.dynamic_index_in_dim(out_part, col ^ k, 0, False) for k in range(cols)]
+    )
+    experts_out = scatter_col(by_slot, col)
     outputs_own = (middle + experts_out).astype(low)
     theirs = lax.dynamic_slice_in_dim(outputs_own, (1 - row) * part_width, part_width, 1)
     mine = lax.dynamic_slice_in_dim(outputs_own, row * part_width, part_width, 1)
     outputs = pair(row, mine, swap(theirs, "row", 1), 0)
-
-    gate_part = dot(expert_in, gate_grad, 0, 0).astype(low)
-    up_part = dot(expert_in, up_grad, 0, 0).astype(low)
-    down_part = dot(hidden, cot_all, 0, 0).astype(low)
-
-    def expert_total(part, hidden_axis):
-        half = halves_sum(part, core, hidden_axis)
+    both_parts = (mine_parts.astype(full) + their_parts.astype(full)).astype(low)
+    both_down = (mine_down.astype(full) + their_down.astype(full)).astype(low)
+
+    def expert_total(half, hidden_axis):
         axis = 1 - hidden_axis
         mine = lax.dynamic_slice_in_dim(half, row * part_width, part_width, axis)
         theirs = lax.dynamic_slice_in_dim(half, (1 - row) * part_width, part_width, axis)
@@ -409,9 +717,9 @@
     def by_expert(flat):
         return flat.reshape(part_width, experts, units).transpose(1, 0, 2)
 
-    gate_total = by_expert(expert_total(gate_part, 1))
-    up_total = by_expert(expert_total(up_part, 1))
-    down_total = expert_total(down_part, 0).reshape(experts, units, part_width)
+    gate_total = by_expert(expert_total(both_parts[0], 1))
+    up_total = by_expert(expert_total(both_parts[1], 1))
+    down_total = expert_total(both_down, 0).reshape(experts, units, part_width)
 
     weighted = mixer_all[None, :] * second_grad
     inner = jnp.sum(weighted * middle, axis=1, keepdims=True)
@@ -473,9 +781,12 @@
     )
     query_total, keyval_total = joint_total[:, :query_block], joint_total[:, query_block:]
 
-    norm_total = lax.psum(norm_partial, ("dp", "col"))
-    mixer_sum = lax.psum(mixer_partial, ("dp", "row", "col"))
-    mixer_total = lax.dynamic_slice_in_dim(mixer_sum, row * part_width, part_width, 0)
+    spread_norm = jnp.where(
+        jnp.arange(2)[:, None] == row, norm_partial[None, :], 0.0
+    ).reshape(width)
+    gain_sums = lax.psum(jnp.stack([spread_norm, mixer_partial]), ("dp", "row", "col"))
+    gain_sums = lax.dynamic_slice_in_dim(gain_sums, row * part_width, part_width, 1)
+    norm_total, mixer_total = gain_sums[0], gain_sums[1]
     return (
         outputs,
         input_grad,

time: 889 us -> 703 us (0.79)
  Pallas kernels: 21.4 us -> 134 us
  matrix products: 104 us -> 15.5 us
  blocking collectives: 122 us -> 47.9 us
  starting transfers between devices: 205 us -> 142 us
  other arithmetic: 107 us -> 77.2 us
  local copies, waits for them, and re-layouts: 84.4 us -> 61.3 us
  waiting for transfers between devices: 228 us -> 212 us
    pallas_call x0 -> x1, Pallas kernels: none -> 113 us  [experts_call(): pl.pallas_call(experts_kernel, in_specs=[vmem] * 6, out_specs=[vmem, vmem...]
    ppermute x42 -> x39, waiting for transfers between devices: 88.8 us -> 185 us  [swap(): return lax.ppermute(block, axis, [(i, i ^ bit) for i in range(count)])]
    dot_general x15 -> x6, matrix products: 96.5 us -> 15.5 us  [dot(): lax.dot_general(left, right, (((left_dim,), (right_dim,)), ((), ())), pre...]
    psum x2 -> x1, blocking collectives: 122 us -> 47.9 us  [shards(): lax.psum(jnp.stack([spread_norm, mixer_partial]), ('dp', 'row', 'col'))]
    ppermute x12 -> x9, waiting for transfers between devices: 54.1 us -> 5.6 us  [scatter_col(): lax.ppermute(to_right, 'col', [(i, i + 1) for i in range(min(step, count...]
    ppermute x12 -> x9, waiting for transfers between devices: 45.7 us -> 1.25 us  [scatter_col(): lax.ppermute(to_left, 'col', [(i, i - 1) for i in range(count - 1, count...]
    ppermute x8, starting transfers between devices: 37.6 us -> 15.2 us  [spread(): arrived.append(lax.ppermute(part, ('row', 'col'), route))]
    ppermute x6 -> x3, waiting for transfers between devices: 30.3 us -> 8.29 us  [gather_col(): lax.ppermute(from_left[-1], 'col', [(i, i + 1) for i in range(step - 1, c...]
  transfers between devices with their start and end apart: 88 -> 73, of which waited for: 25 -> 23; matrix products, arithmetic and copies ran while one was open for 24% -> 20% of each run, Pallas kernels for 2% -> 2%
where the time goes in v2:
time: 703 us; the launch traced here: 692 us
  waiting for transfers between devices  212 us (30%)
  starting transfers between devices  142 us (20%)
  Pallas kernels  134 us (19%)
  other arithmetic  77.2 us (11%)
  local copies, waits for them, and re-layouts  61.3 us (9%)
  blocking collectives  47.9 us (7%)
  matrix products  15.5 us (2%)
    ppermute x39, waiting for transfers between devices, swap(): return lax.ppermute(block, axis, [(i, i ^ bit) for i in range(count)])  185 us
    pallas_call x1, Pallas kernels, experts_call(): pl.pallas_call(experts_kernel, in_specs=[vmem] * 6, out_specs=[vmem, vmem...  113 us
    ppermute x39, starting transfers between devices, swap(): return lax.ppermute(block, axis, [(i, i ^ bit) for i in range(count)])  64.8 us
    psum x1, blocking collectives, shards(): lax.psum(jnp.stack([spread_norm, mixer_partial]), ('dp', 'row', 'col'))  47.9 us
    ppermute x9, starting transfers between devices, scatter_col(): lax.ppermute(to_left, 'col', [(i, i - 1) for i in range(count - 1, count...  26 us
    ppermute x9, starting transfers between devices, scatter_col(): lax.ppermute(to_right, 'col', [(i, i + 1) for i in range(min(step, count...  17.1 us
    dot_general x6, matrix products, dot(): lax.dot_general(left, right, (((left_dim,), (right_dim,)), ((), ())), pre...  15.5 us
    ppermute x8, starting transfers between devices, spread(): arrived.append(lax.ppermute(part, ('row', 'col'), route))  15.2 us
  transfers between devices with their start and end apart: 73, of which 23 were waited for; matrix products, arithmetic and copies ran while one was open for 20% of the time, Pallas kernels for 2%

profile of v2, /device:TPU:17, one launch (start us, length us, event | category | flops | bytes accessed | tf_op | source)
XLA Modules:
  0.0 692.4 jit_solution(10162759283475958184)
XLA Ops:
  28.8 5.0 collective-permute-start.2
  37.5 8.0 %collective-permute-start.30 = (bf16[384,768]{1,0:T(8,128)(2,1)}, bf16[384,768]{1,0:T(8,128)(2,1)S(1)}, u32[]{:S(2)}, u32[]{:S(2)}) collective-permute-start(bf16[384,768]{1,0:T(8,128)(2,1)} %constant_dynamic-slice_fusion.12), channel_id=1, source_target_pairs={{0,4},{4,0},{1,5},{5,1},{2,6},{6,2},{3,7},{7,3},{8,12},{12,8},{9,1... | collective-permute-start | bytes 1769480 | tf_op jit(solution)/shard_map/ppermute | solution.py:19
  54.9 42.9 %collective-permute-done.17 = bf16[256,768]{1,0:T(8,128)(2,1)S(1)} collective-permute-done((bf16[256,768]{1,0:T(8,128)(2,1)S(1)}, bf16[256,768]{1,0:T(8,128)(2,1)S(1)}, u32[]{:S(2)}, u32[]{:S(2)}) %collective-permute-start.17) | collective-permute-done | bytes 393248 | tf_op jit(solution)/shard_map/ppermute | solution.py:19
  101.5 14.7 %collective-permute-done = bf16[512,768]{1,0:T(8,128)(2,1)S(1)} collective-permute-done((bf16[512,768]{1,0:T(8,128)(2,1)S(1)}, bf16[512,768]{1,0:T(8,128)(2,1)S(1)}, u32[]{:S(2)}, u32[]{:S(2)}) %collective-permute-start) | collective-permute-done | bytes 786464 | tf_op jit(solution)/shard_map/ppermute | solution.py:19
  123.6 5.9 collective-permute-done.28
  134.1 8.0 %collective-permute-done.31 = bf16[384,768]{1,0:T(8,128)(2,1)S(1)} collective-permute-done((bf16[384,768]{1,0:T(8,128)(2,1)S(1)}, bf16[384,768]{1,0:T(8,128)(2,1)S(1)}, u32[]{:S(2)}, u32[]{:S(2)}) %collective-permute-start.31) | collective-permute-done | bytes 589856 | tf_op jit(solution)/shard_map/ppermute | solution.py:19
  147.0 7.8 %collective-permute-done.25 = bf16[192,1536]{1,0:T(8,128)(2,1)S(1)} collective-permute-done((bf16[192,1536]{1,0:T(8,128)(2,1)S(1)}, bf16[192,1536]{1,0:T(8,128)(2,1)S(1)}, u32[]{:S(2)}, u32[]{:S(2)}) %collective-permute-start.25) | collective-permute-done | bytes 589856 | tf_op jit(solution)/shard_map/ppermute | solution.py:19
  154.8 6.0 collective-permute-start.32
  174.2 8.3 %collective-permute-done.20 = bf16[256,1536]{1,0:T(8,128)(2,1)} collective-permute-done((bf16[256,1536]{1,0:T(8,128)(2,1)S(1)}, bf16[256,1536]{1,0:T(8,128)(2,1)}, u32[]{:S(2)}, u32[]{:S(2)}) %collective-permute-start.20) | collective-permute-done | bytes 786464 | tf_op jit(solution)/shard_map/ppermute | solution.py:39
  212.5 8.9 %shard_map.204 = (bf16[512,768]{1,0:T(8,128)(2,1)S(1)}, bf16[512,768]{1,0:T(8,128)(2,1)S(1)}) custom-call(f32[512,1024]{1,0:T(8,128)S(1)} %fusion.7.pre_ref, f32[512,128]{1,0:T(8,128)S(1)} %get-tuple-element.199.cosine_ref, f32[512,128]{1,0:T(8,128)S(1)} %get-tuple-element.47.sine_ref, bf16[1024,128]{1,0:T(8,128)(2,1)S(1)} %get-tuple-element.198.key_ref, ...), custom_call_target="tpu_custom_call" | custom-call | flops 1207959552 | bytes 3145728 | tf_op jit(solution)/shard_map/pallas_call | solution.py:182
  228.1 14.5 %collective-permute-done.16 = bf16[256,1536]{1,0:T(8,128)(2,1)S(1)} collective-permute-done((bf16[256,1536]{1,0:T(8,128)(2,1)S(1)}, bf16[256,1536]{1,0:T(8,128)(2,1)S(1)}, u32[]{:S(2)}, u32[]{:S(2)}) %collective-permute-start.16) | collective-permute-done | bytes 786464 | tf_op jit(solution)/shard_map/ppermute | solution.py:19
  245.3 112.6 %shard_map.205 = (f32[256,1536]{1,0:T(8,128)}, bf16[4,256,1536]{2,1,0:T(8,128)(2,1)}, bf16[2,1536,768]{2,1,0:T(8,128)(2,1)}, bf16[2,1536,768]{2,1,0:T(8,128)(2,1...) custom-call(bf16[256,1536]{1,0:T(8,128)(2,1)} %multiply_convert_fusion.own_ref, ...), custom_call_target="tpu_custom_call" | custom-call | flops 43486543872 | bytes 28311552 | tf_op jit(solution)/shard_map/pallas_call | solution.py:507
  376.1 16.1 %collective-permute-done.67 = bf16[768,768]{1,0:T(8,128)(2,1)S(1)} collective-permute-done((bf16[768,768]{1,0:T(8,128)(2,1)S(1)}, bf16[768,768]{1,0:T(8,128)(2,1)S(1)}, u32[]{:S(2)}, u32[]{:S(2)}) %collective-permute-start.67) | collective-permute-done | bytes 1179680 | tf_op jit(solution)/shard_map/ppermute | solution.py:19
  401.6 15.8 %collective-permute-done.64 = bf16[768,768]{1,0:T(8,128)(2,1)S(1)} collective-permute-done((bf16[768,768]{1,0:T(8,128)(2,1)S(1)}, bf16[768,768]{1,0:T(8,128)(2,1)S(1)}, u32[]{:S(2)}, u32[]{:S(2)}) %collective-permute-start.64) | collective-permute-done | bytes 1179680 | tf_op jit(solution)/shard_map/ppermute | solution.py:19
  419.0 23.8 %collective-permute-done.70 = bf16[768,768]{1,0:T(8,128)(2,1)S(1)} collective-permute-done((bf16[768,768]{1,0:T(8,128)(2,1)S(1)}, bf16[768,768]{1,0:T(8,128)(2,1)S(1)}, u32[]{:S(2)}, u32[]{:S(2)}) %collective-permute-start.70) | collective-permute-done | bytes 1179680 | tf_op jit(solution)/shard_map/ppermute | solution.py:19
  457.9 9.1 %collective-permute-done.71 = bf16[768,768]{1,0:T(8,128)(2,1)S(1)} collective-permute-done((bf16[768,768]{1,0:T(8,128)(2,1)S(1)}, bf16[768,768]{1,0:T(8,128)(2,1)S(1)}, u32[]{:S(2)}, u32[]{:S(2)}) %collective-permute-start.71) | collective-permute-done | bytes 1179680 | tf_op jit(solution)/shard_map/ppermute | solution.py:19
  502.4 6.0 reshape.190
  508.3 12.5 %shard_map.206 = (bf16[512,768]{1,0:T(8,128)(2,1)S(1)}, f32[1024,128]{1,0:T(8,128)S(1)}, f32[1024,128]{1,0:T(8,128)S(1)}) custom-call(bf16[512,768]{1,0:T(8,128)(2,1)S(1)} %get-tuple-element.24.rot_ref, f32[512,128]{1,0:T(8,128)S(1)} %get-tuple-element.199.cosine_ref, f32[512,128]{1,0:T(8,128)S(1)} %get-tuple-element.47.sine_ref, ...), custom_call_target="tpu_custom_call" | custom-call | flops 3221225472 | bytes 3145728 | tf_op jit(solution)/shard_map/pallas_call | solution.py:208
  535.9 4.8 reshape.189
  557.5 7.3 %collective-permute-done.55 = bf16[2,192,768]{2,1,0:T(8,128)(2,1)S(1)} collective-permute-done((bf16[2,192,768]{2,1,0:T(8,128)(2,1)S(1)}, bf16[2,192,768]{2,1,0:T(8,128)(2,1)S(1)}, u32[]{:S(2)}, u32[]{:S(2)}) %collective-permute-start.55) | collective-permute-done | bytes 589856 | tf_op jit(solution)/shard_map/ppermute | solution.py:19
  566.3 15.4 %collective-permute-done.45 = bf16[2,384,512]{2,1,0:T(8,128)(2,1)S(1)} collective-permute-done((bf16[2,384,512]{2,1,0:T(8,128)(2,1)S(1)}, bf16[2,384,512]{2,1,0:T(8,128)(2,1)S(1)}, u32[]{:S(2)}, u32[]{:S(2)}) %collective-permute-start.45) | collective-permute-done | bytes 786464 | tf_op jit(solution)/shard_map/ppermute | solution.py:19
  595.1 8.0 %collective-permute-start.60 = (bf16[192,768]{1,0:T(8,128)(2,1)S(1)}, bf16[192,768]{1,0:T(8,128)(2,1)S(1)}, u32[]{:S(2)}, u32[]{:S(2)}) collective-permute-start(bf16[192,768]{1,0:T(8,128)(2,1)S(1)} %get-tuple-element.122), channel_id=1, source_target_pairs={{3,2},{2,1},{7,6},{6,5},{11,10},{10,9},{15,14},{14,13},{19,18},{18... | collective-permute-start | bytes 884744 | tf_op jit(solution)/shard_map/ppermute | solution.py:69
  607.5 5.0 collective-permute-start.50
  625.5 47.9 %psum.7 = f32[2,1536]{1,0:T(2,128)} all-reduce(f32[2,1536]{1,0:T(2,128)S(1)} %pad_maximum_fusion.38), channel_id=1, replica_groups=mesh['dp'=4,'row'=2,'col'=4] {'dp','row','col'}, use_global_device_ids=true, to_apply=%region_9.10 | all-reduce | flops 3072 | bytes 24576 | tf_op jit(solution)/shard_map/psum | solution.py:787
  (433 shorter events, 275.4 us)
Async XLA Ops:
  2.4 31.5 %collective-permute-start.10 = (bf16[96,768]{1,0:T(8,128)(2,1)}, bf16[96,768]{1,0:T(8,128)(2,1)}, u32[]{:S(2)}, u32[]{:S(2)}) collective-permute-start(bf16[96,768]{1,0:T(8,128)(2,1)} %constant_dynamic-slice_fusion.18), channel_id=1, source_target_pairs={{0,0},{1,1},{2,4},{3,5},{4,2},{5,3},{6,6},{7,7},{8,8},{9,9},{10,12... | collective-permute-start | bytes 442376 | tf_op jit(solution)/shard_map/ppermute | solution.py:598
  5.3 29.7 %collective-permute-start.11 = (bf16[96,768]{1,0:T(8,128)(2,1)}, bf16[96,768]{1,0:T(8,128)(2,1)}, u32[]{:S(2)}, u32[]{:S(2)}) collective-permute-start(bf16[96,768]{1,0:T(8,128)(2,1)} %constant_dynamic-slice_fusion.18), channel_id=1, source_target_pairs={{0,1},{1,0},{2,5},{3,4},{4,3},{5,2},{6,7},{7,6},{8,9},{9,8},{10,13... | collective-permute-start | bytes 442376 | tf_op jit(solution)/shard_map/ppermute | solution.py:598
  37.5 81.2 %collective-permute-start.30 = (bf16[384,768]{1,0:T(8,128)(2,1)}, bf16[384,768]{1,0:T(8,128)(2,1)S(1)}, u32[]{:S(2)}, u32[]{:S(2)}) collective-permute-start(bf16[384,768]{1,0:T(8,128)(2,1)} %constant_dynamic-slice_fusion.12), channel_id=1, source_target_pairs={{0,4},{4,0},{1,5},{5,1},{2,6},{6,2},{3,7},{7,3},{8,12},{12,8},{9,1... | collective-permute-start | bytes 1769480 | tf_op jit(solution)/shard_map/ppermute | solution.py:19
  46.8 52.8 %collective-permute-start.27 = (bf16[192,1536]{1,0:T(8,128)(2,1)}, bf16[192,1536]{1,0:T(8,128)(2,1)S(1)}, u32[]{:S(2)}, u32[]{:S(2)}) collective-permute-start(bf16[192,1536]{1,0:T(8,128)(2,1)} %constant_dynamic-slice_fusion.13), channel_id=1, source_target_pairs={{0,4},{4,0},{1,5},{5,1},{2,6},{6,2},{3,7},{7,3},{8,12},{12,8},{9,1... | collective-permute-start | bytes 1769480 | tf_op jit(solution)/shard_map/ppermute | solution.py:19
  51.3 69.3 %collective-permute-start.24 = (bf16[192,1536]{1,0:T(8,128)(2,1)}, bf16[192,1536]{1,0:T(8,128)(2,1)S(1)}, u32[]{:S(2)}, u32[]{:S(2)}) collective-permute-start(bf16[192,1536]{1,0:T(8,128)(2,1)} %constant_dynamic-slice_fusion.14), channel_id=1, source_target_pairs={{0,4},{4,0},{1,5},{5,1},{2,6},{6,2},{3,7},{7,3},{8,12},{12,8},{9,1... | collective-permute-start | bytes 1769480 | tf_op jit(solution)/shard_map/ppermute | solution.py:19
  51.3 46.6 %collective-permute-start.17 = (bf16[256,768]{1,0:T(8,128)(2,1)S(1)}, bf16[256,768]{1,0:T(8,128)(2,1)S(1)}, u32[]{:S(2)}, u32[]{:S(2)}) collective-permute-start(bf16[256,768]{1,0:T(8,128)(2,1)S(1)} %constant_dynamic-slice_fusion.16), channel_id=1, source_target_pairs={{0,4},{4,0},{1,5},{5,1},{2,6},{6,2},{3,7},{7,3},{8,12},{12,8},{9,1... | collective-permute-start | bytes 1179656 | tf_op jit(solution)/shard_map/ppermute | solution.py:19
  53.5 44.5 %collective-permute-start.14 = (bf16[4,96,768]{2,1,0:T(8,128)(2,1)S(1)}, bf16[4,96,768]{2,1,0:T(8,128)(2,1)S(1)}, u32[]{:S(2)}, u32[]{:S(2)}) collective-permute-start(bf16[4,96,768]{2,1,0:T(8,128)(2,1)S(1)} %pad_maximum_fusion.32), channel_id=1, source_target_pairs={{0,16},{8,24},{16,0},{24,8},{1,17},{9,25},{17,1},{25,9},{2,18},{10... | collective-permute-start | bytes 1769480 | tf_op jit(solution)/shard_map/ppermute | solution.py:19
  99.6 61.4 %collective-permute-start.18 = (bf16[256,1536]{1,0:T(8,128)(2,1)S(1)}, bf16[256,1536]{1,0:T(8,128)(2,1)S(1)}, u32[]{:S(2)}, u32[]{:S(2)}) collective-permute-start(bf16[256,1536]{1,0:T(8,128)(2,1)S(1)} %pad_maximum_fusion.30), channel_id=1, source_target_pairs={{0,1},{1,2},{2,3},{4,5},{5,6},{6,7},{8,9},{9,10},{10,11},{12,13},{... | collective-permute-start | bytes 2359304 | tf_op jit(solution)/shard_map/ppermute | solution.py:39
  118.7 42.8 %collective-permute-start.19 = (bf16[256,1536]{1,0:T(8,128)(2,1)S(1)}, bf16[256,1536]{1,0:T(8,128)(2,1)S(1)}, u32[]{:S(2)}, u32[]{:S(2)}) collective-permute-start(bf16[256,1536]{1,0:T(8,128)(2,1)S(1)} %pad_maximum_fusion.30), channel_id=1, source_target_pairs={{1,0},{2,1},{3,2},{5,4},{6,5},{7,6},{9,8},{10,9},{11,10},{13,12},{... | collective-permute-start | bytes 2359304 | tf_op jit(solution)/shard_map/ppermute | solution.py:42
  120.9 33.9 %collective-permute-start.25 = (bf16[192,1536]{1,0:T(8,128)(2,1)S(1)}, bf16[192,1536]{1,0:T(8,128)(2,1)S(1)}, u32[]{:S(2)}, u32[]{:S(2)}) collective-permute-start(bf16[192,1536]{1,0:T(8,128)(2,1)S(1)} %collective-permute-done.24), channel_id=1, source_target_pairs={{0,16},{8,24},{16,0},{24,8},{1,17},{9,25},{17,1},{25,9},{2,18},{10... | collective-permute-start | bytes 1769480 | tf_op jit(solution)/shard_map/ppermute | solution.py:19
  129.5 35.1 %collective-permute-start.15 = (bf16[2,4,96,768]{3,2,1,0:T(8,128)(2,1)S(1)}, bf16[2,4,96,768]{3,2,1,0:T(8,128)(2,1)S(1)}, u32[]{:S(2)}, u32[]{:S(2)}) collective-permute-start(bf16[2,4,96,768]{3,2,1,0:T(8,128)(2,1)S(1)} %pad_maximum_fusion.21), channel_id=1, source_target_pairs={{0,8},{8,0},{16,24},{24,16},{1,9},{9,1},{17,25},{25,17},{2,10},{10... | collective-permute-start | bytes 3538952 | tf_op jit(solution)/shard_map/ppermute | solution.py:19
  142.2 58.7 %collective-permute-start.7 = (bf16[2,4,192,512]{3,2,1,0:T(8,128)(2,1)}, bf16[2,4,192,512]{3,2,1,0:T(8,128)(2,1)}, u32[]{:S(2)}, u32[]{:S(2)}) collective-permute-start(bf16[2,4,192,512]{3,2,1,0:T(8,128)(2,1)} %pad_maximum_fusion.15), channel_id=1, source_target_pairs={{0,8},{8,0},{16,24},{24,16},{1,9},{9,1},{17,25},{25,17},{2,10},{10... | collective-permute-start | bytes 4718600 | tf_op jit(solution)/shard_map/ppermute | solution.py:19
  154.8 32.6 %collective-permute-start.32 = (bf16[2,384,768]{2,1,0:T(8,128)(2,1)S(1)}, bf16[2,384,768]{2,1,0:T(8,128)(2,1)S(1)}, u32[]{:S(2)}, u32[]{:S(2)}) collective-permute-start(bf16[2,384,768]{2,1,0:T(8,128)(2,1)S(1)} %pad_maximum_fusion.24), channel_id=1, source_target_pairs={{0,8},{8,0},{16,24},{24,16},{1,9},{9,1},{17,25},{25,17},{2,10},{10... | collective-permute-start | bytes 3538952 | tf_op jit(solution)/shard_map/ppermute | solution.py:19
  368.9 48.6 %collective-permute-start.64 = (bf16[768,768]{1,0:T(8,128)(2,1)S(1)}, bf16[768,768]{1,0:T(8,128)(2,1)S(1)}, u32[]{:S(2)}, u32[]{:S(2)}) collective-permute-start(bf16[768,768]{1,0:T(8,128)(2,1)S(1)} %dynamic-slice_bitcast_fusion.2), channel_id=1, source_target_pairs={{0,4},{4,0},{1,5},{5,1},{2,6},{6,2},{3,7},{7,3},{8,12},{12,8},{9,1... | collective-permute-start | bytes 3538952 | tf_op jit(solution)/shard_map/ppermute | solution.py:19
  374.5 68.2 %collective-permute-start.70 = (bf16[768,768]{1,0:T(8,128)(2,1)S(1)}, bf16[768,768]{1,0:T(8,128)(2,1)S(1)}, u32[]{:S(2)}, u32[]{:S(2)}) collective-permute-start(bf16[768,768]{1,0:T(8,128)(2,1)S(1)} %constant_dynamic-slice_fusion.1), channel_id=1, source_target_pairs={{0,4},{4,0},{1,5},{5,1},{2,6},{6,2},{3,7},{7,3},{8,12},{12,8},{9,1... | collective-permute-start | bytes 3538952 | tf_op jit(solution)/shard_map/ppermute | solution.py:19
  392.5 59.2 %collective-permute-start.68 = (bf16[768,768]{1,0:T(8,128)(2,1)S(1)}, bf16[768,768]{1,0:T(8,128)(2,1)S(1)}, u32[]{:S(2)}, u32[]{:S(2)}) collective-permute-start(bf16[768,768]{1,0:T(8,128)(2,1)S(1)} %fusion.4), channel_id=1, source_target_pairs={{0,16},{8,24},{16,0},{24,8},{1,17},{9,25},{17,1},{25,9},{2,18},{10... | collective-permute-start | bytes 3538952 | tf_op jit(solution)/shard_map/ppermute | solution.py:19
  398.6 51.0 %collective-permute-start.37 = (bf16[256,1536]{1,0:T(8,128)(2,1)S(1)}, bf16[256,1536]{1,0:T(8,128)(2,1)S(1)}, u32[]{:S(2)}, u32[]{:S(2)}) collective-permute-start(bf16[256,1536]{1,0:T(8,128)(2,1)S(1)} %get-tuple-element.57), channel_id=1, source_target_pairs={{3,2},{2,1},{7,6},{6,5},{11,10},{10,9},{15,14},{14,13},{19,18},{18... | collective-permute-start | bytes 2359304 | tf_op jit(solution)/shard_map/ppermute | solution.py:69
  417.8 38.7 %collective-permute-start.65 = (bf16[768,768]{1,0:T(8,128)(2,1)S(1)}, bf16[768,768]{1,0:T(8,128)(2,1)S(1)}, u32[]{:S(2)}, u32[]{:S(2)}) collective-permute-start(bf16[768,768]{1,0:T(8,128)(2,1)S(1)} %fusion.5), channel_id=1, source_target_pairs={{0,16},{8,24},{16,0},{24,8},{1,17},{9,25},{17,1},{25,9},{2,18},{10... | collective-permute-start | bytes 3538952 | tf_op jit(solution)/shard_map/ppermute | solution.py:19
  468.3 77.4 %collective-permute-start.72 = (bf16[768,768]{1,0:T(8,128)(2,1)}, bf16[768,768]{1,0:T(8,128)(2,1)}, u32[]{:S(2)}, u32[]{:S(2)}) collective-permute-start(bf16[768,768]{1,0:T(8,128)(2,1)} %add_convert_fusion.2), channel_id=1, source_target_pairs={{0,8},{8,0},{16,24},{24,16},{1,9},{9,1},{17,25},{25,17},{2,10},{10... | collective-permute-start | bytes 3538952 | tf_op jit(solution)/shard_map/ppermute | solution.py:19
  476.6 68.9 %collective-permute-start.39 = (bf16[256,768]{1,0:T(8,128)(2,1)}, bf16[256,768]{1,0:T(8,128)(2,1)S(1)}, u32[]{:S(2)}, u32[]{:S(2)}) collective-permute-start(bf16[256,768]{1,0:T(8,128)(2,1)} %constant_dynamic-slice_fusion.7), channel_id=1, source_target_pairs={{0,4},{4,0},{1,5},{5,1},{2,6},{6,2},{3,7},{7,3},{8,12},{12,8},{9,1... | collective-permute-start | bytes 1179656 | tf_op jit(solution)/shard_map/ppermute | solution.py:19
  614.6 60.3 %collective-permute-start.43 = (f32[512]{0:T(512)}, f32[512]{0:T(512)}, u32[]{:S(2)}, u32[]{:S(2)}) collective-permute-start(f32[512]{0:T(512)} %get-tuple-element.33), channel_id=1, source_target_pairs={{0,4},{4,0},{1,5},{5,1},{2,6},{6,2},{3,7},{7,3},{8,12},{12,8},{9,1... | collective-permute-start | bytes 6152 | tf_op jit(solution)/shard_map/ppermute | solution.py:19
  615.8 59.7 %collective-permute-start.48 = (bf16[384,512]{1,0:T(8,128)(2,1)}, bf16[384,512]{1,0:T(8,128)(2,1)}, u32[]{:S(2)}, u32[]{:S(2)}) collective-permute-start(bf16[384,512]{1,0:T(8,128)(2,1)} %get-tuple-element.99), channel_id=1, source_target_pairs={{0,1},{1,2},{2,3},{4,5},{5,6},{6,7},{8,9},{9,10},{10,11},{12,13},{... | collective-permute-start | bytes 1179656 | tf_op jit(solution)/shard_map/ppermute | solution.py:68
  620.3 55.3 %collective-permute-start.51 = (bf16[384,512]{1,0:T(8,128)(2,1)}, bf16[384,512]{1,0:T(8,128)(2,1)}, u32[]{:S(2)}, u32[]{:S(2)}) collective-permute-start(bf16[384,512]{1,0:T(8,128)(2,1)} %fusion.29), channel_id=1, source_target_pairs={{3,2},{2,1},{1,0},{7,6},{6,5},{5,4},{11,10},{10,9},{9,8},{15,14},{... | collective-permute-start | bytes 1179656 | tf_op jit(solution)/shard_map/ppermute | solution.py:69
  624.3 53.8 %collective-permute-start.62 = (bf16[192,768]{1,0:T(8,128)(2,1)}, bf16[192,768]{1,0:T(8,128)(2,1)}, u32[]{:S(2)}, u32[]{:S(2)}) collective-permute-start(bf16[192,768]{1,0:T(8,128)(2,1)} %fusion.39), channel_id=1, source_target_pairs={{0,16},{8,24},{16,0},{24,8},{1,17},{9,25},{17,1},{25,9},{2,18},{10... | collective-permute-start | bytes 884744 | tf_op jit(solution)/shard_map/ppermute | solution.py:19
  (114 other events, 2160.2 us)

commit v3 on v2

v3 whole, which is shorter than its diff:
```python
import functools

import jax
import jax.numpy as jnp
from jax import lax
from jax.experimental import pallas as pl
from jax.experimental.pallas import tpu as pltpu
from jax.sharding import PartitionSpec as P

epsilon = 1e-06
rope_base = 1000000.0
head_dim = 128
low = jnp.bfloat16
full = jnp.float32


def swap(block, axis, bit):
    count = lax.axis_size(axis)
    return lax.ppermute(block, axis, [(i, i ^ bit) for i in range(count)])


def pair(bit, own, other, axis):
    first = jnp.where(bit == 0, own, other)
    second = jnp.where(bit == 0, other, own)
    return jnp.concatenate([first, second], axis=axis)


def dot(left, right, left_dim=1, right_dim=0):
    return lax.dot_general(
        left, right, (((left_dim,), (right_dim,)), ((), ())), preferred_element_type=full
    )


def gather_col(block, col):
    count = lax.axis_size("col")
    from_left, from_right = [block], [block]
    for step in range(1, count):
        from_left.append(
            lax.ppermute(from_left[-1], "col", [(i, i + 1) for i in range(step - 1, count - 1)])
        )
        from_right.append(
            lax.ppermute(from_right[-1], "col", [(i + 1, i) for i in range(count - step)])
        )
    slots = [block]
    for k in range(1, count):
        chosen = None
        for at in range(count):
            there = at ^ k
            value = from_right[there - at] if there > at else from_left[at - there]
            chosen = value if chosen is None else jnp.where(col == at, value, chosen)
        slots.append(chosen)
    return slots


def quarter_of(block, quarter):
    size = block.shape[0] // 4
    return lax.dynamic_slice_in_dim(block, quarter * size, size, 0)


def quarters_all(block, core, side):
    across = swap(block, "dp", 2)
    two = [jnp.where(side == 0, block, across), jnp.where(side == 0, across, block)]
    both = jnp.stack(two)
    near = swap(both, "dp", 1)
    result = []
    for at in range(2):
        result.append(jnp.where(core == 0, both[at], near[at]))
        result.append(jnp.where(core == 0, near[at], both[at]))
    return result


def attention_forward_kernel(
    pre_ref, cosine_ref, sine_ref, key_ref, value_ref, start_ref, out_ref, rot_ref, *, window, tile
):
    rows = pre_ref.shape[0]
    pre = pre_ref[...]
    rot = (pre * cosine_ref[...] + pltpu.roll(pre, head_dim // 2, 1) * sine_ref[...]).astype(low)
    rot_ref[...] = rot
    for at in range(rows // tile):
        first = at * tile
        keys = key_ref[first : first + window, :]
        values = value_ref[first : first + window, :]
        scores = dot(rot[first : first + tile], keys, 1, 1) * head_dim ** (-0.5)
        place = lax.broadcasted_iota(jnp.int32, scores.shape, 1) + first
        query = lax.broadcasted_iota(jnp.int32, scores.shape, 0) + (first + rows)
        allowed = (place <= query) & (place >= start_ref[first : first + tile, :])
        scores = jnp.where(allowed, scores, -1e30)
        exponent = jnp.exp(scores - jnp.max(scores, axis=1, keepdims=True))
        weights = exponent / jnp.sum(exponent, axis=1, keepdims=True)
        out_ref[first : first + tile, :] = dot(weights.astype(low), values).astype(low)


def attention_forward(pre, cosine, sine, keys, values, start, heads):
    rows, reach = pre.shape[0], keys.shape[0]
    whole = lambda shape: pl.BlockSpec(shape, lambda h: (0, 0))
    head = pl.BlockSpec((rows, head_dim), lambda h: (0, h))
    shape = jax.ShapeDtypeStruct((rows, heads * head_dim), low)
    per_half = heads // 2
    return pl.pallas_call(
        functools.partial(attention_forward_kernel, window=reach - rows // 2, tile=rows // 2),
        grid=(heads,),
        in_specs=[
            pl.BlockSpec((rows, head_dim), lambda h: (0, h + h // per_half)),
            whole((rows, head_dim)),
            whole((rows, head_dim)),
            whole((reach, head_dim)),
            whole((reach, head_dim)),
            whole((rows, 1)),
        ],
        out_specs=[head, head],
        out_shape=[shape, shape],
        compiler_params=pltpu.CompilerParams(vmem_limit_bytes=32 * 2**20),
        cost_estimate=pl.CostEstimate(
            flops=heads * rows * reach * 3 * head_dim,
            bytes_accessed=heads * rows * head_dim * 8,
            transcendentals=heads * rows * reach,
        ),
    )(pre, cosine, sine, keys, values, start)


def remote_copy(source, target, send_sem, recv_sem, **device):
    return pltpu.make_async_remote_copy(
        src_ref=source,
        dst_ref=target,
        send_sem=send_sem,
        recv_sem=recv_sem,
        device_id=device,
        device_id_type=pl.DeviceIdType.MESH,
    )


def add_low(left, right):
    return (left.astype(full) + right.astype(full)).astype(low)


class ColSum:
    def __init__(self, stack, arrived, send_sem, recv_sem, col):
        self.stack, self.arrived, self.send_sem, self.recv_sem, self.col = (
            stack,
            arrived,
            send_sem,
            recv_sem,
            col,
        )
        self.last = stack.shape[0] - 1

    def copy(self, block, at, right):
        neighbour = at + 1 if right else at - 1
        slot = block if right or block != neighbour else self.last + 1
        return remote_copy(
            self.stack.at[block],
            self.arrived.at[slot],
            self.send_sem.at[block],
            self.recv_sem.at[slot],
            col=neighbour,
        )

    def wait(self, slot, at):
        remote_copy(
            self.arrived.at[slot],
            self.arrived.at[slot],
            self.send_sem.at[0],
            self.recv_sem.at[slot],
            col=at + 1 if at == 0 else at - 1,
        ).wait_recv()

    def step(self, number):
        for at in range(self.last + 1):

            @pl.when(self.col == at)
            def _(at=at):
                for right in (True, False):
                    block = at + self.last + 1 - number if right else at - self.last - 1 + number
                    if not 0 <= block <= self.last:
                        continue
                    if 0 < at < self.last:
                        self.wait(block, at)
                        self.stack[block] = add_low(self.stack[block], self.arrived[block])
                    self.copy(block, at, right).start()

    def total(self, part):
        for at in range(self.last + 1):

            @pl.when(self.col == at)
            def _(at=at):
                if at > 0:
                    self.wait(at, at)
                if at < self.last:
                    self.wait(self.last + 1, at)
                value = self.stack[at].astype(full)
                if at > 0:
                    value += self.arrived[at].astype(full)
                if at < self.last:
                    value += self.arrived[self.last + 1].astype(full)
                part(value)

    def end(self):
        for at in range(self.last + 1):

            @pl.when(self.col == at)
            def _(at=at):
                for block in range(self.last + 1):
                    if block != at:
                        self.copy(block, at, block > at).wait_send()


def experts_kernel(
    own_ref,
    cot_ref,
    table_ref,
    gate_hbm,
    up_hbm,
    down_hbm,
    sum_ref,
    out_part_ref,
    gate_total_ref,
    up_own_ref,
    up_row_ref,
    up_other_ref,
    down_half_ref,
    weights,
    expert_in,
    gate_grad,
    up_grad,
    hidden,
    send_stage,
    arrived,
    parts,
    stage,
    weights_sem,
    ready,
    ag_recv,
    ag_right,
    ag_left,
    rs_recv,
    rs_send,
    core_send,
    core_recv,
    row_send,
    row_recv,
    side_send,
    side_recv,
    final_sem,
    local_sem,
):
    row, col, dp = lax.axis_index("row"), lax.axis_index("col"), lax.axis_index("dp")
    dps = lax.axis_size("dp")
    core, other = dp % 2, 1 - row
    core_partner = dp + 1 - 2 * core
    side_bits = list(range(1, dps.bit_length() - 1))
    sides = len(side_bits)
    last = cot_ref.shape[0] - 1
    rows, width = own_ref.shape
    half = width // 2
    size = half // 2
    inner = (col > 0) & (col < last)

    def across(bit):
        on = (dp // (1 << bit)) % 2
        return dp + (1 << bit) * (1 - 2 * on)

    gate_ref, up_ref, down_ref = weights.at[0], weights.at[1], weights.at[2]
    loads = [
        pltpu.make_async_copy(source, weights.at[i], weights_sem.at[i])
        for i, source in enumerate((gate_hbm, up_hbm, down_hbm))
    ]
    for copy in loads:
        copy.start()

    barrier = pltpu.get_barrier_semaphore()

    def greet(semaphore, **device):
        pl.semaphore_signal(
            semaphore, inc=1, device_id=device, device_id_type=pl.DeviceIdType.MESH
        )

    greet(barrier, dp=core_partner)
    greet(barrier, row=other)
    for bit in side_bits:
        greet(barrier, dp=across(bit))
    pl.when(col > 0)(lambda: greet(barrier, col=col - 1))
    pl.when(col < last)(lambda: greet(barrier, col=col + 1))
    expert_in[col] = own_ref[...]
    pl.when(inner)(lambda: pl.semaphore_wait(barrier, 4 + sides))
    pl.when(jnp.logical_not(inner))(lambda: pl.semaphore_wait(barrier, 3 + sides))

    def ag_copy(block, right):
        return remote_copy(
            expert_in.at[block],
            expert_in.at[block],
            (ag_right if right else ag_left).at[block],
            ag_recv.at[block],
            col=col + 1 if right else col - 1,
        )

    def rs_copy(block, part, right):
        neighbour = col + 1 if right else col - 1
        slot = block if right else jnp.where(block == neighbour, last + 1, block)
        return remote_copy(
            send_stage.at[block, part],
            arrived.at[slot, part],
            rs_send.at[block, part],
            rs_recv.at[slot, part],
            col=neighbour,
        )

    def rs_wait(slot, part):
        remote_copy(
            arrived.at[slot, part],
            arrived.at[slot, part],
            rs_send.at[0, part],
            rs_recv.at[slot, part],
            col=jnp.where(col > 0, col - 1, col + 1),
        ).wait_recv()

    pl.when(col < last)(lambda: ag_copy(col, True).start())
    pl.when(col > 0)(lambda: ag_copy(col, False).start())
    for copy in loads:
        copy.wait()

    def compute(block):
        tokens = expert_in[block]
        grads = cot_ref[block]
        table = table_ref[block]
        experts = table.shape[1]
        units = width // experts
        for g in range(2):
            cols = slice(g * half, (g + 1) * half)
            gate = dot(tokens, gate_ref[:, cols])
            up = dot(tokens, up_ref[:, cols])
            grad = dot(grads, down_ref[cols, :], 1, 1)
            lane = lax.broadcasted_iota(jnp.int32, gate.shape, 1)
            first = g * experts // 2
            chosen = jnp.broadcast_to(table[:, first : first + 1], gate.shape)
            for e in range(1, experts // 2):
                chosen = jnp.where(lane >= e * units, table[:, first + e : first + e + 1], chosen)
            sigmoid = 1.0 / (1.0 + jnp.exp(-gate))
            silu = gate * sigmoid
            grad = grad * chosen
            hidden[block, :, cols] = (silu * up * chosen).astype(low)
            gate_grad[block, :, cols] = (
                grad * up * (sigmoid * (1.0 + gate * (1.0 - sigmoid)))
            ).astype(low)
            up_grad[block, :, cols] = (grad * silu).astype(low)
        gates_now, ups_now = gate_grad[block], up_grad[block]
        for part in range(2):
            cols = slice(part * half, (part + 1) * half)
            total = dot(gates_now, gate_ref[cols, :], 1, 1) + dot(ups_now, up_ref[cols, :], 1, 1)
            send_stage[block, part] = total.astype(low)
            pl.when((col == 0) & (block != col))(lambda: rs_copy(block, part, True).start())
            pl.when((col == last) & (block != col))(lambda: rs_copy(block, part, False).start())
        out_part_ref[block] = dot(hidden[block], down_ref[...]).astype(low)

    def step(i, carry):
        apart = (i + 1) // 2
        from_left = i % 2 == 1

        @pl.when(from_left & (col - apart >= 0))
        def _():
            block = col - apart
            ag_copy(block, True).wait_recv()
            pl.when(col < last)(lambda: ag_copy(block, True).start())

        @pl.when(from_left & (col + apart <= last))
        def _():
            block = col + apart
            ag_copy(block, False).wait_recv()
            pl.when(col > 0)(lambda: ag_copy(block, False).start())

        block = jnp.where(from_left, col - apart, col + apart)
        pl.when((block >= 0) & (block <= last))(lambda: compute(block))
        return carry

    lax.fori_loop(0, 2 * last + 1, step, 0)

    greet(ready.at[0], dp=core_partner)
    greet(ready.at[1], row=other)
    for number, bit in enumerate(side_bits):
        greet(ready.at[2 + number], dp=across(bit))

    def room(which, down, right):
        return weights.at[
            which, pl.ds(down * half, half), pl.ds(right * half, half)
        ]

    def forward(block, right):
        for part in range(2):
            rs_wait(block, part)
            send_stage[block, part] = add_low(send_stage[block, part], arrived[block, part])
            rs_copy(block, part, right).start()

    def event(number):
        blocks = ((2, 1), (3, 0), (0, 3))[number]
        pl.when(col == 1)(lambda: forward(blocks[0], number < 2))
        pl.when(col == 2)(lambda: forward(blocks[1], number == 2))

    def core_copy(at):
        if at < 4:
            target = room(at // 2, 0, at % 2)
        else:
            target = room(2, 0, at - 4)
        return remote_copy(
            stage.at[at % 2], target, core_send.at[at], core_recv.at[at], dp=core_partner
        )

    def stage_free(at):
        if at >= 2:
            core_copy(at - 2).wait_send()

    def half_lanes(which):
        return pl.ds(pl.multiple_of(which * half, half), half)

    def core_dot(at):
        right = (gate_grad, up_grad)[at // 2]
        left = expert_in[:, :, half_lanes(row if at % 2 else other)].reshape(-1, half)
        stage_free(at)
        stage[at % 2] = dot(
            left, right[:, :, half_lanes(1 - core)].reshape(-1, half), 0, 0
        ).astype(low)
        core_copy(at).start()
        parts[at] = dot(left, right[:, :, half_lanes(core)].reshape(-1, half), 0, 0).astype(low)

    def core_sum(at):
        core_copy(at).wait_recv()
        parts[at] = add_low(parts[at], room(at // 2, 0, at % 2)[...])

    def down_dot():
        left = hidden[:, :, half_lanes(1 - core)].reshape(-1, half)
        for part in range(2):
            lanes = slice(part * half, (part + 1) * half)
            right = cot_ref[:, :, lanes].reshape(-1, half)
            stage_free(4 + part)
            stage[part] = dot(left, right, 0, 0).astype(low)
            core_copy(4 + part).start()
        left = hidden[:, :, half_lanes(core)].reshape(-1, half)
        for part in range(2):
            lanes = slice(part * half, (part + 1) * half)
            right = cot_ref[:, :, lanes].reshape(-1, half)
            room(2, 1, part)[...] = dot(left, right, 0, 0).astype(low)

    def down_sum():
        for part in range(2):
            core_copy(4 + part).wait_recv()
            room(2, 1, part)[...] = add_low(room(2, 1, part)[...], room(2, 0, part)[...])

    down_out = pltpu.make_async_copy(
        weights.at[2, pl.ds(half, half)], down_half_ref, local_sem.at[0]
    )
    up_out = pltpu.make_async_copy(parts.at[3], up_own_ref, local_sem.at[1])
    up_rest = pltpu.make_async_copy(
        parts.at[2, pl.ds(size, size)], up_other_ref, local_sem.at[2]
    )

    def chunk_rows(chunk):
        return pl.ds(chunk * size, size)

    def row_copy(chunk):
        if chunk < 2:
            source = parts.at[0, chunk_rows(chunk)]
            target = weights.at[0, pl.ds(half + chunk * size, size), pl.ds(0, half)]
        else:
            source, target = parts.at[2, chunk_rows(0)], up_row_ref
        return remote_copy(source, target, row_send.at[chunk], row_recv.at[chunk], row=other)

    def side_room(number, chunk):
        which, right = ((0, 1), (1, 0), (1, 1))[number]
        return weights.at[
            which, pl.ds(half + chunk * size, size), pl.ds(right * half, half)
        ]

    def side_copy(chunk, number):
        return remote_copy(
            parts.at[1 - number % 2, chunk_rows(chunk)],
            side_room(number, chunk),
            side_send.at[chunk, number],
            side_recv.at[chunk, number],
            dp=across(side_bits[number]),
        )

    def after_row(chunk):
        copy = row_copy(chunk)
        copy.wait_recv()
        copy.wait_send()
        here = chunk_rows(chunk)
        landed = weights.at[0, pl.ds(half + chunk * size, size), pl.ds(0, half)]
        parts[1, here] = add_low(parts[1, here], landed[...])
        if sides:
            if chunk == 0:
                for number in range(sides):
                    pl.semaphore_wait(ready.at[2 + number], 1)
            side_copy(chunk, 0).start()

    def final_copies(chunk):
        source = parts.at[1 - sides % 2, chunk_rows(chunk)]
        target = gate_total_ref.at[chunk_rows(chunk), half_lanes(core)]
        return (
            remote_copy(
                source, target, final_sem.at[chunk, 0], final_sem.at[chunk, 1], dp=core_partner
            ),
            pltpu.make_async_copy(source, target, final_sem.at[chunk, 2]),
        )

    def after_side(chunk):
        here = chunk_rows(chunk)
        for number in range(sides):
            copy = side_copy(chunk, number)
            copy.wait_recv()
            copy.wait_send()
            parts[number % 2, here] = add_low(
                parts[1 - number % 2, here], side_room(number, chunk)[...]
            )
            if number + 1 < sides:
                side_copy(chunk, number + 1).start()
        for copy in final_copies(chunk):
            copy.start()

    pl.semaphore_wait(ready.at[0], 1)
    core_dot(0)
    core_dot(1)
    core_sum(0)
    pl.semaphore_wait(ready.at[1], 1)
    row_copy(0).start()
    row_copy(1).start()
    event(0)
    core_dot(2)
    core_sum(1)
    core_sum(2)
    row_copy(2).start()
    up_rest.start()
    core_dot(3)
    down_dot()
    core_sum(3)
    up_out.start()
    event(1)
    after_row(0)
    down_sum()
    down_out.start()
    event(2)
    after_row(1)

    for part in range(2):
        cols = slice(part * half, (part + 1) * half)
        sum_ref[:, cols] = send_stage[col, part].astype(full)

        @pl.when(col > 0)
        def _():
            rs_wait(col, part)
            sum_ref[:, cols] += arrived[col, part].astype(full)

        @pl.when(col < last)
        def _():
            rs_wait(last + 1, part)
            sum_ref[:, cols] += arrived[last + 1, part].astype(full)

    after_side(0)
    after_side(1)

    for block in range(last + 1):
        pl.when((block <= col) & (col < last))(lambda: ag_copy(block, True).wait_send())
        pl.when((block >= col) & (col > 0))(lambda: ag_copy(block, False).wait_send())
        for part in range(2):
            pl.when(block > col)(lambda: rs_copy(block, part, True).wait_send())
            pl.when(block < col)(lambda: rs_copy(block, part, False).wait_send())
    for at in range(4, 6):
        core_copy(at).wait_send()
    row_copy(2).wait()
    for copy in (down_out, up_out, up_rest):
        copy.wait()
    for chunk in range(2):
        remote, local = final_copies(chunk)
        remote.wait()
        local.wait()


def experts_call(own, cot, table, gate_all, up_all, down_all):
    rows, width = own.shape
    blocks, half = cot.shape[0], width // 2
    sides = lax.axis_size("dp").bit_length() - 2
    vmem = pl.BlockSpec(memory_space=pltpu.VMEM)
    anywhere = pl.BlockSpec(memory_space=pl.ANY)
    dma = pltpu.SemaphoreType.DMA
    shape = jax.ShapeDtypeStruct
    return pl.pallas_call(
        experts_kernel,
        in_specs=[vmem] * 3 + [anywhere] * 3,
        out_specs=[vmem, vmem] + [anywhere] * 5,
        out_shape=[
            shape((rows, width), full),
            shape((blocks, rows, width), low),
            shape((half, width), low),
            shape((half, half), low),
            shape((half // 2, half), low),
            shape((half // 2, half), low),
            shape((half, width), low),
        ],
        scratch_shapes=[pltpu.VMEM((3, width, width), low)]
        + [pltpu.VMEM((blocks, rows, width), low)] * 4
        + [
            pltpu.VMEM((blocks, 2, rows, half), low),
            pltpu.VMEM((blocks + 1, 2, rows, half), low),
            pltpu.VMEM((4, half, half), low),
            pltpu.VMEM((2, half, half), low),
            dma((3,)),
            pltpu.SemaphoreType.REGULAR((2 + max(sides, 1),)),
            dma((blocks,)),
            dma((blocks,)),
            dma((blocks,)),
            dma((blocks + 1, 2)),
            dma((blocks, 2)),
            dma((6,)),
            dma((6,)),
            dma((3,)),
            dma((3,)),
            dma((2, max(sides, 1))),
            dma((2, max(sides, 1))),
            dma((2, 3)),
            dma((3,)),
        ],
        compiler_params=pltpu.CompilerParams(
            collective_id=1, has_side_effects=True, vmem_limit_bytes=60 * 2**20
        ),
        cost_estimate=pl.CostEstimate(
            flops=9 * 2 * blocks * rows * width * width,
            bytes_accessed=12 * width * width,
            transcendentals=blocks * rows * width,
        ),
    )(own, cot, table, gate_all, up_all, down_all)


def finish_kernel(
    sum_ref,
    middle_ref,
    cot_ref,
    mixer_ref,
    gain_ref,
    scale_ref,
    inputs_ref,
    attended_ref,
    rot_ref,
    key_ref,
    value_ref,
    cosine_ref,
    sine_ref,
    start_ref,
    head_output_ref,
    joint_ref,
    normed_ref,
    out_part_ref,
    up_own_ref,
    up_row_ref,
    up_other_ref,
    down_half_ref,
    outputs_ref,
    input_grad_ref,
    gains_ref,
    output_total_ref,
    joint_total_ref,
    up_total_ref,
    down_total_ref,
    item_side,
    branch,
    branch_sem,
    out_stack,
    out_arrived,
    out_load,
    out_send,
    out_recv,
    own_out_sem,
    grad_heads,
    joint_grad,
    key_grad,
    value_grad,
    pair_stage,
    pair_arrived,
    pair_sem,
    normed_arrived,
    normed_own,
    normed_sem,
    inner_stage,
    inner_arrived,
    inner_sem,
    sums,
    sums_arrived,
    sums_sem,
    item_mine,
    item_other,
    item_row,
    item_sem,
    item_load_sem,
    wo_parts,
    wo_core,
    wo_row,
    wo_stack,
    wo_arrived,
    wo_side,
    wo_sem,
    wo_send,
    wo_recv,
    wa_parts,
    wa_core,
    wa_row,
    wa_stack,
    wa_arrived,
    wa_side,
    wa_sem,
    wa_send,
    wa_recv,
):
    row, col, dp = lax.axis_index("row"), lax.axis_index("col"), lax.axis_index("dp")
    cols, dps = lax.axis_size("col"), lax.axis_size("dp")
    core, other = dp % 2, 1 - row
    core_partner = dp + 1 - 2 * core
    side_bits = [bit for bit in range(1, dps.bit_length() - 1)]

    def across(bit):
        on = (dp // (1 << bit)) % 2
        return dp + (1 << bit) * (1 - 2 * on)

    rows, width = middle_ref.shape
    tokens, part_width = inputs_ref.shape
    heads = attended_ref.shape[1] // head_dim
    per_block = heads // 2

    barrier = pltpu.get_barrier_semaphore()

    def greet(**device):
        pl.semaphore_signal(
            barrier, inc=1, device_id=device, device_id_type=pl.DeviceIdType.MESH
        )

    greet(row=other)
    for apart in range(1, cols):
        greet(col=(col + apart) % cols)
    greet(dp=core_partner)
    for bit in side_bits:
        greet(dp=across(bit))

    out_copy = pltpu.make_async_copy(out_part_ref, out_stack, out_load)
    out_copy.start()
    size = item_mine.shape[1]
    items = item_mine.shape[0]

    def item_loads(at):
        chunk = at % 2
        place = pl.ds(chunk * size, size)
        if at < 2:
            sources = (up_own_ref.at[place], (up_row_ref, up_other_ref)[chunk])
        else:
            sources = [
                down_half_ref.at[place, pl.ds(pl.multiple_of(which * part_width, 128), part_width)]
                for which in (row, other)
            ]
        targets = (item_mine.at[at], item_row.at[at] if at == 0 else item_other.at[at])
        return [
            pltpu.make_async_copy(source, target, item_load_sem.at[at, number])
            for number, (source, target) in enumerate(zip(sources, targets))
        ]

    for at in range(items):
        for copy in item_loads(at):
            copy.start()

    pl.semaphore_wait(barrier, cols + 1 + len(side_bits))

    sums[0] = jnp.zeros_like(sums[0])
    piece = 64

    def norm_piece(at, mixer_sum):
        place = pl.ds(pl.multiple_of(at * piece, piece), piece)
        middle = middle_ref[place, :]
        second = sum_ref[place, :]
        scale = lax.rsqrt(jnp.mean(middle * middle, axis=1, keepdims=True) + epsilon)
        weighted = mixer_ref[...] * second
        inner = jnp.sum(weighted * middle, axis=1, keepdims=True)
        grad = (
            cot_ref[place, :].astype(full)
            + scale * weighted
            - middle * (scale * scale * scale) * (inner / width)
        )
        branch[row, place, :] = grad.astype(low)
        return mixer_sum + jnp.sum(second * middle * scale, axis=0, keepdims=True)

    mixer_sum = lax.fori_loop(0, rows // piece, norm_piece, jnp.zeros((1, width), full))
    sums[0, 1:2, :] = mixer_sum
    branch_copy = remote_copy(
        branch.at[row], branch.at[row], branch_sem.at[0], branch_sem.at[1], row=other
    )
    branch_copy.start()

    outs = ColSum(out_stack, out_arrived, out_send, out_recv, col)
    out_copy.wait()
    outs.step(1)
    for at in range(items):
        for copy in item_loads(at):
            copy.wait()

    def item_row_copy(at):
        return remote_copy(
            item_other.at[at], item_row.at[at], item_sem.at[at, 0], item_sem.at[at, 1], row=other
        )

    def item_side_copy(at, number):
        source = item_mine if number % 2 == 0 else item_other
        return remote_copy(
            source.at[at],
            item_side.at[at, number],
            item_sem.at[at, 2 + 2 * number],
            item_sem.at[at, 3 + 2 * number],
            dp=across(side_bits[number]),
        )

    last_side = len(side_bits)

    def item_value(at):
        return item_mine if last_side % 2 == 0 else item_other

    def item_places(at):
        which, chunk = at // 2, at % 2
        total = (up_total_ref, down_total_ref)[which]
        if which < 1:
            lanes = pl.ds(pl.multiple_of(core * part_width, 128), part_width)
            return total.at[pl.ds(chunk * size, size), lanes]
        return total.at[pl.ds(pl.multiple_of(core * part_width + chunk * size, 128), size), :]

    def item_core_copies(at):
        source, target = item_value(at).at[at], item_places(at)
        base = 2 + 2 * last_side
        return (
            remote_copy(
                source, target, item_sem.at[at, base], item_sem.at[at, base + 1], dp=core_partner
            ),
            pltpu.make_async_copy(source, target, item_sem.at[at, base + 2]),
        )

    def item_after_row(at):
        if at > 0:
            copy = item_row_copy(at)
            copy.wait_recv()
            copy.wait_send()
        item_mine[at] = add_low(item_mine[at], item_row[at])
        if last_side:
            item_side_copy(at, 0).start()

    def item_after_side(at):
        for number in range(last_side):
            copy = item_side_copy(at, number)
            copy.wait_recv()
            landed = pltpu.make_async_copy(
                item_side.at[at, number], item_row.at[at], item_load_sem.at[at, 0]
            )
            landed.start()
            copy.wait_send()
            landed.wait()
            source = item_mine if number % 2 == 0 else item_other
            target = item_other if number % 2 == 0 else item_mine
            target[at] = add_low(source[at], item_row[at])
            if number + 1 < last_side:
                item_side_copy(at, number + 1).start()
        for copy in item_core_copies(at):
            copy.start()

    def item_end(at):
        remote, local = item_core_copies(at)
        remote.wait_recv()
        remote.wait_send()
        local.wait()

    item_after_row(0)

    branch_copy.wait_recv()
    branch_all = branch[...].reshape(tokens, width)
    half_lanes = heads * head_dim // 2
    for part in range(2):
        lanes = slice(part * half_lanes, (part + 1) * half_lanes)
        grad_heads[:, lanes] = dot(branch_all, head_output_ref[lanes, :], 1, 1).astype(low)
    item_row_copy(1).start()

    wo_size = wo_parts.shape[2]
    for b in range(2):
        lanes = slice(b * half_lanes, (b + 1) * half_lanes)
        value = dot(attended_ref[:, lanes], branch_all, 0, 0).astype(low)
        for part in range(2):
            wo_parts[b, part] = value[part * wo_size : (part + 1) * wo_size, :]

    def wo_core_copy(b):
        return remote_copy(
            wo_parts.at[b, 1 - core], wo_core.at[b], wo_sem.at[0, b], wo_sem.at[1, b], dp=core_partner
        )

    for b in range(2):
        wo_core_copy(b).start()
    outs.step(2)

    key_grad[...] = jnp.zeros_like(key_grad)
    value_grad[...] = jnp.zeros_like(value_grad)
    tile = tokens // 2
    window = key_ref.shape[0] - tile

    def head_step(head, carry):
        here = pl.ds(pl.multiple_of(head * head_dim, head_dim), head_dim)
        there = pl.ds(
            pl.multiple_of((head + head // per_block) * head_dim, head_dim), head_dim
        )
        for at in range(tokens // tile):
            first = at * tile
            rot = rot_ref[first : first + tile, here]
            grad = grad_heads[first : first + tile, here]
            keys = key_ref[first : first + window, :]
            values = value_ref[first : first + window, :]
            scores = dot(rot, keys, 1, 1) * head_dim ** (-0.5)
            place = lax.broadcasted_iota(jnp.int32, scores.shape, 1) + first
            query = lax.broadcasted_iota(jnp.int32, scores.shape, 0) + (first + tokens)
            allowed = (place <= query) & (place >= start_ref[first : first + tile, :])
            scores = jnp.where(allowed, scores, -1e30)
            exponent = jnp.exp(scores - jnp.max(scores, axis=1, keepdims=True))
            probs = exponent / jnp.sum(exponent, axis=1, keepdims=True)
            prob_grad = dot(grad, values, 1, 1)
            inner = jnp.sum(probs * prob_grad, axis=1, keepdims=True)
            score_grad = (probs * (prob_grad - inner) * head_dim ** (-0.5)).astype(low)
            rot_grad = dot(score_grad, keys)
            joint_grad[first : first + tile, there] = (
                rot_grad * cosine_ref[first : first + tile, :]
                - pltpu.roll(rot_grad, head_dim // 2, 1) * sine_ref[first : first + tile, :]
            ).astype(low)
            key_grad[first : first + window, :] += dot(score_grad, rot, 0, 0)
            value_grad[first : first + window, :] += dot(probs.astype(low), grad, 0, 0)
        return carry

    lax.fori_loop(0, heads, head_step, 0)

    pair_stage[:, :head_dim] = key_grad[:tokens, :].astype(low)
    pair_stage[:, head_dim:] = value_grad[:tokens, :].astype(low)
    odd = col % 2 == 1

    def pair_copy():
        return remote_copy(
            pair_stage, pair_arrived, pair_sem.at[0], pair_sem.at[1], col=col + 1 - 2 * (col % 2)
        )

    pl.when(odd)(lambda: pair_copy().start())

    def wo_row_copy(b):
        lanes = pl.ds(pl.multiple_of(other * part_width, 128), part_width)
        return remote_copy(
            wo_parts.at[b, core, :, lanes],
            wo_row.at[b],
            wo_sem.at[2, b],
            wo_sem.at[3, b],
            row=other,
        )

    for b in range(2):
        wo_core_copy(b).wait_recv()
        wo_parts[b, core] = add_low(wo_parts[b, core], wo_core[b])
        wo_row_copy(b).start()
    item_after_row(1)

    @pl.when(jnp.logical_not(odd))
    def _():
        pair_copy().wait_recv()
        key_grad[tokens:, :] += pair_arrived[:, :head_dim].astype(full)
        value_grad[tokens:, :] += pair_arrived[:, head_dim:].astype(full)

    key_total = key_grad[tokens:, :]
    key_lanes = slice(per_block * head_dim, (per_block + 1) * head_dim)
    value_lanes = slice((2 * per_block + 1) * head_dim, (2 * per_block + 2) * head_dim)
    joint_grad[:, key_lanes] = (
        key_total * cosine_ref[...] - pltpu.roll(key_total, head_dim // 2, 1) * sine_ref[...]
    ).astype(low)
    joint_grad[:, value_lanes] = value_grad[tokens:, :].astype(low)

    wa_size = wa_core.shape[1]

    def wa_core_copy(r0):
        return remote_copy(
            wa_parts.at[r0, 1 - core], wa_core.at[r0], wa_sem.at[0, r0], wa_sem.at[1, r0], dp=core_partner
        )

    def wa_dot(r0, which):
        first = pl.multiple_of(r0 * part_width + which * wa_size, 128)
        wa_parts[r0, which] = dot(
            normed_ref[:, pl.ds(first, wa_size)], joint_grad[...], 0, 0
        ).astype(low)

    wa_dot(other, 1 - core)
    wa_core_copy(other).start()
    wa_dot(row, 1 - core)
    wa_core_copy(row).start()
    wa_dot(other, core)
    wa_dot(row, core)
    chunk_rows = wa_size // 2

    def wa_row_copy(chunk):
        return remote_copy(
            wa_parts.at[other, core, pl.ds(chunk * chunk_rows, chunk_rows)],
            wa_row.at[chunk],
            wa_sem.at[2, chunk],
            wa_sem.at[3, chunk],
            row=other,
        )

    wa_core_copy(other).wait_recv()
    wa_parts[other, core] = add_low(wa_parts[other, core], wa_core[other])
    for chunk in range(2):
        wa_row_copy(chunk).start()

    def normed_dot(which):
        place = pl.ds(pl.multiple_of(which * part_width, 128), part_width)
        return dot(joint_grad[...], joint_ref[place, :], 1, 1)

    normed_stage = grad_heads
    normed_stage[...] = normed_dot(other).astype(low)
    normed_copy = remote_copy(
        normed_stage, normed_arrived, normed_sem.at[0], normed_sem.at[1], row=other
    )
    normed_copy.start()
    normed_own[...] = normed_dot(row)
    wa_core_copy(row).wait_recv()
    wa_parts[row, core] = add_low(wa_parts[row, core], wa_core[row])

    wo_total = ColSum(wo_stack, wo_arrived, wo_send, wo_recv, col)
    for b in range(2):
        wo_row_copy(b).wait_recv()
        lanes = pl.ds(pl.multiple_of(row * part_width, 128), part_width)
        wo_stack[2 * row + b] = wo_parts[b, core, :, lanes]
        wo_stack[2 * other + b] = wo_row[b]
    wo_total.step(1)
    item_after_side(0)
    item_row_copy(2).start()
    outs.step(3)
    wo_total.step(2)

    wa_total = [
        ColSum(wa_stack.at[c], wa_arrived.at[c], wa_send.at[c], wa_recv.at[c], col)
        for c in range(2)
    ]
    block_lanes = wa_stack.shape[3]
    for chunk in range(2):
        wa_row_copy(chunk).wait_recv()
        place = pl.ds(chunk * chunk_rows, chunk_rows)
        for b in range(2):
            lanes = slice(b * block_lanes, (b + 1) * block_lanes)
            wa_stack[chunk, 2 * row + b] = wa_parts[row, core, place, lanes]
            wa_stack[chunk, 2 * other + b] = wa_row[chunk, :, lanes]
        wa_total[chunk].step(1)
    wo_total.step(3)
    for chunk in range(2):
        wa_total[chunk].step(2)

    normed_copy.wait_recv()
    scale = scale_ref[...]
    normed_own[...] += normed_arrived[...].astype(full)
    inner = jnp.sum(
        gain_ref[...] * normed_own[...] * inputs_ref[...].astype(full), axis=1, keepdims=True
    )
    inner_stage[...] = jnp.transpose(jnp.broadcast_to(inner, (tokens, head_dim)))[:8, :]
    inner_copy = remote_copy(
        inner_stage, inner_arrived, inner_sem.at[0], inner_sem.at[1], row=other
    )
    inner_copy.start()
    for chunk in range(2):
        wa_total[chunk].step(3)
    sums[0, 0:1, pl.ds(pl.multiple_of(row * part_width, 128), part_width)] = jnp.sum(
        normed_own[...] * inputs_ref[...].astype(full) * scale, axis=0, keepdims=True
    )
    inner_copy.wait_recv()
    both = inner_stage[...] + inner_arrived[...]
    inner = jnp.transpose(jnp.concatenate([both] * (head_dim // 8), axis=0))[:, 0:1]
    lanes = pl.ds(pl.multiple_of(row * part_width, 128), part_width)
    input_grad_ref[...] = (
        branch[:, :, lanes].reshape(tokens, part_width).astype(full)
        + scale * (gain_ref[...] * normed_own[...])
        - inputs_ref[...].astype(full) * (scale * scale * scale) * (inner / width)
    ).astype(low)

    partners = [dict(row=other), dict(col=col + 1 - 2 * (col % 2))]
    partners.append(dict(col=col + 2 - 4 * ((col // 2) % 2)))
    partners.append(dict(dp=core_partner))
    partners += [dict(dp=across(bit)) for bit in side_bits]

    def sums_copy(number):
        return remote_copy(
            sums.at[number],
            sums_arrived.at[number],
            sums_sem.at[number, 0],
            sums_sem.at[number, 1],
            **partners[number],
        )

    def sums_step(number):
        sums_copy(number).wait_recv()
        sums[number + 1] = sums[number] + sums_arrived[number]
        if number + 1 < len(partners):
            sums_copy(number + 1).start()

    sums_copy(0).start()

    def own_tokens(value):
        total = (middle_ref[...] + value).astype(low)
        out_stack[col] = total

    outs.total(own_tokens)

    def outputs_copy():
        place = pl.ds(pl.multiple_of(row * rows, rows), rows)
        lanes = pl.ds(pl.multiple_of(other * part_width, 128), part_width)
        return remote_copy(
            out_stack.at[col, :, lanes],
            outputs_ref.at[place],
            own_out_sem.at[0],
            own_out_sem.at[1],
            row=other,
        )

    outputs_copy().start()
    outputs_ref[pl.ds(pl.multiple_of(row * rows, rows), rows), :] = out_stack[
        col, :, pl.ds(pl.multiple_of(row * part_width, 128), part_width)
    ]
    sums_step(0)
    for at in range(3, items):
        item_row_copy(at).start()

    def over_dp(side, sems):
        def copy(number):
            return remote_copy(
                side.at[number % 2],
                side.at[2 + number],
                sems.at[2 * number],
                sems.at[2 * number + 1],
                dp=across(side_bits[number]),
            )

        def start(number):
            copy(number).start()

        def finish(number):
            copy(number).wait()
            side[1 - number % 2] = add_low(side[number % 2], side[2 + number])
            if number + 1 < last_side:
                start(number + 1)

        return copy, start, finish

    def set_side(side):
        def part(value):
            side[0] = value.astype(low)

        return part

    chains = [(wo_total, wo_side, wo_sem.at[4])] + [
        (wa_total[c], wa_side.at[c], wa_sem.at[4 + c]) for c in range(2)
    ]
    steps = []
    for total, side, sems in chains:
        total.total(set_side(side))
        steps.append(over_dp(side, sems))
        if last_side:
            steps[-1][1](0)
    sums_step(1)
    item_after_side(1)
    item_after_row(2)
    for _, _, finish in steps:
        for number in range(last_side):
            finish(number)
    sums_step(2)

    def block_copies(number):
        _, side, sems = chains[number]
        base, value = 2 * last_side, side.at[last_side % 2]
        if number == 0:
            target = output_total_ref.at[pl.ds(pl.multiple_of(core * wo_size, 16), wo_size)]
        else:
            first = pl.multiple_of(core * wa_size + (number - 1) * chunk_rows, 16)
            target = joint_total_ref.at[pl.ds(first, chunk_rows)]
        return (
            remote_copy(
                value, target, sems.at[base], sems.at[base + 1], dp=core_partner
            ),
            pltpu.make_async_copy(value, target, sems.at[base + 2]),
        )

    for number in range(3):
        for copy in block_copies(number):
            copy.start()
    for number in range(3, len(partners)):
        sums_step(number)
    gains_ref[...] = sums[len(partners)]

    item_after_side(2)
    item_after_row(3)
    item_after_side(3)

    branch_copy.wait_send()
    pl.when(odd)(lambda: pair_copy().wait_send())
    for b in range(2):
        wo_core_copy(b).wait_send()
        wo_row_copy(b).wait_send()
        wa_core_copy(b).wait_send()
        wa_row_copy(b).wait_send()
    normed_copy.wait_send()
    inner_copy.wait_send()
    outputs_copy().wait()
    for number in range(len(partners)):
        sums_copy(number).wait_send()
    for total in [outs, wo_total] + wa_total:
        total.end()
    for number in range(3):
        remote, local = block_copies(number)
        remote.wait()
        local.wait()
    for at in range(items):
        item_end(at)


def finish_call(
    sums, middle, cot, mixer, gain, scale, inputs, attended, rot, keys, values, cosine, sine,
    start, head_output, joint_weight, normed, out_part, up_own, up_row, up_other, down_half,
    query_block, both_block,
):
    rows, width = middle.shape
    tokens, part_width = inputs.shape
    cols, dps = lax.axis_size("col"), lax.axis_size("dp")
    sides = dps.bit_length() - 2
    heads_width = attended.shape[1]
    reach = keys.shape[0]
    vmem = pl.BlockSpec(memory_space=pltpu.VMEM)
    anywhere = pl.BlockSpec(memory_space=pl.ANY)
    dma = pltpu.SemaphoreType.DMA
    hidden = 2 * up_own.shape[1]
    size = part_width // 2
    items = 4
    wo_size, wa_size = query_block // 2, part_width // 2
    shape = jax.ShapeDtypeStruct
    sums_count = 4 + sides
    return pl.pallas_call(
        finish_kernel,
        in_specs=[vmem] * 17 + [anywhere] * 5,
        out_specs=[vmem] * 5 + [anywhere] * 3,
        out_shape=[
            shape((tokens, part_width), low),
            shape((tokens, part_width), low),
            shape((8, width), full),
            shape((query_block, part_width), low),
            shape((part_width, both_block), low),
            shape((part_width, hidden), low),
            shape((hidden, part_width), low),
            shape((items, max(sides, 1), size, part_width), low),
        ],
        scratch_shapes=[
            pltpu.VMEM((2, rows, width), low),
            dma((2,)),
            pltpu.VMEM((cols, rows, width), low),
            pltpu.VMEM((cols + 1, rows, width), low),
            dma,
            dma((cols,)),
            dma((cols + 1,)),
            dma((2,)),
            pltpu.VMEM((tokens, heads_width), low),
            pltpu.VMEM((tokens, 2 * both_block), low),
            pltpu.VMEM((reach, head_dim), full),
            pltpu.VMEM((reach, head_dim), full),
            pltpu.VMEM((tokens, 2 * head_dim), low),
            pltpu.VMEM((tokens, 2 * head_dim), low),
            dma((2,)),
            pltpu.VMEM((tokens, part_width), low),
            pltpu.VMEM((tokens, part_width), full),
            dma((2,)),
            pltpu.VMEM((8, tokens), full),
            pltpu.VMEM((8, tokens), full),
            dma((2,)),
            pltpu.VMEM((sums_count + 1, 8, width), full),
            pltpu.VMEM((sums_count, 8, width), full),
            dma((sums_count, 2)),
            pltpu.VMEM((items, size, part_width), low),
            pltpu.VMEM((items, size, part_width), low),
            pltpu.VMEM((items, size, part_width), low),
            dma((items, 5 + 2 * sides)),
            dma((items, 2)),
            pltpu.VMEM((2, 2, wo_size, width), low),
            pltpu.VMEM((2, wo_size, width), low),
            pltpu.VMEM((2, wo_size, part_width), low),
            pltpu.VMEM((cols, wo_size, part_width), low),
            pltpu.VMEM((cols + 1, wo_size, part_width), low),
            pltpu.VMEM((2 + sides, wo_size, part_width), low),
            dma((5, 3 + 2 * sides)),
            dma((cols,)),
            dma((cols + 1,)),
            pltpu.VMEM((2, 2, wa_size, 2 * both_block), low),
            pltpu.VMEM((2, wa_size, 2 * both_block), low),
            pltpu.VMEM((2, wa_size // 2, 2 * both_block), low),
            pltpu.VMEM((2, cols, wa_size // 2, both_block), low),
            pltpu.VMEM((2, cols + 1, wa_size // 2, both_block), low),
            pltpu.VMEM((2, 2 + sides, wa_size // 2, both_block), low),
            dma((6, 3 + 2 * sides)),
            dma((2, cols)),
            dma((2, cols + 1)),
        ],
        compiler_params=pltpu.CompilerParams(
            collective_id=2, has_side_effects=True, vmem_limit_bytes=63 * 2**20
        ),
        cost_estimate=pl.CostEstimate(
            flops=10 * 10**9, bytes_accessed=40 * 10**6, transcendentals=4 * 10**6
        ),
    )(
        sums, middle, cot, mixer, gain, scale, inputs, attended, rot, keys, values, cosine, sine,
        start, head_output, joint_weight, normed, out_part, up_own, up_row, up_other, down_half,
    )


def rotate(matrix, cosine, sine):
    return matrix * cosine + jnp.roll(matrix, head_dim // 2, axis=1) * sine


def shards(
    inputs,
    norm_gain,
    query_weight,
    key_value_matrix,
    output_weight,
    mixer_gain,
    gate_weight,
    up_weight,
    down_weight,
    lengths,
    routes,
    route_gates,
    cotangent,
):
    row, col, dp = lax.axis_index("row"), lax.axis_index("col"), lax.axis_index("dp")
    core, side, quarter = dp % 2, (dp // 2) % 2, dp % 4
    cols = lax.axis_size("col")
    tokens, part_width = inputs.shape
    width = 2 * part_width
    own_tokens = tokens // 2
    experts, _, units = gate_weight.shape
    hidden_width = experts * units
    query_block, keyval_block = query_weight.shape[1], key_value_matrix.shape[1]
    heads = 2 * query_block // head_dim

    inputs_all = pair(row, inputs, swap(inputs, "row", 1), 1)
    gains = jnp.stack([norm_gain, mixer_gain])
    gains = pair(row, gains, swap(gains, "row", 1), 1)
    norm_all, mixer_all = gains[0], gains[1]
    lengths_all = pair(row, lengths, swap(lengths, "row", 1), 0)
    lengths_row = jnp.where(col < cols // 2, lengths_all[0], lengths_all[1])

    blocks = 2 * cols
    joint = jnp.concatenate([query_weight, key_value_matrix], axis=1)
    joint_part = quarter_of(joint, quarter)
    output_part = quarter_of(output_weight, quarter)

    def spread(part):
        arrived = []
        for k in range(cols):
            route = []
            for index in range(blocks):
                from_row, from_col = index // cols, index % cols
                to_row, to_col = from_col // 2, (2 * from_row + from_col % 2) ^ k
                route.append((index, to_row * cols + to_col))
            arrived.append(lax.ppermute(part, ("row", "col"), route))
        for bit in (1, 2):
            arrived = [
                jnp.where(col & bit == 0, arrived[k], arrived[k ^ bit]) for k in range(cols)
            ]
        return jnp.stack(arrived)

    joint_quarters = quarters_all(spread(joint_part), core, side)
    output_quarters = quarters_all(spread(output_part), core, side)
    joint_weight = jnp.concatenate(
        [
            jnp.concatenate(
                [piece[2 * r + b] for r in range(2) for piece in joint_quarters], axis=0
            )
            for b in range(2)
        ],
        axis=1,
    )
    head_output = jnp.concatenate(
        [
            jnp.concatenate(
                [piece[2 * r + b] for b in range(2) for piece in output_quarters], axis=0
            )
            for r in range(2)
        ],
        axis=1,
    )

    def flat_units(weight):
        return weight.transpose(1, 0, 2).reshape(part_width, hidden_width)

    gate_flat, up_flat = flat_units(gate_weight), flat_units(up_weight)
    down_flat = down_weight.reshape(hidden_width, part_width)

    def partner_of(flat):
        part = swap(quarter_of(flat, quarter), "row", 1)
        return jnp.concatenate(quarters_all(part, core, side), axis=0)

    gate_all = pair(row, gate_flat, partner_of(gate_flat), 0)
    up_all = pair(row, up_flat, partner_of(up_flat), 0)
    down_all = pair(row, down_flat, partner_of(down_flat), 1)

    kept = lax.dynamic_slice_in_dim(cotangent, row * own_tokens, own_tokens, 0)
    sent = lax.dynamic_slice_in_dim(cotangent, (1 - row) * own_tokens, own_tokens, 0)
    cot_own = pair(row, kept, swap(sent, "row", 1), 1)
    cot_slots = gather_col(cot_own, col)
    for bit in (1, 2):
        cot_slots = [
            jnp.where(col & bit == 0, cot_slots[k], cot_slots[k ^ bit]) for k in range(cols)
        ]
    cot_all = jnp.stack(cot_slots)

    chosen = routes[:, :, None] == jnp.arange(experts, dtype=jnp.int32)[None, None, :]
    table = jnp.sum(jnp.where(chosen, route_gates[:, :, None], 0.0), axis=1)
    tables = lax.dynamic_index_in_dim(
        table.reshape(cols, 2, own_tokens, experts), row, 1, False
    )

    inputs_full = inputs_all.astype(full)
    first_scale = lax.rsqrt(jnp.mean(inputs_full * inputs_full, axis=1, keepdims=True) + epsilon)
    normed = (inputs_full * first_scale * norm_all[None, :]).astype(low)
    projected = dot(normed, joint_weight)
    ends = jnp.cumsum(lengths_row)
    starts = ends - lengths_row
    odd = col % 2
    place = odd * tokens + jnp.arange(tokens, dtype=jnp.int32)
    begin = jnp.max(jnp.where(starts[None, :] <= place[:, None], starts[None, :], 0), axis=1)
    position = place - begin
    start = (begin + (1 - odd) * tokens)[:, None]
    theta = rope_base ** (-jnp.arange(0, head_dim, 2, dtype=full) / head_dim)
    angles = position.astype(full)[:, None] * theta[None, :]
    cosine, sine = jnp.cos(angles), jnp.sin(angles)
    cosine = jnp.concatenate([cosine, cosine], axis=1)
    sine = jnp.concatenate([-sine, sine], axis=1)
    key_at = query_block
    value_at = 2 * query_block + keyval_block
    key_own = rotate(projected[:, key_at : key_at + head_dim], cosine, sine).astype(low)
    value_own = projected[:, value_at : value_at + head_dim].astype(low)
    own_pair = jnp.concatenate([key_own, value_own], axis=1)
    before = lax.ppermute(own_pair, "col", [(i, i + 1) for i in range(0, cols, 2)])
    pairs = jnp.concatenate([before, own_pair], axis=0)
    keys, values = pairs[:, :head_dim], pairs[:, head_dim:]
    attended, rot = attention_forward(projected, cosine, sine, keys, values, start, heads)

    branch_part = dot(attended, head_output).astype(low)
    kept = lax.dynamic_slice_in_dim(branch_part, row * own_tokens, own_tokens, 0)
    sent = lax.dynamic_slice_in_dim(branch_part, (1 - row) * own_tokens, own_tokens, 0)
    branch = kept.astype(full) + swap(sent, "row", 1).astype(full)
    inputs_own = lax.dynamic_slice_in_dim(inputs_all, row * own_tokens, own_tokens, 0)
    middle = inputs_own.astype(full) + branch
    second_scale = lax.rsqrt(jnp.mean(middle * middle, axis=1, keepdims=True) + epsilon)
    expert_own = (middle * second_scale * mixer_all[None, :]).astype(low)
    second_grad, out_part, gate_total, up_own, up_row, up_other, down_half = experts_call(
        expert_own, cot_all, tables, gate_all, up_all, down_all
    )

    both_block = query_block + keyval_block
    (
        outputs,
        input_grad,
        gain_sums,
        output_total,
        joint_total,
        up_total,
        down_total,
        _,
    ) = finish_call(
        second_grad, middle, cot_own, mixer_all[None, :], norm_gain[None, :], first_scale, inputs,
        attended, rot, keys, values, cosine, sine, start, head_output, joint_weight, normed,
        out_part, up_own, up_row, up_other, down_half, query_block, both_block,
    )
    gain_sums = lax.dynamic_slice_in_dim(gain_sums, row * part_width, part_width, 1)
    norm_total, mixer_total = gain_sums[0], gain_sums[1]

    def by_expert(flat):
        return flat.reshape(part_width, experts, units).transpose(1, 0, 2).astype(full)

    gate_total, up_total = by_expert(gate_total), by_expert(up_total)
    down_total = down_total.reshape(experts, units, part_width).astype(full)
    output_total = output_total.astype(full)
    joint_total = joint_total.astype(full)
    query_total, keyval_total = joint_total[:, :query_block], joint_total[:, query_block:]
    return (
        outputs,
        input_grad,
        norm_total,
        query_total,
        keyval_total,
        output_total,
        mixer_total,
        gate_total,
        up_total,
        down_total,
    )


def solution(mesh):
    return jax.shard_map(
        shards,
        mesh=mesh,
        in_specs=(
            P(("dp", "col"), "row"),
            P("row"),
            P("row", "col"),
            P("row", "col"),
            P("col", "row"),
            P("row"),
            P(None, "row", "col"),
            P(None, "row", "col"),
            P(None, "col", "row"),
            P(("dp", "row"), None),
            P("dp", None),
            P("dp", None),
            P(("dp", "col"), "row"),
        ),
        out_specs=(
            P(("dp", "col"), "row"),
            P(("dp", "col"), "row"),
            P("row"),
            P("row", "col"),
            P("row", "col"),
            P("col", "row"),
            P("row"),
            P(None, "row", "col"),
            P(None, "row", "col"),
            P(None, "col", "row"),
        ),
        check_vma=False,
    )
```

time: 703 us -> 550 us (0.78)
  Pallas kernels: 134 us -> 294 us
  waiting for transfers between devices: 212 us -> 95.5 us
  starting transfers between devices: 142 us -> 66.3 us
  blocking collectives: 47.9 us -> 0 us
  other arithmetic: 77.2 us -> 43.8 us
  local copies, waits for them, and re-layouts: 61.3 us -> 37.5 us
  matrix products: 15.5 us -> 3.18 us
    pallas_call x2, Pallas kernels: 125 us -> 285 us  [the longest x1 167 us: finish_call(): pl.pallas_call(finish_kernel, in_specs=[vmem] * 17 + [anywhere] * 5, out_...]
    ppermute x39 -> x18, waiting for transfers between devices: 185 us -> 70.7 us  [swap(): return lax.ppermute(block, axis, [(i, i ^ bit) for i in range(count)])]
    psum x1 -> x0, blocking collectives: 47.9 us -> none  [shards(): lax.psum(jnp.stack([spread_norm, mixer_partial]), ('dp', 'row', 'col'))]
    ppermute x19 -> x0, starting transfers between devices: 44.8 us -> none  [the longest x9 26 us: scatter_col(): lax.ppermute(to_left, 'col', [(i, i - 1) for i in range(count - 1, count...]
    ppermute x39 -> x18, starting transfers between devices: 64.8 us -> 28.2 us  [swap(): return lax.ppermute(block, axis, [(i, i ^ bit) for i in range(count)])]
    convert_element_type x29 -> x3, other arithmetic: 26.2 us -> 7.13 us  [the longest x1 4.42 us: shards(): down_total = down_total.reshape(experts, units, part_width).astype(full)]
    dot_general x6 -> x2, matrix products: 15.5 us -> 3.18 us  [dot(): lax.dot_general(left, right, (((left_dim,), (right_dim,)), ((), ())), pre...]
    reshape x2 -> x0, local copies, waits for them, and re-layouts: 10.8 us -> none  [the longest x1 5.99 us: shards(): output_part_grad.reshape(2, query_block, 2, part_width)]
  transfers between devices with their start and end apart: 73 -> 33, of which waited for: 23 -> 11; matrix products, arithmetic and copies ran while one was open for 20% -> 10% of each run, Pallas kernels for 2% -> 0%
where the time goes in v3:
time: 550 us; the launch traced here: 542 us
  Pallas kernels  294 us (53%)
  waiting for transfers between devices  95.5 us (17%)
  starting transfers between devices  66.3 us (12%)
  other arithmetic  43.8 us (8%)
  local copies, waits for them, and re-layouts  37.5 us (7%)
    pallas_call x1, Pallas kernels, finish_call(): pl.pallas_call(finish_kernel, in_specs=[vmem] * 17 + [anywhere] * 5, out_...  167 us
    pallas_call x1, Pallas kernels, experts_call(): pl.pallas_call(experts_kernel, in_specs=[vmem] * 3 + [anywhere] * 3, out_...  117 us
    ppermute x18, waiting for transfers between devices, swap(): return lax.ppermute(block, axis, [(i, i ^ bit) for i in range(count)])  70.7 us
    ppermute x18, starting transfers between devices, swap(): return lax.ppermute(block, axis, [(i, i ^ bit) for i in range(count)])  28.2 us
    ppermute x3, starting transfers between devices, gather_col(): lax.ppermute(from_left[-1], 'col', [(i, i + 1) for i in range(step - 1, c...  15.3 us
    ppermute x8, starting transfers between devices, spread(): arrived.append(lax.ppermute(part, ('row', 'col'), route))  15.1 us
    ppermute x8, waiting for transfers between devices, spread(): arrived.append(lax.ppermute(part, ('row', 'col'), route))  12.8 us
    unnamed x102, local copies, waits for them, and re-layouts  11.2 us
  transfers between devices with their start and end apart: 33, of which 11 were waited for; matrix products, arithmetic and copies ran while one was open for 10% of the time, Pallas kernels for 0%

profile of v3, /device:TPU:17, one launch (start us, length us, event | category | flops | bytes accessed | tf_op | source)
XLA Modules:
  0.0 542.0 jit_solution(13557802112212072686)
XLA Ops:
  9.3 4.3 copy.49
  27.0 5.0 collective-permute-start.2
  37.6 7.3 %collective-permute-done.2 = bf16[192,512]{1,0:T(8,128)(2,1)S(1)} collective-permute-done((bf16[192,512]{1,0:T(8,128)(2,1)S(1)}, bf16[192,512]{1,0:T(8,128)(2,1)S(1)}, u32[]{:S(2)}, u32[]{:S(2)}) %collective-permute-start.2) | collective-permute-done | bytes 196640 | tf_op jit(solution)/shard_map/ppermute | solution.py:1360
  44.9 4.3 collective-permute-done.3
  54.2 33.1 %collective-permute-done.17 = bf16[256,768]{1,0:T(8,128)(2,1)S(1)} collective-permute-done((bf16[256,768]{1,0:T(8,128)(2,1)S(1)}, bf16[256,768]{1,0:T(8,128)(2,1)S(1)}, u32[]{:S(2)}, u32[]{:S(2)}) %collective-permute-start.17) | collective-permute-done | bytes 393248 | tf_op jit(solution)/shard_map/ppermute | solution.py:19
  93.2 5.0 collective-permute-start.18
  98.3 6.4 %collective-permute-done = bf16[512,768]{1,0:T(8,128)(2,1)S(1)} collective-permute-done((bf16[512,768]{1,0:T(8,128)(2,1)S(1)}, bf16[512,768]{1,0:T(8,128)(2,1)S(1)}, u32[]{:S(2)}, u32[]{:S(2)}) %collective-permute-start) | collective-permute-done | bytes 786464 | tf_op jit(solution)/shard_map/ppermute | solution.py:19
  114.5 6.0 %collective-permute-done.28 = bf16[192,1536]{1,0:T(8,128)(2,1)} collective-permute-done((bf16[192,1536]{1,0:T(8,128)(2,1)}, bf16[192,1536]{1,0:T(8,128)(2,1)}, u32[]{:S(2)}, u32[]{:S(2)}) %collective-permute-start.28) | collective-permute-done | bytes 589856 | tf_op jit(solution)/shard_map/ppermute | solution.py:19
  120.5 5.9 %collective-permute-start.15 = (bf16[2,4,96,768]{3,2,1,0:T(8,128)(2,1)S(1)}, bf16[2,4,96,768]{3,2,1,0:T(8,128)(2,1)S(1)}, u32[]{:S(2)}, u32[]{:S(2)}) collective-permute-start(bf16[2,4,96,768]{3,2,1,0:T(8,128)(2,1)S(1)} %copy-done.27), channel_id=1, source_target_pairs={{0,8},{8,0},{16,24},{24,16},{1,9},{9,1},{17,25},{25,17},{2,10},{10... | collective-permute-start | bytes 3538952 | tf_op jit(solution)/shard_map/ppermute | solution.py:19
  127.7 5.3 collective-permute-done.31
  133.0 5.9 %collective-permute-start.7 = (bf16[2,4,192,512]{3,2,1,0:T(8,128)(2,1)S(1)}, bf16[2,4,192,512]{3,2,1,0:T(8,128)(2,1)}, u32[]{:S(2)}, u32[]{:S(2)}) collective-permute-start(bf16[2,4,192,512]{3,2,1,0:T(8,128)(2,1)S(1)} %pad_maximum_fusion.10), channel_id=1, source_target_pairs={{0,8},{8,0},{16,24},{24,16},{1,9},{9,1},{17,25},{25,17},{2,10},{10... | collective-permute-start | bytes 4718600 | tf_op jit(solution)/shard_map/ppermute | solution.py:19
  140.3 5.4 collective-permute-done.25
  145.6 3.1 collective-permute-start.32
  150.2 5.3 collective-permute-start.20
  161.2 11.0 %collective-permute-done.20 = bf16[256,1536]{1,0:T(8,128)(2,1)} collective-permute-done((bf16[256,1536]{1,0:T(8,128)(2,1)}, bf16[256,1536]{1,0:T(8,128)(2,1)}, u32[]{:S(2)}, u32[]{:S(2)}) %collective-permute-start.20) | collective-permute-done | bytes 786464 | tf_op jit(solution)/shard_map/ppermute | solution.py:39
  173.5 5.0 collective-permute-start.22
  189.7 3.8 pad_maximum_fusion
  206.3 8.9 %shard_map.204 = (bf16[512,768]{1,0:T(8,128)(2,1)S(1)}, bf16[512,768]{1,0:T(8,128)(2,1)S(1)}) custom-call(f32[512,1024]{1,0:T(8,128)S(1)} %fusion.44.pre_ref, f32[512,128]{1,0:T(8,128)S(1)} %get-tuple-element.151.cosine_ref, f32[512,128]{1,0:T(8,128)S(1)} %get-tuple-element.53.sine_ref, bf16[1024,128]{1,0:T(8,128)(2,1)S(1)} %get-tuple-element.150.key_ref, ...), custom_call_target="tpu_custom_call" | custom-call | flops 1207959552 | bytes 3145728 | tf_op jit(solution)/shard_map/pallas_call | solution.py:99
  220.6 14.5 %collective-permute-done.16 = bf16[256,1536]{1,0:T(8,128)(2,1)S(1)} collective-permute-done((bf16[256,1536]{1,0:T(8,128)(2,1)S(1)}, bf16[256,1536]{1,0:T(8,128)(2,1)S(1)}, u32[]{:S(2)}, u32[]{:S(2)}) %collective-permute-start.16) | collective-permute-done | bytes 786464 | tf_op jit(solution)/shard_map/ppermute | solution.py:19
  237.8 117.3 %shard_map.205 = (f32[256,1536]{1,0:T(8,128)}, bf16[4,256,1536]{2,1,0:T(8,128)(2,1)}, bf16[768,1536]{1,0:T(8,128)(2,1)}, bf16[768,768]{1,0:T(8,128)(2,1)}, bf16[...) custom-call(bf16[256,1536]{1,0:T(8,128)(2,1)} %multiply_convert_fusion.own_ref, ...), custom_call_target="tpu_custom_call" | custom-call | flops 43486543872 | bytes 28311552 | tf_op jit(solution)/shard_map/pallas_call | solution.py:583
  355.1 167.3 %shard_map.206 = (bf16[512,768]{1,0:T(8,128)(2,1)}, bf16[512,768]{1,0:T(8,128)(2,1)}, f32[8,1536]{1,0:T(8,128)}, bf16[384,768]{1,0:T(8,128)(2,1)}, bf16[768,512]...) custom-call(f32[256,1536]{1,0:T(8,128)} %get-tuple-element.27.sum_ref, ...), custom_call_target="tpu_custom_call" | custom-call | flops 10000000000 | bytes 40000000 | tf_op jit(solution)/shard_map/pallas_call | solution.py:1235
  525.6 3.0 copy.54
  528.5 4.4 convert.9
  534.0 3.0 copy.53
  (229 shorter events, 99.3 us)
Async XLA Ops:
  1.7 30.9 %collective-permute-start.10 = (bf16[96,768]{1,0:T(8,128)(2,1)S(1)}, bf16[96,768]{1,0:T(8,128)(2,1)S(1)}, u32[]{:S(2)}, u32[]{:S(2)}) collective-permute-start(bf16[96,768]{1,0:T(8,128)(2,1)S(1)} %constant_dynamic-slice_fusion.6), channel_id=1, source_target_pairs={{0,0},{1,1},{2,4},{3,5},{4,2},{5,3},{6,6},{7,7},{8,8},{9,9},{10,12... | collective-permute-start | bytes 442376 | tf_op jit(solution)/shard_map/ppermute | solution.py:1360
  4.7 29.1 %collective-permute-start.11 = (bf16[96,768]{1,0:T(8,128)(2,1)S(1)}, bf16[96,768]{1,0:T(8,128)(2,1)}, u32[]{:S(2)}, u32[]{:S(2)}) collective-permute-start(bf16[96,768]{1,0:T(8,128)(2,1)S(1)} %constant_dynamic-slice_fusion.6), channel_id=1, source_target_pairs={{0,1},{1,0},{2,5},{3,4},{4,3},{5,2},{6,7},{7,6},{8,9},{9,8},{10,13... | collective-permute-start | bytes 442376 | tf_op jit(solution)/shard_map/ppermute | solution.py:1360
  7.1 26.6 %collective-permute-start.12 = (bf16[96,768]{1,0:T(8,128)(2,1)S(1)}, bf16[96,768]{1,0:T(8,128)(2,1)}, u32[]{:S(2)}, u32[]{:S(2)}) collective-permute-start(bf16[96,768]{1,0:T(8,128)(2,1)S(1)} %constant_dynamic-slice_fusion.6), channel_id=1, source_target_pairs={{0,2},{1,3},{2,6},{3,7},{4,0},{5,1},{6,4},{7,5},{8,10},{9,11},{10,... | collective-permute-start | bytes 442376 | tf_op jit(solution)/shard_map/ppermute | solution.py:1360
  7.1 29.1 %collective-permute-start.13 = (bf16[96,768]{1,0:T(8,128)(2,1)S(1)}, bf16[96,768]{1,0:T(8,128)(2,1)}, u32[]{:S(2)}, u32[]{:S(2)}) collective-permute-start(bf16[96,768]{1,0:T(8,128)(2,1)S(1)} %constant_dynamic-slice_fusion.6), channel_id=1, source_target_pairs={{0,3},{1,2},{2,7},{3,6},{4,1},{5,0},{6,5},{7,4},{8,11},{9,10},{10,... | collective-permute-start | bytes 442376 | tf_op jit(solution)/shard_map/ppermute | solution.py:1360
  33.7 18.1 %collective-permute-start.5 = (bf16[192,512]{1,0:T(8,128)(2,1)S(1)}, bf16[192,512]{1,0:T(8,128)(2,1)S(1)}, u32[]{:S(2)}, u32[]{:S(2)}) collective-permute-start(bf16[192,512]{1,0:T(8,128)(2,1)S(1)} %fusion.7), channel_id=1, source_target_pairs={{0,3},{1,2},{2,7},{3,6},{4,1},{5,0},{6,5},{7,4},{8,11},{9,10},{10,... | collective-permute-start | bytes 589832 | tf_op jit(solution)/shard_map/ppermute | solution.py:1360
  36.2 72.8 %collective-permute-start.30 = (bf16[384,768]{1,0:T(8,128)(2,1)}, bf16[384,768]{1,0:T(8,128)(2,1)}, u32[]{:S(2)}, u32[]{:S(2)}) collective-permute-start(bf16[384,768]{1,0:T(8,128)(2,1)} %constant_dynamic-slice_fusion), channel_id=1, source_target_pairs={{0,4},{4,0},{1,5},{5,1},{2,6},{6,2},{3,7},{7,3},{8,12},{12,8},{9,1... | collective-permute-start | bytes 1769480 | tf_op jit(solution)/shard_map/ppermute | solution.py:19
  44.9 48.4 %collective-permute-start.27 = (bf16[192,1536]{1,0:T(8,128)(2,1)}, bf16[192,1536]{1,0:T(8,128)(2,1)}, u32[]{:S(2)}, u32[]{:S(2)}) collective-permute-start(bf16[192,1536]{1,0:T(8,128)(2,1)} %constant_dynamic-slice_fusion.1), channel_id=1, source_target_pairs={{0,4},{4,0},{1,5},{5,1},{2,6},{6,2},{3,7},{7,3},{8,12},{12,8},{9,1... | collective-permute-start | bytes 1769480 | tf_op jit(solution)/shard_map/ppermute | solution.py:19
  49.2 62.1 %collective-permute-start.24 = (bf16[192,1536]{1,0:T(8,128)(2,1)}, bf16[192,1536]{1,0:T(8,128)(2,1)}, u32[]{:S(2)}, u32[]{:S(2)}) collective-permute-start(bf16[192,1536]{1,0:T(8,128)(2,1)} %constant_dynamic-slice_fusion.2), channel_id=1, source_target_pairs={{0,4},{4,0},{1,5},{5,1},{2,6},{6,2},{3,7},{7,3},{8,12},{12,8},{9,1... | collective-permute-start | bytes 1769480 | tf_op jit(solution)/shard_map/ppermute | solution.py:19
  49.2 38.2 %collective-permute-start.17 = (bf16[256,768]{1,0:T(8,128)(2,1)S(1)}, bf16[256,768]{1,0:T(8,128)(2,1)S(1)}, u32[]{:S(2)}, u32[]{:S(2)}) collective-permute-start(bf16[256,768]{1,0:T(8,128)(2,1)S(1)} %constant_dynamic-slice_fusion.4), channel_id=1, source_target_pairs={{0,4},{4,0},{1,5},{5,1},{2,6},{6,2},{3,7},{7,3},{8,12},{12,8},{9,1... | collective-permute-start | bytes 1179656 | tf_op jit(solution)/shard_map/ppermute | solution.py:19
  51.9 38.8 %collective-permute-start.14 = (bf16[4,96,768]{2,1,0:T(8,128)(2,1)S(1)}, bf16[4,96,768]{2,1,0:T(8,128)(2,1)S(1)}, u32[]{:S(2)}, u32[]{:S(2)}) collective-permute-start(bf16[4,96,768]{2,1,0:T(8,128)(2,1)S(1)} %pad_maximum_fusion.17), channel_id=1, source_target_pairs={{0,16},{8,24},{16,0},{24,8},{1,17},{9,25},{17,1},{25,9},{2,18},{10... | collective-permute-start | bytes 1769480 | tf_op jit(solution)/shard_map/ppermute | solution.py:19
  90.7 21.0 %collective-permute-start.6 = (bf16[4,192,512]{2,1,0:T(8,128)(2,1)}, bf16[4,192,512]{2,1,0:T(8,128)(2,1)}, u32[]{:S(2)}, u32[]{:S(2)}) collective-permute-start(bf16[4,192,512]{2,1,0:T(8,128)(2,1)} %pad_maximum_fusion.15), channel_id=1, source_target_pairs={{0,16},{8,24},{16,0},{24,8},{1,17},{9,25},{17,1},{25,9},{2,18},{10... | collective-permute-start | bytes 2359304 | tf_op jit(solution)/shard_map/ppermute | solution.py:19
  93.2 56.8 %collective-permute-start.18 = (bf16[256,1536]{1,0:T(8,128)(2,1)}, bf16[256,1536]{1,0:T(8,128)(2,1)}, u32[]{:S(2)}, u32[]{:S(2)}) collective-permute-start(bf16[256,1536]{1,0:T(8,128)(2,1)} %pad_maximum_fusion.16.cot_ref), channel_id=1, source_target_pairs={{0,1},{1,2},{2,3},{4,5},{5,6},{6,7},{8,9},{9,10},{10,11},{12,13},{... | collective-permute-start | bytes 2359304 | tf_op jit(solution)/shard_map/ppermute | solution.py:39
  108.9 41.2 %collective-permute-start.19 = (bf16[256,1536]{1,0:T(8,128)(2,1)}, bf16[256,1536]{1,0:T(8,128)(2,1)S(1)}, u32[]{:S(2)}, u32[]{:S(2)}) collective-permute-start(bf16[256,1536]{1,0:T(8,128)(2,1)} %pad_maximum_fusion.16.cot_ref), channel_id=1, source_target_pairs={{1,0},{2,1},{3,2},{5,4},{6,5},{7,6},{9,8},{10,9},{11,10},{13,12},{... | collective-permute-start | bytes 2359304 | tf_op jit(solution)/shard_map/ppermute | solution.py:42
  111.3 21.7 %collective-permute-start.31 = (bf16[384,768]{1,0:T(8,128)(2,1)}, bf16[384,768]{1,0:T(8,128)(2,1)S(1)}, u32[]{:S(2)}, u32[]{:S(2)}) collective-permute-start(bf16[384,768]{1,0:T(8,128)(2,1)} %collective-permute-done.30), channel_id=1, source_target_pairs={{0,16},{8,24},{16,0},{24,8},{1,17},{9,25},{17,1},{25,9},{2,18},{10... | collective-permute-start | bytes 1769480 | tf_op jit(solution)/shard_map/ppermute | solution.py:19
  111.7 34.0 %collective-permute-start.25 = (bf16[192,1536]{1,0:T(8,128)(2,1)}, bf16[192,1536]{1,0:T(8,128)(2,1)S(1)}, u32[]{:S(2)}, u32[]{:S(2)}) collective-permute-start(bf16[192,1536]{1,0:T(8,128)(2,1)} %collective-permute-done.24), channel_id=1, source_target_pairs={{0,16},{8,24},{16,0},{24,8},{1,17},{9,25},{17,1},{25,9},{2,18},{10... | collective-permute-start | bytes 1769480 | tf_op jit(solution)/shard_map/ppermute | solution.py:19
  120.5 35.0 %collective-permute-start.15 = (bf16[2,4,96,768]{3,2,1,0:T(8,128)(2,1)S(1)}, bf16[2,4,96,768]{3,2,1,0:T(8,128)(2,1)S(1)}, u32[]{:S(2)}, u32[]{:S(2)}) collective-permute-start(bf16[2,4,96,768]{3,2,1,0:T(8,128)(2,1)S(1)} %copy-done.27), channel_id=1, source_target_pairs={{0,8},{8,0},{16,24},{24,16},{1,9},{9,1},{17,25},{25,17},{2,10},{10... | collective-permute-start | bytes 3538952 | tf_op jit(solution)/shard_map/ppermute | solution.py:19
  133.0 60.5 %collective-permute-start.7 = (bf16[2,4,192,512]{3,2,1,0:T(8,128)(2,1)S(1)}, bf16[2,4,192,512]{3,2,1,0:T(8,128)(2,1)}, u32[]{:S(2)}, u32[]{:S(2)}) collective-permute-start(bf16[2,4,192,512]{3,2,1,0:T(8,128)(2,1)S(1)} %pad_maximum_fusion.10), channel_id=1, source_target_pairs={{0,8},{8,0},{16,24},{24,16},{1,9},{9,1},{17,25},{25,17},{2,10},{10... | collective-permute-start | bytes 4718600 | tf_op jit(solution)/shard_map/ppermute | solution.py:19
  145.6 32.9 %collective-permute-start.32 = (bf16[2,384,768]{2,1,0:T(8,128)(2,1)S(1)}, bf16[2,384,768]{2,1,0:T(8,128)(2,1)S(1)}, u32[]{:S(2)}, u32[]{:S(2)}) collective-permute-start(bf16[2,384,768]{2,1,0:T(8,128)(2,1)S(1)} %pad_maximum_fusion.14), channel_id=1, source_target_pairs={{0,8},{8,0},{16,24},{24,16},{1,9},{9,1},{17,25},{25,17},{2,10},{10... | collective-permute-start | bytes 3538952 | tf_op jit(solution)/shard_map/ppermute | solution.py:19
  150.1 31.8 %collective-permute-start.29 = (bf16[2,192,1536]{2,1,0:T(8,128)(2,1)S(1)}, bf16[2,192,1536]{2,1,0:T(8,128)(2,1)S(1)}, u32[]{:S(2)}, u32[]{:S(2)}) collective-permute-start(bf16[2,192,1536]{2,1,0:T(8,128)(2,1)S(1)} %pad_maximum_fusion.13), channel_id=1, source_target_pairs={{0,8},{8,0},{16,24},{24,16},{1,9},{9,1},{17,25},{25,17},{2,10},{10... | collective-permute-start | bytes 3538952 | tf_op jit(solution)/shard_map/ppermute | solution.py:19
  150.2 22.0 %collective-permute-start.20 = (bf16[256,1536]{1,0:T(8,128)(2,1)}, bf16[256,1536]{1,0:T(8,128)(2,1)}, u32[]{:S(2)}, u32[]{:S(2)}) collective-permute-start(bf16[256,1536]{1,0:T(8,128)(2,1)} %collective-permute-done.18), channel_id=1, source_target_pairs={{1,2},{2,3},{5,6},{6,7},{9,10},{10,11},{13,14},{14,15},{17,18},{18... | collective-permute-start | bytes 2359304 | tf_op jit(solution)/shard_map/ppermute | solution.py:39
  155.5 18.0 %collective-permute-start.21 = (bf16[256,1536]{1,0:T(8,128)(2,1)S(1)}, bf16[256,1536]{1,0:T(8,128)(2,1)}, u32[]{:S(2)}, u32[]{:S(2)}) collective-permute-start(bf16[256,1536]{1,0:T(8,128)(2,1)S(1)} %collective-permute-done.19), channel_id=1, source_target_pairs={{1,0},{2,1},{5,4},{6,5},{9,8},{10,9},{13,12},{14,13},{17,16},{18,1... | collective-permute-start | bytes 2359304 | tf_op jit(solution)/shard_map/ppermute | solution.py:42
  173.5 29.0 %collective-permute-start.22 = (bf16[256,1536]{1,0:T(8,128)(2,1)}, bf16[256,1536]{1,0:T(8,128)(2,1)}, u32[]{:S(2)}, u32[]{:S(2)}) collective-permute-start(bf16[256,1536]{1,0:T(8,128)(2,1)} %collective-permute-done.20), channel_id=1, source_target_pairs={{2,3},{6,7},{10,11},{14,15},{18,19},{22,23},{26,27},{30,31}} | collective-permute-start | bytes 2359304 | tf_op jit(solution)/shard_map/ppermute | solution.py:39
  178.5 24.0 %collective-permute-start.23 = (bf16[256,1536]{1,0:T(8,128)(2,1)}, bf16[256,1536]{1,0:T(8,128)(2,1)}, u32[]{:S(2)}, u32[]{:S(2)}) collective-permute-start(bf16[256,1536]{1,0:T(8,128)(2,1)} %collective-permute-done.21), channel_id=1, source_target_pairs={{1,0},{5,4},{9,8},{13,12},{17,16},{21,20},{25,24},{29,28}} | collective-permute-start | bytes 2359304 | tf_op jit(solution)/shard_map/ppermute | solution.py:42
  216.7 18.3 %collective-permute-start.16 = (bf16[256,1536]{1,0:T(8,128)(2,1)S(1)}, bf16[256,1536]{1,0:T(8,128)(2,1)S(1)}, u32[]{:S(2)}, u32[]{:S(2)}) collective-permute-start(bf16[256,1536]{1,0:T(8,128)(2,1)S(1)} %constant_dynamic-slice_fusion.5), channel_id=1, source_target_pairs={{0,4},{4,0},{1,5},{5,1},{2,6},{6,2},{3,7},{7,3},{8,12},{12,8},{9,1... | collective-permute-start | bytes 2359304 | tf_op jit(solution)/shard_map/ppermute | solution.py:19
  (52 other events, 692.1 us)

commit v4 on v3

--- a/solution.py
+++ b/solution.py
@@ -14,108 +14,10 @@
 full = jnp.float32
 
 
-def swap(block, axis, bit):
-    count = lax.axis_size(axis)
-    return lax.ppermute(block, axis, [(i, i ^ bit) for i in range(count)])
-
-
-def pair(bit, own, other, axis):
-    first = jnp.where(bit == 0, own, other)
-    second = jnp.where(bit == 0, other, own)
-    return jnp.concatenate([first, second], axis=axis)
-
-
 def dot(left, right, left_dim=1, right_dim=0):
     return lax.dot_general(
         left, right, (((left_dim,), (right_dim,)), ((), ())), preferred_element_type=full
     )
-
-
-def gather_col(block, col):
-    count = lax.axis_size("col")
-    from_left, from_right = [block], [block]
-    for step in range(1, count):
-        from_left.append(
-            lax.ppermute(from_left[-1], "col", [(i, i + 1) for i in range(step - 1, count - 1)])
-        )
-        from_right.append(
-            lax.ppermute(from_right[-1], "col", [(i + 1, i) for i in range(count - step)])
-        )
-    slots = [block]
-    for k in range(1, count):
-        chosen = None
-        for at in range(count):
-            there = at ^ k
-            value = from_right[there - at] if there > at else from_left[at - there]
-            chosen = value if chosen is None else jnp.where(col == at, value, chosen)
-        slots.append(chosen)
-    return slots
-
-
-def quarter_of(block, quarter):
-    size = block.shape[0] // 4
-    return lax.dynamic_slice_in_dim(block, quarter * size, size, 0)
-
-
-def quarters_all(block, core, side):
-    across = swap(block, "dp", 2)
-    two = [jnp.where(side == 0, block, across), jnp.where(side == 0, across, block)]
-    both = jnp.stack(two)
-    near = swap(both, "dp", 1)
-    result = []
-    for at in range(2):
-        result.append(jnp.where(core == 0, both[at], near[at]))
-        result.append(jnp.where(core == 0, near[at], both[at]))
-    return result
-
-
-def attention_forward_kernel(
-    pre_ref, cosine_ref, sine_ref, key_ref, value_ref, start_ref, out_ref, rot_ref, *, window, tile
-):
-    rows = pre_ref.shape[0]
-    pre = pre_ref[...]
-    rot = (pre * cosine_ref[...] + pltpu.roll(pre, head_dim // 2, 1) * sine_ref[...]).astype(low)
-    rot_ref[...] = rot
-    for at in range(rows // tile):
-        first = at * tile
-        keys = key_ref[first : first + window, :]
-        values = value_ref[first : first + window, :]
-        scores = dot(rot[first : first + tile], keys, 1, 1) * head_dim ** (-0.5)
-        place = lax.broadcasted_iota(jnp.int32, scores.shape, 1) + first
-        query = lax.broadcasted_iota(jnp.int32, scores.shape, 0) + (first + rows)
-        allowed = (place <= query) & (place >= start_ref[first : first + tile, :])
-        scores = jnp.where(allowed, scores, -1e30)
-        exponent = jnp.exp(scores - jnp.max(scores, axis=1, keepdims=True))
-        weights = exponent / jnp.sum(exponent, axis=1, keepdims=True)
-        out_ref[first : first + tile, :] = dot(weights.astype(low), values).astype(low)
-
-
-def attention_forward(pre, cosine, sine, keys, values, start, heads):
-    rows, reach = pre.shape[0], keys.shape[0]
-    whole = lambda shape: pl.BlockSpec(shape, lambda h: (0, 0))
-    head = pl.BlockSpec((rows, head_dim), lambda h: (0, h))
-    shape = jax.ShapeDtypeStruct((rows, heads * head_dim), low)
-    per_half = heads // 2
-    return pl.pallas_call(
-        functools.partial(attention_forward_kernel, window=reach - rows // 2, tile=rows // 2),
-        grid=(heads,),
-        in_specs=[
-            pl.BlockSpec((rows, head_dim), lambda h: (0, h + h // per_half)),
-            whole((rows, head_dim)),
-            whole((rows, head_dim)),
-            whole((reach, head_dim)),
-            whole((reach, head_dim)),
-            whole((rows, 1)),
-        ],
-        out_specs=[head, head],
-        out_shape=[shape, shape],
-        compiler_params=pltpu.CompilerParams(vmem_limit_bytes=32 * 2**20),
-        cost_estimate=pl.CostEstimate(
-            flops=heads * rows * reach * 3 * head_dim,
-            bytes_accessed=heads * rows * head_dim * 8,
-            transcendentals=heads * rows * reach,
-        ),
-    )(pre, cosine, sine, keys, values, start)
 
 
 def remote_copy(source, target, send_sem, recv_sem, **device):
@@ -625,6 +527,652 @@
             transcendentals=blocks * rows * width,
         ),
     )(own, cot, table, gate_all, up_all, down_all)
+
+
+def prologue_kernel(
+    inputs_ref,
+    small_ref,
+    theta_ref,
+    routes_ref,
+    route_gates_ref,
+    query_hbm,
+    keyval_hbm,
+    output_hbm,
+    gate_hbm,
+    up_hbm,
+    down_hbm,
+    cot_hbm,
+    normed_ref,
+    scale_ref,
+    mixer_ref,
+    key_ref,
+    value_ref,
+    cosine_ref,
+    sine_ref,
+    start_ref,
+    attended_ref,
+    rot_ref,
+    joint_ref,
+    head_output_ref,
+    middle_ref,
+    expert_ref,
+    table_ref,
+    cot_all_ref,
+    gate_all_ref,
+    up_all_ref,
+    down_all_ref,
+    inputs_all,
+    inputs_sem,
+    small,
+    small_sem,
+    raw,
+    raw_sem,
+    flat,
+    flat_sem,
+    projected,
+    branch_own,
+    branch_stage,
+    branch_arrived,
+    branch_sem,
+    pair_sem,
+    joint_uni,
+    joint_side,
+    joint_core,
+    output_uni,
+    output_side,
+    output_core,
+    expert_row,
+    expert_side,
+    expert_core,
+    cot_sem,
+    cot_recv,
+    cot_send,
+    *,
+    sequences,
+):
+    row, col, dp = lax.axis_index("row"), lax.axis_index("col"), lax.axis_index("dp")
+    cols = lax.axis_size("col")
+    last = cols - 1
+    core, side, other = dp % 2, (dp // 2) % 2, 1 - row
+    quarter = dp % 4
+    core_partner, side_partner = dp + 1 - 2 * core, dp + 2 - 4 * side
+    tokens, part_width = inputs_ref.shape
+    width, rows = 2 * part_width, tokens // 2
+    query_block, keyval_block = query_hbm.shape[1], keyval_hbm.shape[1]
+    block = query_block + keyval_block
+    experts, units = gate_hbm.shape[0], gate_hbm.shape[2]
+
+    raws = [
+        pltpu.make_async_copy(source, raw.at[i], raw_sem.at[i])
+        for i, source in enumerate((gate_hbm, up_hbm))
+    ]
+    for copy in raws:
+        copy.start()
+
+    barrier = pltpu.get_barrier_semaphore()
+
+    def greet(**device):
+        pl.semaphore_signal(
+            barrier, inc=1, device_id=device, device_id_type=pl.DeviceIdType.MESH
+        )
+
+    for there in range(1, 2 * cols):
+        greet(row=(row + there // cols) % 2, col=(col + there % cols) % cols)
+    greet(dp=core_partner)
+    greet(dp=side_partner)
+
+    def part_lanes(which):
+        return pl.ds(pl.multiple_of(which * part_width, 128), part_width)
+
+    inputs_all[:, part_lanes(row)] = inputs_ref[...]
+    small[row] = small_ref[...]
+    pl.semaphore_wait(barrier, 2 * cols + 1)
+
+    inputs_copy = remote_copy(
+        inputs_ref,
+        inputs_all.at[:, part_lanes(row)],
+        inputs_sem.at[0],
+        inputs_sem.at[1],
+        row=other,
+    )
+    small_copy = remote_copy(
+        small.at[row], small.at[row], small_sem.at[0], small_sem.at[1], row=other
+    )
+    inputs_copy.start()
+    small_copy.start()
+
+    joint_size, output_size = query_hbm.shape[0] // 4, output_hbm.shape[0] // 4
+
+    def joint_region(r0, b, which):
+        return joint_ref.at[
+            pl.ds(pl.multiple_of(r0 * part_width + which * joint_size, 16), joint_size),
+            pl.ds(pl.multiple_of(b * block, 128), block),
+        ]
+
+    def output_region(r0, b, which):
+        return head_output_ref.at[
+            pl.ds(pl.multiple_of(b * query_block + which * output_size, 16), output_size),
+            part_lanes(r0),
+        ]
+
+    def own_joint():
+        b = col % 2
+        first = pl.ds(pl.multiple_of(quarter * joint_size, 16), joint_size)
+        at = pl.ds(pl.multiple_of(row * part_width + quarter * joint_size, 16), joint_size)
+        return (
+            (
+                query_hbm.at[first],
+                joint_ref.at[at, pl.ds(pl.multiple_of(b * block, 128), query_block)],
+            ),
+            (
+                keyval_hbm.at[first],
+                joint_ref.at[
+                    at, pl.ds(pl.multiple_of(b * block + query_block, 128), keyval_block)
+                ],
+            ),
+        )
+
+    def own_output():
+        first = pl.ds(pl.multiple_of(quarter * output_size, 16), output_size)
+        return ((output_hbm.at[first], output_region(row, col % 2, quarter)),)
+
+    def spread(pieces, sems):
+        def copies(k):
+            to_row, to_col = col // 2, (2 * row + col % 2 + k) % cols
+            return [
+                remote_copy(
+                    source, target, sems.at[k, 2 * n], sems.at[k, 2 * n + 1], row=to_row, col=to_col
+                )
+                for n, (source, target) in enumerate(pieces)
+            ]
+
+        def here():
+            return [
+                pltpu.make_async_copy(source, target, sems.at[0, 2 * n + 1])
+                for n, (source, target) in enumerate(pieces)
+            ]
+
+        home = col // 2 == row
+
+        def start():
+            for k in range(cols):
+                if k == 0:
+
+                    @pl.when(home)
+                    def _():
+                        for copy in here():
+                            copy.start()
+
+                    @pl.when(jnp.logical_not(home))
+                    def _():
+                        for copy in copies(0):
+                            copy.start()
+
+                else:
+                    for copy in copies(k):
+                        copy.start()
+
+        def wait_recv(k):
+            if k == 0:
+
+                @pl.when(home)
+                def _():
+                    for copy in here():
+                        copy.wait()
+
+                @pl.when(jnp.logical_not(home))
+                def _():
+                    for copy in copies(0):
+                        copy.wait_recv()
+
+            else:
+                for copy in copies(k):
+                    copy.wait_recv()
+
+        def wait_send():
+            for k in range(cols):
+                if k == 0:
+
+                    @pl.when(jnp.logical_not(home))
+                    def _():
+                        for copy in copies(0):
+                            copy.wait_send()
+
+                else:
+                    for copy in copies(k):
+                        copy.wait_send()
+
+        return start, wait_recv, wait_send
+
+    def came_from(k):
+        j = (col - k + cols) % cols
+        return j // 2, j % 2
+
+    def relay(region, side_sems, core_sems):
+        def side_copy(k):
+            there = region(*came_from(k), quarter)
+            return remote_copy(
+                there, there, side_sems.at[k, 0], side_sems.at[k, 1], dp=side_partner
+            )
+
+        def core_copies(k):
+            result = []
+            for n in range(2):
+                there = region(*came_from(k), core + 2 * n)
+                result.append(
+                    remote_copy(
+                        there,
+                        there,
+                        core_sems.at[k, 2 * n],
+                        core_sems.at[k, 2 * n + 1],
+                        dp=core_partner,
+                    )
+                )
+            return result
+
+        return side_copy, core_copies
+
+    joint_start, joint_wait, joint_sent = spread(own_joint(), joint_uni)
+    output_start, output_wait, output_sent = spread(own_output(), output_uni)
+    joint_side_copy, joint_core_copies = relay(joint_region, joint_side, joint_core)
+    output_side_copy, output_core_copies = relay(output_region, output_side, output_core)
+    joint_start()
+
+    expert_size = part_width // 4
+    down_size = down_hbm.shape[0] // 4
+
+    def flatten(which):
+        raws[which].wait()
+        for e in range(0, experts, 2):
+            flat[which, :, e * units : (e + 2) * units] = jnp.concatenate(
+                [raw[which, e], raw[which, e + 1]], axis=1
+            )
+
+    totals = (gate_all_ref, up_all_ref, down_all_ref)
+
+    def expert_region(which, of_row, of_quarter):
+        if which < 2:
+            first = pl.multiple_of(of_row * part_width + of_quarter * expert_size, 16)
+            return totals[which].at[pl.ds(first, expert_size)]
+        first = pl.multiple_of(of_quarter * down_size, 16)
+        return totals[2].at[pl.ds(first, down_size), part_lanes(of_row)]
+
+    def expert_local(which):
+        if which < 2:
+            target = totals[which].at[pl.ds(pl.multiple_of(row * part_width, 16), part_width)]
+            return pltpu.make_async_copy(flat.at[which], target, flat_sem.at[which])
+        return pltpu.make_async_copy(down_hbm, totals[2].at[:, part_lanes(row)], flat_sem.at[2])
+
+    def expert_row_copy(which):
+        if which < 2:
+            source = flat.at[which, pl.ds(pl.multiple_of(quarter * expert_size, 16), expert_size)]
+        else:
+            source = down_hbm.at[pl.ds(pl.multiple_of(quarter * down_size, 16), down_size)]
+        return remote_copy(
+            source,
+            expert_region(which, row, quarter),
+            expert_row.at[which, 0],
+            expert_row.at[which, 1],
+            row=other,
+        )
+
+    def expert_side_copy(which):
+        there = expert_region(which, other, quarter)
+        return remote_copy(
+            there, there, expert_side.at[which, 0], expert_side.at[which, 1], dp=side_partner
+        )
+
+    def expert_core_copies(which):
+        result = []
+        for n in range(2):
+            there = expert_region(which, other, core + 2 * n)
+            result.append(
+                remote_copy(
+                    there,
+                    there,
+                    expert_core.at[which, 2 * n],
+                    expert_core.at[which, 2 * n + 1],
+                    dp=core_partner,
+                )
+            )
+        return result
+
+    def expert_after_row(which):
+        expert_row_copy(which).wait_recv()
+        expert_side_copy(which).start()
+
+    def expert_after_side(which):
+        expert_side_copy(which).wait_recv()
+        for copy in expert_core_copies(which):
+            copy.start()
+
+    def token_rows(which):
+        return pl.ds(pl.multiple_of(which * rows, 16), rows)
+
+    cot_target = cot_all_ref.at[col, :, part_lanes(row)]
+    cot_local = pltpu.make_async_copy(cot_hbm.at[token_rows(row)], cot_target, cot_sem.at[0])
+    cot_row = remote_copy(
+        cot_hbm.at[token_rows(other)], cot_target, cot_sem.at[1], cot_sem.at[2], row=other
+    )
+
+    def cot_copy(block_at, right):
+        return remote_copy(
+            cot_all_ref.at[block_at],
+            cot_all_ref.at[block_at],
+            cot_send.at[block_at, 1 if right else 0],
+            cot_recv.at[block_at],
+            col=col + 1 if right else col - 1,
+        )
+
+    def cot_first():
+        cot_local.wait()
+        cot_row.wait_recv()
+        pl.when(col < last)(lambda: cot_copy(col, True).start())
+        pl.when(col > 0)(lambda: cot_copy(col, False).start())
+
+    def cot_pass(apart):
+        @pl.when(col - apart >= 0)
+        def _():
+            cot_copy(col - apart, True).wait_recv()
+            pl.when(col < last)(lambda: cot_copy(col - apart, True).start())
+
+        @pl.when(col + apart <= last)
+        def _():
+            cot_copy(col + apart, False).wait_recv()
+            pl.when(col > 0)(lambda: cot_copy(col + apart, False).start())
+
+    cot_local.start()
+    expert_local(2).start()
+
+    for at in range(cols):
+        place = pl.ds(pl.multiple_of(at * tokens + row * rows, 16), rows)
+        chosen, gates = routes_ref[place, :], route_gates_ref[place, :]
+        lane = lax.broadcasted_iota(jnp.int32, (rows, experts), 1)
+        table = jnp.zeros((rows, experts), full)
+        for k in range(chosen.shape[1]):
+            table += jnp.where(chosen[:, k : k + 1] == lane, gates[:, k : k + 1], 0.0)
+        table_ref[at] = table
+
+    for which in range(2):
+        flatten(which)
+        expert_local(which).start()
+
+    small_copy.wait_recv()
+    mixer_ref[:, :part_width] = small[0, 1:2, :]
+    mixer_ref[:, part_width:] = small[1, 1:2, :]
+    half = col // 2
+    lens = small[half, 2:3, :]
+    odd = (col % 2).astype(full)
+    place = lax.broadcasted_iota(jnp.int32, (tokens, 1), 0).astype(full) + odd * tokens
+    begin = jnp.zeros((tokens, 1), full)
+    total = lens[:, 0:1]
+    for n in range(1, sequences):
+        begin = jnp.where(place >= total, total, begin)
+        total = total + lens[:, n : n + 1]
+    start_ref[...] = begin + (1.0 - odd) * tokens
+    angles = (place - begin) * theta_ref[...]
+    cosine_ref[...] = jnp.cos(angles)
+    sine = jnp.sin(angles)
+    lane = lax.broadcasted_iota(jnp.int32, sine.shape, 1)
+    sine_ref[...] = jnp.where(lane < head_dim // 2, -sine, sine)
+
+    for k in range(cols):
+        joint_wait(k)
+        joint_side_copy(k).start()
+    inputs_copy.wait_recv()
+    cot_row.start()
+    output_start()
+    expert_row_copy(0).start()
+
+    piece = 64
+
+    def norm_piece(at, carry):
+        here = pl.ds(pl.multiple_of(at * piece, piece), piece)
+        values = inputs_all[here, :].astype(full)
+        scale = lax.rsqrt(jnp.mean(values * values, axis=1, keepdims=True) + epsilon)
+        scale_ref[here, :] = scale
+        for which in range(2):
+            lanes = slice(which * part_width, (which + 1) * part_width)
+            normed_ref[here, lanes] = (values[:, lanes] * scale * small[which, 0:1, :]).astype(low)
+        return carry
+
+    lax.fori_loop(0, tokens // piece, norm_piece, 0)
+    for k in range(cols):
+        joint_side_copy(k).wait_recv()
+        for copy in joint_core_copies(k):
+            copy.start()
+    expert_row_copy(1).start()
+    for k in range(cols):
+        for copy in joint_core_copies(k):
+            copy.wait_recv()
+
+    projected[...] = dot(normed_ref[...], joint_ref[...])
+    own = slice(tokens, 2 * tokens)
+    key = projected[:, query_block : query_block + head_dim]
+    key_ref[own, :] = (
+        key * cosine_ref[...] + pltpu.roll(key, head_dim // 2, 1) * sine_ref[...]
+    ).astype(low)
+    value_ref[own, :] = projected[:, block + query_block : block + query_block + head_dim].astype(low)
+
+    def pair_copies():
+        return [
+            remote_copy(
+                ref.at[pl.ds(tokens, tokens)],
+                ref.at[pl.ds(0, tokens)],
+                pair_sem.at[n, 0],
+                pair_sem.at[n, 1],
+                col=col + 1 - 2 * (col % 2),
+            )
+            for n, ref in enumerate((key_ref, value_ref))
+        ]
+
+    @pl.when(col % 2 == 0)
+    def _():
+        for copy in pair_copies():
+            copy.start()
+        key_ref[:tokens, :] = jnp.zeros((tokens, head_dim), low)
+        value_ref[:tokens, :] = jnp.zeros((tokens, head_dim), low)
+
+    for k in range(cols):
+        output_wait(k)
+        output_side_copy(k).start()
+    cot_first()
+    expert_row_copy(2).start()
+
+    @pl.when(col % 2 == 1)
+    def _():
+        for copy in pair_copies():
+            copy.wait_recv()
+
+    heads = 2 * query_block // head_dim
+    per_block = heads // 2
+    tile = tokens // 2
+    window = key_ref.shape[0] - tile
+
+    def head_step(head, carry):
+        here = pl.ds(pl.multiple_of(head * head_dim, head_dim), head_dim)
+        there = pl.ds(
+            pl.multiple_of((head + head // per_block) * head_dim, head_dim), head_dim
+        )
+        pre = projected[:, there]
+        rot = (pre * cosine_ref[...] + pltpu.roll(pre, head_dim // 2, 1) * sine_ref[...]).astype(low)
+        rot_ref[:, here] = rot
+        for at in range(tokens // tile):
+            first = at * tile
+            keys = key_ref[first : first + window, :]
+            values = value_ref[first : first + window, :]
+            scores = dot(rot[first : first + tile], keys, 1, 1) * head_dim ** (-0.5)
+            key_place = lax.broadcasted_iota(jnp.int32, scores.shape, 1) + first
+            query_place = lax.broadcasted_iota(jnp.int32, scores.shape, 0) + (first + tokens)
+            allowed = (key_place <= query_place) & (
+                key_place.astype(full) >= start_ref[first : first + tile, :]
+            )
+            scores = jnp.where(allowed, scores, -1e30)
+            exponent = jnp.exp(scores - jnp.max(scores, axis=1, keepdims=True))
+            weights = exponent / jnp.sum(exponent, axis=1, keepdims=True)
+            attended_ref[first : first + tile, here] = dot(weights.astype(low), values).astype(low)
+        return carry
+
+    lax.fori_loop(0, heads, head_step, 0)
+
+    for k in range(cols):
+        output_side_copy(k).wait_recv()
+        for copy in output_core_copies(k):
+            copy.start()
+    expert_after_row(0)
+    cot_pass(1)
+    for k in range(cols):
+        for copy in output_core_copies(k):
+            copy.wait_recv()
+
+    def branch_copy(part):
+        return remote_copy(
+            branch_stage.at[part],
+            branch_arrived.at[part],
+            branch_sem.at[part, 0],
+            branch_sem.at[part, 1],
+            row=other,
+        )
+
+    theirs = attended_ref[token_rows(other), :]
+    for part in range(2):
+        lanes = slice(part * part_width, (part + 1) * part_width)
+        branch_stage[part] = dot(theirs, head_output_ref[:, lanes]).astype(low)
+        branch_copy(part).start()
+    mine = attended_ref[token_rows(row), :]
+    branch_own[...] = dot(mine, head_output_ref[...])
+    expert_after_row(1)
+    expert_after_side(0)
+    cot_pass(2)
+    expert_after_row(2)
+    for part in range(2):
+        lanes = slice(part * part_width, (part + 1) * part_width)
+        branch_copy(part).wait_recv()
+        middle_ref[:, lanes] = (
+            inputs_all[token_rows(row), lanes].astype(full)
+            + branch_own[:, lanes]
+            + branch_arrived[part].astype(full)
+        )
+
+    def second_piece(at, carry):
+        here = pl.ds(pl.multiple_of(at * piece, piece), piece)
+        values = middle_ref[here, :]
+        scale = lax.rsqrt(jnp.mean(values * values, axis=1, keepdims=True) + epsilon)
+        expert_ref[here, :] = (values * scale * mixer_ref[...]).astype(low)
+        return carry
+
+    lax.fori_loop(0, rows // piece, second_piece, 0)
+    expert_after_side(1)
+    cot_pass(3)
+    expert_after_side(2)
+
+    inputs_copy.wait_send()
+    small_copy.wait_send()
+    joint_sent()
+    output_sent()
+    for k in range(cols):
+        for copy in [joint_side_copy(k), output_side_copy(k)]:
+            copy.wait_send()
+        for copy in joint_core_copies(k) + output_core_copies(k):
+            copy.wait_send()
+    for which in range(3):
+        expert_local(which).wait()
+        expert_row_copy(which).wait_send()
+        expert_side_copy(which).wait_send()
+        for copy in expert_core_copies(which):
+            copy.wait()
+    cot_row.wait_send()
+    for at in range(cols):
+        pl.when((at <= col) & (col < last))(lambda: cot_copy(at, True).wait_send())
+        pl.when((at >= col) & (col > 0))(lambda: cot_copy(at, False).wait_send())
+
+    @pl.when(col % 2 == 0)
+    def _():
+        for copy in pair_copies():
+            copy.wait_send()
+
+    for part in range(2):
+        branch_copy(part).wait_send()
+
+
+def prologue_call(
+    inputs, small, theta, routes, route_gates, query_weight, key_value_matrix, output_weight,
+    gate_weight, up_weight, down_flat, cotangent, sequences,
+):
+    tokens, part_width = inputs.shape
+    cols = lax.axis_size("col")
+    width, rows = 2 * part_width, tokens // 2
+    query_block, keyval_block = query_weight.shape[1], key_value_matrix.shape[1]
+    block = query_block + keyval_block
+    experts, _, units = gate_weight.shape
+    hidden = experts * units
+    vmem = pl.BlockSpec(memory_space=pltpu.VMEM)
+    anywhere = pl.BlockSpec(memory_space=pl.ANY)
+    dma = pltpu.SemaphoreType.DMA
+    shape = jax.ShapeDtypeStruct
+    return pl.pallas_call(
+        functools.partial(prologue_kernel, sequences=sequences),
+        in_specs=[vmem] * 5 + [anywhere] * 7,
+        out_specs=[vmem] * 15 + [anywhere] * 4,
+        out_shape=[
+            shape((tokens, width), low),
+            shape((tokens, 1), full),
+            shape((1, width), full),
+            shape((2 * tokens, head_dim), low),
+            shape((2 * tokens, head_dim), low),
+            shape((tokens, head_dim), full),
+            shape((tokens, head_dim), full),
+            shape((tokens, 1), full),
+            shape((tokens, 2 * query_block), low),
+            shape((tokens, 2 * query_block), low),
+            shape((width, 2 * block), low),
+            shape((2 * query_block, width), low),
+            shape((rows, width), full),
+            shape((rows, width), low),
+            shape((cols, rows, experts), full),
+            shape((cols, rows, width), low),
+            shape((width, hidden), low),
+            shape((width, hidden), low),
+            shape((hidden, width), low),
+        ],
+        scratch_shapes=[
+            pltpu.VMEM((tokens, width), low),
+            dma((2,)),
+            pltpu.VMEM((2,) + small.shape, full),
+            dma((2,)),
+            pltpu.VMEM((2,) + gate_weight.shape, low),
+            dma((2,)),
+            pltpu.VMEM((2, part_width, hidden), low),
+            dma((3,)),
+            pltpu.VMEM((tokens, 2 * block), full),
+            pltpu.VMEM((rows, width), full),
+            pltpu.VMEM((2, rows, part_width), low),
+            pltpu.VMEM((2, rows, part_width), low),
+            dma((2, 2)),
+            dma((2, 2)),
+            dma((cols, 4)),
+            dma((cols, 2)),
+            dma((cols, 4)),
+            dma((cols, 2)),
+            dma((cols, 2)),
+            dma((cols, 4)),
+            dma((3, 2)),
+            dma((3, 2)),
+            dma((3, 4)),
+            dma((3,)),
+            dma((cols,)),
+            dma((cols, 2)),
+        ],
+        compiler_params=pltpu.CompilerParams(
+            collective_id=3, has_side_effects=True, vmem_limit_bytes=60 * 2**20
+        ),
+        cost_estimate=pl.CostEstimate(
+            flops=5 * 10**9, bytes_accessed=30 * 10**6, transcendentals=3 * 10**6
+        ),
+    )(
+        inputs, small, theta, routes, route_gates, query_weight, key_value_matrix, output_weight,
+        gate_weight, up_weight, down_flat, cotangent,
+    )
 
 
 def finish_kernel(
@@ -910,7 +1458,7 @@
             scores = dot(rot, keys, 1, 1) * head_dim ** (-0.5)
             place = lax.broadcasted_iota(jnp.int32, scores.shape, 1) + first
             query = lax.broadcasted_iota(jnp.int32, scores.shape, 0) + (first + tokens)
-            allowed = (place <= query) & (place >= start_ref[first : first + tile, :])
+            allowed = (place <= query) & (place.astype(full) >= start_ref[first : first + tile, :])
             scores = jnp.where(allowed, scores, -1e30)
             exponent = jnp.exp(scores - jnp.max(scores, axis=1, keepdims=True))
             probs = exponent / jnp.sum(exponent, axis=1, keepdims=True)
@@ -1307,10 +1855,6 @@
     )
 
 
-def rotate(matrix, cosine, sine):
-    return matrix * cosine + jnp.roll(matrix, head_dim // 2, axis=1) * sine
-
-
 def shards(
     inputs,
     norm_gain,
@@ -1326,129 +1870,42 @@
     route_gates,
     cotangent,
 ):
-    row, col, dp = lax.axis_index("row"), lax.axis_index("col"), lax.axis_index("dp")
-    core, side, quarter = dp % 2, (dp // 2) % 2, dp % 4
-    cols = lax.axis_size("col")
-    tokens, part_width = inputs.shape
-    width = 2 * part_width
-    own_tokens = tokens // 2
+    row, col = lax.axis_index("row"), lax.axis_index("col")
+    part_width = inputs.shape[1]
     experts, _, units = gate_weight.shape
     hidden_width = experts * units
     query_block, keyval_block = query_weight.shape[1], key_value_matrix.shape[1]
-    heads = 2 * query_block // head_dim
-
-    inputs_all = pair(row, inputs, swap(inputs, "row", 1), 1)
-    gains = jnp.stack([norm_gain, mixer_gain])
-    gains = pair(row, gains, swap(gains, "row", 1), 1)
-    norm_all, mixer_all = gains[0], gains[1]
-    lengths_all = pair(row, lengths, swap(lengths, "row", 1), 0)
-    lengths_row = jnp.where(col < cols // 2, lengths_all[0], lengths_all[1])
-
-    blocks = 2 * cols
-    joint = jnp.concatenate([query_weight, key_value_matrix], axis=1)
-    joint_part = quarter_of(joint, quarter)
-    output_part = quarter_of(output_weight, quarter)
-
-    def spread(part):
-        arrived = []
-        for k in range(cols):
-            route = []
-            for index in range(blocks):
-                from_row, from_col = index // cols, index % cols
-                to_row, to_col = from_col // 2, (2 * from_row + from_col % 2) ^ k
-                route.append((index, to_row * cols + to_col))
-            arrived.append(lax.ppermute(part, ("row", "col"), route))
-        for bit in (1, 2):
-            arrived = [
-                jnp.where(col & bit == 0, arrived[k], arrived[k ^ bit]) for k in range(cols)
-            ]
-        return jnp.stack(arrived)
-
-    joint_quarters = quarters_all(spread(joint_part), core, side)
-    output_quarters = quarters_all(spread(output_part), core, side)
-    joint_weight = jnp.concatenate(
-        [
-            jnp.concatenate(
-                [piece[2 * r + b] for r in range(2) for piece in joint_quarters], axis=0
-            )
-            for b in range(2)
-        ],
-        axis=1,
+    small = jnp.zeros((8, part_width), full)
+    small = small.at[0].set(norm_gain).at[1].set(mixer_gain)
+    sequences = lengths.shape[1]
+    small = small.at[2, :sequences].set(lengths[0].astype(full))
+    theta = rope_base ** (-jnp.arange(0, head_dim, 2, dtype=full) / head_dim)
+    theta = jnp.concatenate([theta, theta])[None, :]
+    (
+        normed,
+        first_scale,
+        mixer_all,
+        keys,
+        values,
+        cosine,
+        sine,
+        start,
+        attended,
+        rot,
+        joint_weight,
+        head_output,
+        middle,
+        expert_own,
+        tables,
+        cot_all,
+        gate_all,
+        up_all,
+        down_all,
+    ) = prologue_call(
+        inputs, small, theta, routes, route_gates, query_weight, key_value_matrix, output_weight,
+        gate_weight, up_weight, down_weight.reshape(hidden_width, part_width), cotangent, sequences,
     )
-    head_output = jnp.concatenate(
-        [
-            jnp.concatenate(
-                [piece[2 * r + b] for b in range(2) for piece in output_quarters], axis=0
-            )
-            for r in range(2)
-        ],
-        axis=1,
-    )
-
-    def flat_units(weight):
-        return weight.transpose(1, 0, 2).reshape(part_width, hidden_width)
-
-    gate_flat, up_flat = flat_units(gate_weight), flat_units(up_weight)
-    down_flat = down_weight.reshape(hidden_width, part_width)
-
-    def partner_of(flat):
-        part = swap(quarter_of(flat, quarter), "row", 1)
-        return jnp.concatenate(quarters_all(part, core, side), axis=0)
-
-    gate_all = pair(row, gate_flat, partner_of(gate_flat), 0)
-    up_all = pair(row, up_flat, partner_of(up_flat), 0)
-    down_all = pair(row, down_flat, partner_of(down_flat), 1)
-
-    kept = lax.dynamic_slice_in_dim(cotangent, row * own_tokens, own_tokens, 0)
-    sent = lax.dynamic_slice_in_dim(cotangent, (1 - row) * own_tokens, own_tokens, 0)
-    cot_own = pair(row, kept, swap(sent, "row", 1), 1)
-    cot_slots = gather_col(cot_own, col)
-    for bit in (1, 2):
-        cot_slots = [
-            jnp.where(col & bit == 0, cot_slots[k], cot_slots[k ^ bit]) for k in range(cols)
-        ]
-    cot_all = jnp.stack(cot_slots)
-
-    chosen = routes[:, :, None] == jnp.arange(experts, dtype=jnp.int32)[None, None, :]
-    table = jnp.sum(jnp.where(chosen, route_gates[:, :, None], 0.0), axis=1)
-    tables = lax.dynamic_index_in_dim(
-        table.reshape(cols, 2, own_tokens, experts), row, 1, False
-    )
-
-    inputs_full = inputs_all.astype(full)
-    first_scale = lax.rsqrt(jnp.mean(inputs_full * inputs_full, axis=1, keepdims=True) + epsilon)
-    normed = (inputs_full * first_scale * norm_all[None, :]).astype(low)
-    projected = dot(normed, joint_weight)
-    ends = jnp.cumsum(lengths_row)
-    starts = ends - lengths_row
-    odd = col % 2
-    place = odd * tokens + jnp.arange(tokens, dtype=jnp.int32)
-    begin = jnp.max(jnp.where(starts[None, :] <= place[:, None], starts[None, :], 0), axis=1)
-    position = place - begin
-    start = (begin + (1 - odd) * tokens)[:, None]
-    theta = rope_base ** (-jnp.arange(0, head_dim, 2, dtype=full) / head_dim)
-    angles = position.astype(full)[:, None] * theta[None, :]
-    cosine, sine = jnp.cos(angles), jnp.sin(angles)
-    cosine = jnp.concatenate([cosine, cosine], axis=1)
-    sine = jnp.concatenate([-sine, sine], axis=1)
-    key_at = query_block
-    value_at = 2 * query_block + keyval_block
-    key_own = rotate(projected[:, key_at : key_at + head_dim], cosine, sine).astype(low)
-    value_own = projected[:, value_at : value_at + head_dim].astype(low)
-    own_pair = jnp.concatenate([key_own, value_own], axis=1)
-    before = lax.ppermute(own_pair, "col", [(i, i + 1) for i in range(0, cols, 2)])
-    pairs = jnp.concatenate([before, own_pair], axis=0)
-    keys, values = pairs[:, :head_dim], pairs[:, head_dim:]
-    attended, rot = attention_forward(projected, cosine, sine, keys, values, start, heads)
-
-    branch_part = dot(attended, head_output).astype(low)
-    kept = lax.dynamic_slice_in_dim(branch_part, row * own_tokens, own_tokens, 0)
-    sent = lax.dynamic_slice_in_dim(branch_part, (1 - row) * own_tokens, own_tokens, 0)
-    branch = kept.astype(full) + swap(sent, "row", 1).astype(full)
-    inputs_own = lax.dynamic_slice_in_dim(inputs_all, row * own_tokens, own_tokens, 0)
-    middle = inputs_own.astype(full) + branch
-    second_scale = lax.rsqrt(jnp.mean(middle * middle, axis=1, keepdims=True) + epsilon)
-    expert_own = (middle * second_scale * mixer_all[None, :]).astype(low)
+    cot_own = lax.dynamic_index_in_dim(cot_all, col, 0, False)
     second_grad, out_part, gate_total, up_own, up_row, up_other, down_half = experts_call(
         expert_own, cot_all, tables, gate_all, up_all, down_all
     )
@@ -1464,7 +1921,7 @@
         down_total,
         _,
     ) = finish_call(
-        second_grad, middle, cot_own, mixer_all[None, :], norm_gain[None, :], first_scale, inputs,
+        second_grad, middle, cot_own, mixer_all, norm_gain[None, :], first_scale, inputs,
         attended, rot, keys, values, cosine, sine, start, head_output, joint_weight, normed,
         out_part, up_own, up_row, up_other, down_half, query_block, both_block,
     )

time: 550 us -> 450 us (0.82)
  Pallas kernels: 294 us -> 408 us
  waiting for transfers between devices: 95.5 us -> 0 us
  starting transfers between devices: 66.3 us -> 0 us
  other arithmetic: 43.8 us -> 4.97 us
  local copies, waits for them, and re-layouts: 37.5 us -> 28 us
    pallas_call x1, Pallas kernels: 8.9 us -> 117 us  [prologue_call(): pl.pallas_call(functools.partial(prologue_kernel, sequences=sequences), i...]
    ppermute x33 -> x0, waiting for transfers between devices: 95.5 us -> none  [the longest x18 70.7 us: swap(): return lax.ppermute(block, axis, [(i, i ^ bit) for i in range(count)])]
    ppermute x33 -> x0, starting transfers between devices: 66.3 us -> none  [the longest x18 28.2 us: swap(): return lax.ppermute(block, axis, [(i, i ^ bit) for i in range(count)])]
    concatenate x8 -> x0, other arithmetic: 11.2 us -> none  [the longest x3 7.33 us: pair(): return jnp.concatenate([first, second], axis=axis)]
    select_n x17 -> x0, other arithmetic: 11.2 us -> none  [the longest x3 3.61 us: quarters_all(): jnp.where(side == 0, block, across)]
    another operation x14 -> x0, other arithmetic: 9.41 us -> none  [the longest x3 5.25 us: shards(): cot_all = jnp.stack(cot_slots)]
    dynamic_slice x8 -> x0, local copies, waits for them, and re-layouts: 7.4 us -> none  [the longest x4 5.31 us: quarter_of(): return lax.dynamic_slice_in_dim(block, quarter * size, size, 0)]
    reshape x2 -> x0, local copies, waits for them, and re-layouts: 7.11 us -> none  [flat_units(): return weight.transpose(1, 0, 2).reshape(part_width, hidden_width)]
  transfers between devices with their start and end apart: 33 -> 0, of which waited for: 11 -> 0; matrix products, arithmetic and copies ran while one was open for 10% -> 0% of each run, Pallas kernels for 0% -> 0%
where the time goes in v4:
time: 450 us; the launch traced here: 442 us
  Pallas kernels  408 us (91%)
  local copies, waits for them, and re-layouts  28 us (6%)
  other arithmetic  4.97 us (1%)
    pallas_call x1, Pallas kernels, finish_call(): pl.pallas_call(finish_kernel, in_specs=[vmem] * 17 + [anywhere] * 5, out_...  167 us
    pallas_call x1, Pallas kernels, experts_call(): pl.pallas_call(experts_kernel, in_specs=[vmem] * 3 + [anywhere] * 3, out_...  124 us
    pallas_call x1, Pallas kernels, prologue_call(): pl.pallas_call(functools.partial(prologue_kernel, sequences=sequences), i...  117 us
    unnamed x26, local copies, waits for them, and re-layouts  13.4 us

profile of v4, /device:TPU:17, one launch (start us, length us, event | category | flops | bytes accessed | tf_op | source)
XLA Modules:
  0.0 442.0 jit_solution(361614238718028307)
XLA Ops:
  0.6 0.7 reshape.111.gain_ref
  1.3 0.7 reshape.112
  2.1 0.7 convert_element_type.34
  2.8 0.1 scatter.14.small_ref
  2.9 0.0 copy-start.3
  2.9 4.6 %copy.31.gate_hbm = bf16[8,768,192]{2,1,0:T(8,128)(2,1)} copy(bf16[8,768,192]{1,2,0:T(8,128)(2,1)} %param.25) | data formatting | bytes 4718592 | tf_op args[6]
  7.6 2.7 copy.32.up_hbm
  10.3 1.3 copy.29.routes_ref
  11.6 1.3 copy.30.route_gates_ref
  13.0 0.6 maximum_bitcast_fusion.theta_ref
  13.6 116.5 %shard_map.204 = (bf16[512,1536]{1,0:T(8,128)(2,1)}, f32[512,1]{1,0:T(8,128)}, f32[1,1536]{1,0:T(1,128)}, bf16[1024,128]{1,0:T(8,128)(2,1)}, bf16[1024,128]{1,0:...) custom-call(bf16[512,768]{1,0:T(8,128)(2,1)} %inputs_ref.3, ...), custom_call_target="tpu_custom_call" | custom-call | flops 5000000000 | bytes 30000000 | tf_op jit(solution)/shard_map/pallas_call | solution.py:1113
  130.1 124.3 %shard_map.205 = (f32[256,1536]{1,0:T(8,128)}, bf16[4,256,1536]{2,1,0:T(8,128)(2,1)}, bf16[768,1536]{1,0:T(8,128)(2,1)}, bf16[768,768]{1,0:T(8,128)(2,1)}, bf16[...) custom-call(bf16[256,1536]{1,0:T(8,128)(2,1)} %get-tuple-element.79.own_ref, ...), custom_call_target="tpu_custom_call" | custom-call | flops 43486543872 | bytes 28311552 | tf_op jit(solution)/shard_map/pallas_call | solution.py:485
  254.4 2.1 dynamic-slice_bitcast_fusion.cot_ref
  256.5 167.0 %shard_map.206 = (bf16[512,768]{1,0:T(8,128)(2,1)}, bf16[512,768]{1,0:T(8,128)(2,1)}, f32[8,1536]{1,0:T(8,128)}, bf16[384,768]{1,0:T(8,128)(2,1)}, bf16[768,512]...) custom-call(f32[256,1536]{1,0:T(8,128)} %get-tuple-element.85.sum_ref, ...), custom_call_target="tpu_custom_call" | custom-call | flops 10000000000 | bytes 40000000 | tf_op jit(solution)/shard_map/pallas_call | solution.py:1783
  423.5 4.7 %copy.34 = f32[768,1536]{0,1:T(8,128)} copy(bf16[768,1536]{1,0:T(8,128)(2,1)} %get-tuple-element.110) | data formatting | bytes 7077888 | tf_op jit(solution)/shard_map/convert_element_type | solution.py:1932
  428.2 2.6 convert.5
  430.8 1.1 convert_element_type.36
  431.9 0.4 copy-done
  432.3 1.1 slice.64
  433.4 0.8 slice.65
  434.2 1.5 dynamic-slice_reduce_fusion
  435.7 3.0 copy.33
  438.6 2.1 copy.39
  440.7 0.9 copy.40
  (21 shorter events, 0.1 us)
Async XLA Ops:
  1.3 6.2 %copy-start.9 = (f32[1,768]{1,0:T(1,128)}, f32[1,768]{1,0:T(1,128)S(1)}, u32[]{:S(2)}) copy-start(f32[1,768]{1,0:T(1,128)S(1)} %reshape.111.gain_ref) | copy-start | bytes 9220
  2.9 4.7 %copy-start.8 = (f32[8,768]{1,0:T(8,128)}, f32[8,768]{1,0:T(8,128)S(1)}, u32[]{:S(2)}) copy-start(f32[8,768]{1,0:T(8,128)S(1)} %scatter.14.small_ref) | copy-start | bytes 73732
  2.9 4.7 %copy-start.3 = (bf16[8,768,192]{1,2,0:T(8,128)(2,1)S(1)}, bf16[8,768,192]{1,2,0:T(8,128)(2,1)}, u32[]{:S(2)}) copy-start(bf16[8,768,192]{1,2,0:T(8,128)(2,1)} %param.26) | copy-start | bytes 7077892
  7.5 2.8 copy-start.6
  7.6 4.1 copy-start.7
  423.5 4.7 %copy-start.2 = (bf16[1536,768]{1,0:T(8,128)(2,1)S(1)}, bf16[1536,768]{1,0:T(8,128)(2,1)}, u32[]{:S(2)}) copy-start(bf16[1536,768]{1,0:T(8,128)(2,1)} %get-tuple-element.111) | copy-start | bytes 7077892
  428.2 2.6 copy-start.5
  430.8 1.5 copy-start
  430.8 4.8 %copy-start.1 = (bf16[768,1536]{1,0:T(8,128)(2,1)S(1)}, bf16[768,1536]{1,0:T(8,128)(2,1)}, u32[]{:S(2)}) copy-start(bf16[768,1536]{1,0:T(8,128)(2,1)} %get-tuple-element.109) | copy-start | bytes 7077892
  435.7 5.0 %copy-start.4 = (bf16[512,768]{1,0:T(8,128)(2,1)S(1)}, bf16[512,768]{1,0:T(8,128)(2,1)}, u32[]{:S(2)}) copy-start(bf16[512,768]{1,0:T(8,128)(2,1)} %get-tuple-element.125) | copy-start | bytes 2359300

commit v5 on v4

v5 whole, which is shorter than its diff:
```python
import functools

import jax
import jax.numpy as jnp
from jax import lax
from jax.experimental import pallas as pl
from jax.experimental.pallas import tpu as pltpu
from jax.sharding import PartitionSpec as P

epsilon = 1e-06
rope_base = 1000000.0
head_dim = 128
low = jnp.bfloat16
full = jnp.float32


def dot(left, right, left_dim=1, right_dim=0):
    return lax.dot_general(
        left, right, (((left_dim,), (right_dim,)), ((), ())), preferred_element_type=full
    )


def remote_copy(source, target, send_sem, recv_sem, **device):
    return pltpu.make_async_remote_copy(
        src_ref=source,
        dst_ref=target,
        send_sem=send_sem,
        recv_sem=recv_sem,
        device_id=device,
        device_id_type=pl.DeviceIdType.MESH,
    )


def add_low(left, right):
    return (left.astype(full) + right.astype(full)).astype(low)


class ColSum:
    def __init__(self, stack, arrived, send_sem, recv_sem, col, count, blocks):
        self.stack, self.arrived, self.send_sem, self.recv_sem = stack, arrived, send_sem, recv_sem
        self.col, self.last, self.blocks = col, count - 1, list(blocks)

    def copy(self, block, at, right):
        neighbour = at + 1 if right else at - 1
        n = self.blocks.index(block)
        slot = n if right or block != neighbour else len(self.blocks)
        return remote_copy(
            self.stack.at[n],
            self.arrived.at[slot],
            self.send_sem.at[n],
            self.recv_sem.at[slot],
            col=neighbour,
        )

    def wait(self, slot, at):
        remote_copy(
            self.arrived.at[slot],
            self.arrived.at[slot],
            self.send_sem.at[0],
            self.recv_sem.at[slot],
            col=at + 1 if at == 0 else at - 1,
        ).wait_recv()

    def step(self, number, placed=False):
        for at in range(self.last + 1):
            ways = []
            for right in (True, False):
                block = at + self.last + 1 - number if right else at - self.last - 1 + number
                if block in self.blocks:
                    ways.append((block, right))
            if not ways:
                continue

            @pl.when(self.col == at)
            def _(at=at, ways=ways):
                for block, right in ways:
                    n = self.blocks.index(block)
                    if 0 < at < self.last:
                        if not placed:
                            self.wait(n, at)
                        self.stack[n] = add_low(self.stack[n], self.arrived[n])
                    self.copy(block, at, right).start()

    def total(self, part):
        for n, at in enumerate(self.blocks):

            @pl.when(self.col == at)
            def _(n=n, at=at):
                value = self.stack[n].astype(full)
                if at > 0:
                    self.wait(n, at)
                    value += self.arrived[n].astype(full)
                if at < self.last:
                    self.wait(len(self.blocks), at)
                    value += self.arrived[len(self.blocks)].astype(full)
                part(value)

    def end(self, first=True):
        for at in range(self.last + 1):

            @pl.when(self.col == at)
            def _(at=at):
                for block in self.blocks:
                    if block != at and (first or abs(block - at) < self.last):
                        self.copy(block, at, block > at).wait_send()


def experts_kernel(
    own_ref,
    cot_ref,
    table_ref,
    gate_hbm,
    gate_other_hbm,
    up_hbm,
    up_other_hbm,
    down_hbm,
    down_other_hbm,
    sum_ref,
    out_part_ref,
    gate_total_ref,
    up_own_ref,
    up_row_ref,
    up_other_ref,
    down_half_ref,
    out_first_ref,
    weights,
    expert_in,
    gate_grad,
    up_grad,
    hidden,
    send_stage,
    arrived,
    parts,
    stage,
    weights_sem,
    down_sem,
    ready,
    ag_recv,
    ag_right,
    ag_left,
    rs_recv,
    rs_send,
    core_send,
    core_recv,
    row_send,
    row_recv,
    side_send,
    side_recv,
    final_sem,
    local_sem,
    out_sem,
):
    row, col, dp = lax.axis_index("row"), lax.axis_index("col"), lax.axis_index("dp")
    dps = lax.axis_size("dp")
    core, other = dp % 2, 1 - row
    core_partner = dp + 1 - 2 * core
    side_bits = list(range(1, dps.bit_length() - 1))
    sides = len(side_bits)
    last = cot_ref.shape[0] - 1
    rows, width = own_ref.shape
    half = width // 2
    size = half // 2
    inner = (col > 0) & (col < last)

    def across(bit):
        on = (dp // (1 << bit)) % 2
        return dp + (1 << bit) * (1 - 2 * on)

    def half_lanes(which):
        return pl.ds(pl.multiple_of(which * half, half), half)

    gate_ref, up_ref, down_ref = weights.at[0], weights.at[1], weights.at[2]
    sources = (gate_hbm, gate_other_hbm, up_hbm, up_other_hbm, down_hbm, down_other_hbm)
    loads = [
        pltpu.make_async_copy(
            source,
            weights.at[i // 2, :, half_lanes((row, other)[i % 2])],
            weights_sem.at[i],
        )
        for i, source in enumerate(sources)
    ]
    for copy in loads[:5]:
        copy.start()

    barrier = pltpu.get_barrier_semaphore()

    def greet(semaphore, **device):
        pl.semaphore_signal(
            semaphore, inc=1, device_id=device, device_id_type=pl.DeviceIdType.MESH
        )

    greet(barrier, dp=core_partner)
    greet(barrier, row=other)
    for bit in side_bits:
        greet(barrier, dp=across(bit))
    pl.when(col > 0)(lambda: greet(barrier, col=col - 1))
    pl.when(col < last)(lambda: greet(barrier, col=col + 1))
    expert_in[col] = own_ref[...]
    pl.when(inner)(lambda: pl.semaphore_wait(barrier, 4 + sides))
    pl.when(jnp.logical_not(inner))(lambda: pl.semaphore_wait(barrier, 3 + sides))

    def ag_copy(block, right):
        return remote_copy(
            expert_in.at[block],
            expert_in.at[block],
            (ag_right if right else ag_left).at[block],
            ag_recv.at[block],
            col=col + 1 if right else col - 1,
        )

    def rs_copy(block, part, right):
        neighbour = col + 1 if right else col - 1
        slot = block if right else jnp.where(block == neighbour, last + 1, block)
        return remote_copy(
            send_stage.at[block, part],
            arrived.at[slot, part],
            rs_send.at[block, part],
            rs_recv.at[slot, part],
            col=neighbour,
        )

    def rs_wait(slot, part):
        remote_copy(
            arrived.at[slot, part],
            arrived.at[slot, part],
            rs_send.at[0, part],
            rs_recv.at[slot, part],
            col=jnp.where(col > 0, col - 1, col + 1),
        ).wait_recv()

    pl.when(col < last)(lambda: ag_copy(col, True).start())
    pl.when(col > 0)(lambda: ag_copy(col, False).start())
    quarter_size = down_other_hbm.shape[0] // 4

    def down_quarter(which):
        return down_other_hbm.at[
            pl.ds(pl.multiple_of(which * quarter_size, 16), quarter_size)
        ]

    def down_room(which):
        first = pl.multiple_of(which * quarter_size, 16)
        return weights.at[2, pl.ds(first, quarter_size), half_lanes(other)]

    quarter = dp % 4
    down_side = remote_copy(
        down_quarter(quarter), down_room(quarter), down_sem.at[0], down_sem.at[1], dp=across(1)
    )
    down_own = pltpu.make_async_copy(down_quarter(quarter), down_room(quarter), weights_sem.at[5])

    def down_core(n):
        there = down_room(core + 2 * n)
        return remote_copy(
            there, there, down_sem.at[2 + 2 * n], down_sem.at[3 + 2 * n], dp=core_partner
        )

    down_side.start()
    down_own.start()
    for copy in loads[:5]:
        copy.wait()
    down_own.wait()
    down_side.wait_recv()
    for n in range(2):
        down_core(n).start()
    for n in range(2):
        down_core(n).wait()
    down_side.wait_send()

    def compute(block):
        tokens = expert_in[block]
        grads = cot_ref[block]
        table = table_ref[block]
        experts = table.shape[1]
        units = width // experts
        for g in range(2):
            cols = slice(g * half, (g + 1) * half)
            gate = dot(tokens, gate_ref[cols, :], 1, 1)
            up = dot(tokens, up_ref[cols, :], 1, 1)
            grad = dot(grads, down_ref[cols, :], 1, 1)
            lane = lax.broadcasted_iota(jnp.int32, gate.shape, 1)
            first = g * experts // 2
            chosen = jnp.broadcast_to(table[:, first : first + 1], gate.shape)
            for e in range(1, experts // 2):
                chosen = jnp.where(lane >= e * units, table[:, first + e : first + e + 1], chosen)
            sigmoid = 1.0 / (1.0 + jnp.exp(-gate))
            silu = gate * sigmoid
            grad = grad * chosen
            hidden[block, :, cols] = (silu * up * chosen).astype(low)
            gate_grad[block, :, cols] = (
                grad * up * (sigmoid * (1.0 + gate * (1.0 - sigmoid)))
            ).astype(low)
            up_grad[block, :, cols] = (grad * silu).astype(low)
        gates_now, ups_now = gate_grad[block], up_grad[block]
        for part in range(2):
            cols = slice(part * half, (part + 1) * half)
            total = dot(gates_now, gate_ref[:, cols]) + dot(ups_now, up_ref[:, cols])
            send_stage[block, part] = total.astype(low)
            pl.when((col == 0) & (block != col))(lambda: rs_copy(block, part, True).start())
            pl.when((col == last) & (block != col))(lambda: rs_copy(block, part, False).start())
        out_part_ref[block] = dot(hidden[block], down_ref[...]).astype(low)

    def step(i, carry):
        apart = (i + 1) // 2
        from_left = i % 2 == 1

        @pl.when(from_left & (col - apart >= 0))
        def _():
            block = col - apart
            ag_copy(block, True).wait_recv()
            pl.when(col < last)(lambda: ag_copy(block, True).start())

        @pl.when(from_left & (col + apart <= last))
        def _():
            block = col + apart
            ag_copy(block, False).wait_recv()
            pl.when(col > 0)(lambda: ag_copy(block, False).start())

        block = jnp.where(from_left, col - apart, col + apart)
        pl.when((block >= 0) & (block <= last))(lambda: compute(block))
        return carry

    lax.fori_loop(0, 2 * last + 1, step, 0)

    greet(ready.at[0], dp=core_partner)
    greet(ready.at[1], row=other)
    for number, bit in enumerate(side_bits):
        greet(ready.at[2 + number], dp=across(bit))

    def room(which, down, right):
        return weights.at[
            which, pl.ds(down * half, half), pl.ds(right * half, half)
        ]

    def forward(block, right):
        for part in range(2):
            rs_wait(block, part)
            send_stage[block, part] = add_low(send_stage[block, part], arrived[block, part])
            rs_copy(block, part, right).start()

    def event(number):
        blocks = ((2, 1), (3, 0), (0, 3))[number]
        pl.when(col == 1)(lambda: forward(blocks[0], number < 2))
        pl.when(col == 2)(lambda: forward(blocks[1], number == 2))

    def core_copy(at):
        if at < 4:
            target = room(at // 2, 0, at % 2)
        else:
            target = room(2, 0, at - 4)
        return remote_copy(
            stage.at[at % 2], target, core_send.at[at], core_recv.at[at], dp=core_partner
        )

    def stage_free(at):
        if at >= 2:
            core_copy(at - 2).wait_send()

    def core_dot(at):
        left = (gate_grad, up_grad)[at // 2]
        right = expert_in[:, :, half_lanes(row if at % 2 else other)].reshape(-1, half)
        stage_free(at)
        stage[at % 2] = dot(
            left[:, :, half_lanes(1 - core)].reshape(-1, half), right, 0, 0
        ).astype(low)
        core_copy(at).start()
        parts[at] = dot(left[:, :, half_lanes(core)].reshape(-1, half), right, 0, 0).astype(low)

    def core_sum(at):
        core_copy(at).wait_recv()
        parts[at] = add_low(parts[at], room(at // 2, 0, at % 2)[...])

    def down_dot_partner():
        left = hidden[:, :, half_lanes(1 - core)].reshape(-1, half)
        for part in range(2):
            lanes = slice(part * half, (part + 1) * half)
            right = cot_ref[:, :, lanes].reshape(-1, half)
            stage_free(4 + part)
            stage[part] = dot(left, right, 0, 0).astype(low)
            core_copy(4 + part).start()

    def down_dot_own():
        left = hidden[:, :, half_lanes(core)].reshape(-1, half)
        for part in range(2):
            lanes = slice(part * half, (part + 1) * half)
            right = cot_ref[:, :, lanes].reshape(-1, half)
            room(2, 1, part)[...] = dot(left, right, 0, 0).astype(low)

    def down_sum():
        for part in range(2):
            core_copy(4 + part).wait_recv()
            room(2, 1, part)[...] = add_low(room(2, 1, part)[...], room(2, 0, part)[...])

    down_out = pltpu.make_async_copy(
        weights.at[2, pl.ds(half, half)], down_half_ref, local_sem.at[0]
    )
    up_out = pltpu.make_async_copy(parts.at[3], up_own_ref, local_sem.at[1])
    up_rest = pltpu.make_async_copy(
        parts.at[2, pl.ds(size, size)], up_other_ref, local_sem.at[2]
    )

    def chunk_rows(chunk):
        return pl.ds(chunk * size, size)

    def row_copy(chunk):
        if chunk < 2:
            source = parts.at[0, chunk_rows(chunk)]
            target = weights.at[0, pl.ds(half + chunk * size, size), pl.ds(0, half)]
        else:
            source, target = parts.at[2, chunk_rows(0)], up_row_ref
        return remote_copy(source, target, row_send.at[chunk], row_recv.at[chunk], row=other)

    def side_room(number, chunk):
        which, right = ((0, 1), (1, 0), (1, 1))[number]
        return weights.at[
            which, pl.ds(half + chunk * size, size), pl.ds(right * half, half)
        ]

    def side_copy(chunk, number):
        return remote_copy(
            parts.at[1 - number % 2, chunk_rows(chunk)],
            side_room(number, chunk),
            side_send.at[chunk, number],
            side_recv.at[chunk, number],
            dp=across(side_bits[number]),
        )

    def after_row(chunk):
        copy = row_copy(chunk)
        copy.wait_recv()
        copy.wait_send()
        here = chunk_rows(chunk)
        landed = weights.at[0, pl.ds(half + chunk * size, size), pl.ds(0, half)]
        parts[1, here] = add_low(parts[1, here], landed[...])
        if sides:
            if chunk == 0:
                for number in range(sides):
                    pl.semaphore_wait(ready.at[2 + number], 1)
            side_copy(chunk, 0).start()

    def final_copies(chunk):
        source = parts.at[1 - sides % 2, chunk_rows(chunk)]
        first = pl.multiple_of(core * half + chunk * size, 16)
        target = gate_total_ref.at[pl.ds(first, size)]
        return (
            remote_copy(
                source, target, final_sem.at[chunk, 0], final_sem.at[chunk, 1], dp=core_partner
            ),
            pltpu.make_async_copy(source, target, final_sem.at[chunk, 2]),
        )

    def after_side(chunk):
        here = chunk_rows(chunk)
        for number in range(sides):
            copy = side_copy(chunk, number)
            copy.wait_recv()
            copy.wait_send()
            parts[number % 2, here] = add_low(
                parts[1 - number % 2, here], side_room(number, chunk)[...]
            )
            if number + 1 < sides:
                side_copy(chunk, number + 1).start()
        for copy in final_copies(chunk):
            copy.start()

    def out_copy(right):
        return remote_copy(
            out_part_ref.at[last if right else 0],
            out_first_ref,
            out_sem.at[0],
            out_sem.at[1],
            col=col + 1 if right else col - 1,
        )

    pl.semaphore_wait(ready.at[0], 1)
    core_dot(0)
    event(0)
    core_dot(1)
    core_sum(0)
    pl.semaphore_wait(ready.at[1], 1)
    row_copy(0).start()
    core_dot(2)
    core_sum(1)
    core_sum(2)
    up_rest.start()
    core_dot(3)
    event(1)
    pl.when(col == 0)(lambda: out_copy(True).start())
    pl.when(col == last)(lambda: out_copy(False).start())
    down_dot_partner()
    after_row(0)
    row_copy(1).start()
    core_sum(3)
    up_out.start()
    event(2)
    down_dot_own()
    down_sum()
    down_out.start()

    for part in range(2):
        sum_ref[part] = send_stage[col, part].astype(full)

        @pl.when(col > 0)
        def _():
            rs_wait(col, part)
            sum_ref[part] += arrived[col, part].astype(full)

        @pl.when(col < last)
        def _():
            rs_wait(last + 1, part)
            sum_ref[part] += arrived[last + 1, part].astype(full)

    after_row(1)
    row_copy(2).start()
    after_side(0)
    after_side(1)

    for block in range(last + 1):
        pl.when((block <= col) & (col < last))(lambda: ag_copy(block, True).wait_send())
        pl.when((block >= col) & (col > 0))(lambda: ag_copy(block, False).wait_send())
        for part in range(2):
            pl.when(block > col)(lambda: rs_copy(block, part, True).wait_send())
            pl.when(block < col)(lambda: rs_copy(block, part, False).wait_send())
    for at in range(4, 6):
        core_copy(at).wait_send()
    row_copy(2).wait()
    pl.when(col == 0)(lambda: out_copy(True).wait_send())
    pl.when(col == last)(lambda: out_copy(False).wait_send())
    pl.when(inner)(lambda: out_copy(False).wait_recv())
    for copy in (down_out, up_out, up_rest):
        copy.wait()
    for chunk in range(2):
        remote, local = final_copies(chunk)
        remote.wait()
        local.wait()


def experts_call(own, cot, table, *halves):
    rows, width = own.shape
    blocks, half = cot.shape[0], width // 2
    sides = lax.axis_size("dp").bit_length() - 2
    vmem = pl.BlockSpec(memory_space=pltpu.VMEM)
    anywhere = pl.BlockSpec(memory_space=pl.ANY)
    dma = pltpu.SemaphoreType.DMA
    shape = jax.ShapeDtypeStruct
    return pl.pallas_call(
        experts_kernel,
        in_specs=[vmem] * 3 + [anywhere] * 6,
        out_specs=[vmem, vmem] + [anywhere] * 6,
        out_shape=[
            shape((2, rows, half), full),
            shape((blocks, rows, width), low),
            shape((width, half), low),
            shape((half, half), low),
            shape((half // 2, half), low),
            shape((half // 2, half), low),
            shape((half, width), low),
            shape((rows, width), low),
        ],
        scratch_shapes=[pltpu.VMEM((3, width, width), low)]
        + [pltpu.VMEM((blocks, rows, width), low)] * 4
        + [
            pltpu.VMEM((blocks, 2, rows, half), low),
            pltpu.VMEM((blocks + 1, 2, rows, half), low),
            pltpu.VMEM((4, half, half), low),
            pltpu.VMEM((2, half, half), low),
            dma((6,)),
            dma((6,)),
            pltpu.SemaphoreType.REGULAR((2 + max(sides, 1),)),
            dma((blocks,)),
            dma((blocks,)),
            dma((blocks,)),
            dma((blocks + 1, 2)),
            dma((blocks, 2)),
            dma((6,)),
            dma((6,)),
            dma((3,)),
            dma((3,)),
            dma((2, max(sides, 1))),
            dma((2, max(sides, 1))),
            dma((2, 3)),
            dma((3,)),
            dma((2,)),
        ],
        compiler_params=pltpu.CompilerParams(
            collective_id=1, has_side_effects=True, vmem_limit_bytes=60 * 2**20
        ),
        cost_estimate=pl.CostEstimate(
            flops=9 * 2 * blocks * rows * width * width,
            bytes_accessed=12 * width * width,
            transcendentals=blocks * rows * width,
        ),
    )(own, cot, table, *halves)


def prologue_kernel(
    inputs_ref,
    small_ref,
    theta_ref,
    routes_ref,
    route_gates_ref,
    cot_ref,
    query_hbm,
    keyval_hbm,
    output_hbm,
    gate_hbm,
    up_hbm,
    down_hbm,
    normed_ref,
    scale_ref,
    gains_ref,
    key_ref,
    value_ref,
    cosine_ref,
    sine_ref,
    start_ref,
    attended_ref,
    rot_ref,
    joint_ref,
    head_output_ref,
    middle_ref,
    expert_ref,
    table_ref,
    cot_all_ref,
    gate_all_ref,
    up_all_ref,
    down_all_ref,
    inputs_all,
    inputs_sem,
    small,
    small_sem,
    projected,
    branch_own,
    branch_stage,
    branch_arrived,
    branch_sem,
    pair_sem,
    joint_line,
    joint_load,
    joint_hop,
    joint_row,
    joint_side,
    joint_core,
    output_line,
    output_load,
    output_hop,
    output_row,
    output_side,
    output_core,
    expert_row,
    expert_side,
    expert_core,
    cot_sem,
    cot_recv,
    cot_send,
    *,
    sequences,
):
    row, col, dp = lax.axis_index("row"), lax.axis_index("col"), lax.axis_index("dp")
    cols = lax.axis_size("col")
    last = cols - 1
    core, side, other = dp % 2, (dp // 2) % 2, 1 - row
    quarter = dp % 4
    core_partner, side_partner = dp + 1 - 2 * core, dp + 2 - 4 * side
    tokens, part_width = inputs_ref.shape
    width, rows = 2 * part_width, tokens // 2
    query_block, keyval_block = query_hbm.shape[1], keyval_hbm.shape[1]
    block = query_block + keyval_block
    experts = table_ref.shape[2]

    barrier = pltpu.get_barrier_semaphore()

    def greet(**device):
        pl.semaphore_signal(
            barrier, inc=1, device_id=device, device_id_type=pl.DeviceIdType.MESH
        )

    greet(row=other)
    for apart in range(1, cols):
        greet(col=(col + apart) % cols)
    greet(dp=core_partner)
    greet(dp=side_partner)

    def part_lanes(which):
        return pl.ds(pl.multiple_of(which * part_width, 128), part_width)

    inputs_all[:, part_lanes(row)] = inputs_ref[...]
    small[row] = small_ref[...]
    inputs_copy = remote_copy(
        inputs_ref,
        inputs_all.at[:, part_lanes(row)],
        inputs_sem.at[0],
        inputs_sem.at[1],
        row=other,
    )
    small_copy = remote_copy(
        small.at[row], small.at[row], small_sem.at[0], small_sem.at[1], row=other
    )

    joint_size, output_size = query_hbm.shape[0] // 4, output_hbm.shape[0] // 4

    def joint_region(r0, b, which):
        return joint_ref.at[
            pl.ds(pl.multiple_of(r0 * part_width + which * joint_size, 16), joint_size),
            pl.ds(pl.multiple_of(b * block, 128), block),
        ]

    def output_region(r0, b, which):
        return head_output_ref.at[
            pl.ds(pl.multiple_of(b * query_block + which * output_size, 16), output_size),
            part_lanes(r0),
        ]

    class Gather:
        def __init__(self, line, pieces, load, hop, row_sems, side_sems, core_sems, region):
            self.line, self.region, self.hop, self.row_sems = line, region, hop, row_sems
            self.side_sems, self.core_sems = side_sems, core_sems
            self.loads = [
                pltpu.make_async_copy(source, target, load.at[n])
                for n, (source, target) in enumerate(pieces)
            ]

        def copy(self, at, right):
            return remote_copy(
                self.line.at[at],
                self.line.at[at],
                self.hop.at[at, 1 if right else 0],
                self.hop.at[at, 2],
                col=col + 1 if right else col - 1,
            )

        def row_copy(self, b):
            return remote_copy(
                self.line.at[2 * other + b],
                self.region(row, b, quarter),
                self.row_sems.at[b, 0],
                self.row_sems.at[b, 1],
                row=other,
            )

        def side_copy(self, n):
            there = self.region((row, other)[n // 2], n % 2, quarter)
            return remote_copy(
                there, there, self.side_sems.at[n, 0], self.side_sems.at[n, 1], dp=side_partner
            )

        def core_copies(self, n):
            result = []
            for part in range(2):
                there = self.region((row, other)[n // 2], n % 2, core + 2 * part)
                result.append(
                    remote_copy(
                        there,
                        there,
                        self.core_sems.at[n, 2 * part],
                        self.core_sems.at[n, 2 * part + 1],
                        dp=core_partner,
                    )
                )
            return result

        def use(self, at):
            for b in range(2):

                @pl.when(at == 2 * row + b)
                def _(b=b):
                    there = self.region(row, b, quarter)
                    there[...] = self.line[at]
                    self.side_copy(b).start()

                @pl.when(at == 2 * other + b)
                def _(b=b):
                    self.row_copy(b).start()

        def load(self):
            for copy in self.loads:
                copy.start()

        def first(self):
            for copy in self.loads:
                copy.wait()
            pl.when(col < last)(lambda: self.copy(col, True).start())
            pl.when(col > 0)(lambda: self.copy(col, False).start())
            self.use(col)

        def step(self, apart):
            @pl.when(col - apart >= 0)
            def _():
                self.copy(col - apart, True).wait_recv()
                pl.when(col < last)(lambda: self.copy(col - apart, True).start())
                self.use(col - apart)

            @pl.when(col + apart <= last)
            def _():
                self.copy(col + apart, False).wait_recv()
                pl.when(col > 0)(lambda: self.copy(col + apart, False).start())
                self.use(col + apart)

        def from_row(self):
            for b in range(2):
                self.row_copy(b).wait_recv()
                self.side_copy(2 + b).start()

        def to_core(self):
            for n in range(4):
                self.side_copy(n).wait_recv()
                for copy in self.core_copies(n):
                    copy.start()

        def ready(self):
            for n in range(4):
                for copy in self.core_copies(n):
                    copy.wait_recv()

        def end(self):
            for at in range(cols):
                pl.when((at <= col) & (col < last))(lambda: self.copy(at, True).wait_send())
                pl.when((at >= col) & (col > 0))(lambda: self.copy(at, False).wait_send())
            for b in range(2):
                self.row_copy(b).wait_send()
            for n in range(4):
                self.side_copy(n).wait_send()
                for copy in self.core_copies(n):
                    copy.wait_send()

    first_joint = pl.ds(pl.multiple_of(quarter * joint_size, 16), joint_size)
    first_output = pl.ds(pl.multiple_of(quarter * output_size, 16), output_size)
    joint = Gather(
        joint_line,
        (
            (query_hbm.at[first_joint], joint_line.at[col, :, pl.ds(0, query_block)]),
            (keyval_hbm.at[first_joint], joint_line.at[col, :, pl.ds(query_block, keyval_block)]),
        ),
        joint_load,
        joint_hop,
        joint_row,
        joint_side,
        joint_core,
        joint_region,
    )
    output = Gather(
        output_line,
        ((output_hbm.at[first_output], output_line.at[col]),),
        output_load,
        output_hop,
        output_row,
        output_side,
        output_core,
        output_region,
    )

    def token_rows(which):
        return pl.ds(pl.multiple_of(which * rows, 16), rows)

    cot_row = remote_copy(
        cot_ref.at[token_rows(other)],
        cot_all_ref.at[col, :, part_lanes(row)],
        cot_sem.at[0],
        cot_sem.at[1],
        row=other,
    )

    def cot_copy(block_at, right):
        return remote_copy(
            cot_all_ref.at[block_at],
            cot_all_ref.at[block_at],
            cot_send.at[block_at, 1 if right else 0],
            cot_recv.at[block_at],
            col=col + 1 if right else col - 1,
        )

    def cot_first():
        cot_row.wait_recv()
        pl.when(col < last)(lambda: cot_copy(col, True).start())
        pl.when(col > 0)(lambda: cot_copy(col, False).start())

    def cot_pass(apart):
        @pl.when(col - apart >= 0)
        def _():
            cot_copy(col - apart, True).wait_recv()
            pl.when(col < last)(lambda: cot_copy(col - apart, True).start())

        @pl.when(col + apart <= last)
        def _():
            cot_copy(col + apart, False).wait_recv()
            pl.when(col > 0)(lambda: cot_copy(col + apart, False).start())

    joint.load()
    output.load()
    pl.semaphore_wait(barrier, cols + 2)
    joint.first()
    small_copy.start()
    inputs_copy.start()
    cot_row.start()

    expert_size = down_hbm.shape[0] // 4
    weights = (gate_hbm, up_hbm, down_hbm)
    totals = (gate_all_ref, up_all_ref, down_all_ref)

    def expert_region(which, of_quarter):
        first = pl.multiple_of(of_quarter * expert_size, 16)
        return totals[which].at[pl.ds(first, expert_size)]

    def expert_row_copy(which):
        first = pl.multiple_of(quarter * expert_size, 16)
        return remote_copy(
            weights[which].at[pl.ds(first, expert_size)],
            expert_region(which, quarter),
            expert_row.at[which, 0],
            expert_row.at[which, 1],
            row=other,
        )

    def expert_side_copy(which):
        there = expert_region(which, quarter)
        return remote_copy(
            there, there, expert_side.at[which, 0], expert_side.at[which, 1], dp=side_partner
        )

    def expert_core_copies(which):
        result = []
        for n in range(2):
            there = expert_region(which, core + 2 * n)
            result.append(
                remote_copy(
                    there,
                    there,
                    expert_core.at[which, 2 * n],
                    expert_core.at[which, 2 * n + 1],
                    dp=core_partner,
                )
            )
        return result

    def expert_after_row(which):
        expert_row_copy(which).wait_recv()
        expert_side_copy(which).start()

    def expert_after_side(which):
        expert_side_copy(which).wait_recv()
        for copy in expert_core_copies(which):
            copy.start()

    cot_all_ref[col, :, part_lanes(row)] = cot_ref[token_rows(row), :]

    for at in range(cols):
        place = pl.ds(pl.multiple_of(at * tokens + row * rows, 128), rows)
        chosen, gates = routes_ref[:, place], route_gates_ref[:, place]
        expert = lax.broadcasted_iota(jnp.int32, (experts, rows), 0)
        table = jnp.zeros((experts, rows), full)
        for k in range(chosen.shape[0]):
            table += jnp.where(chosen[k : k + 1, :] == expert, gates[k : k + 1, :], 0.0)
        table_ref[at] = jnp.transpose(table)

    joint.step(1)
    joint.step(2)
    joint.step(3)
    output.first()
    joint.from_row()
    cot_first()

    small_copy.wait_recv()
    gains_ref[:, :part_width] = small[0, 0:2, :]
    gains_ref[:, part_width:] = small[1, 0:2, :]
    half = col // 2
    lens = small[half, 2:3, :]
    odd = (col % 2).astype(full)
    place = lax.broadcasted_iota(jnp.int32, (tokens, 1), 0).astype(full) + odd * tokens
    begin = jnp.zeros((tokens, 1), full)
    total = lens[:, 0:1]
    for n in range(1, sequences):
        begin = jnp.where(place >= total, total, begin)
        total = total + lens[:, n : n + 1]
    start_ref[...] = begin + (1.0 - odd) * tokens
    angles = (place - begin) * theta_ref[...]
    cosine_ref[...] = jnp.cos(angles)
    sine = jnp.sin(angles)
    lane = lax.broadcasted_iota(jnp.int32, sine.shape, 1)
    sine_ref[...] = jnp.where(lane < head_dim // 2, -sine, sine)

    output.step(1)
    inputs_copy.wait_recv()
    expert_row_copy(0).start()

    piece = 64

    def norm_piece(at, carry):
        here = pl.ds(pl.multiple_of(at * piece, piece), piece)
        values = inputs_all[here, :].astype(full)
        scale = lax.rsqrt(jnp.mean(values * values, axis=1, keepdims=True) + epsilon)
        scale_ref[here, :] = scale
        for which in range(2):
            lanes = slice(which * part_width, (which + 1) * part_width)
            normed_ref[here, lanes] = (values[:, lanes] * scale * small[which, 0:1, :]).astype(low)
        return carry

    lax.fori_loop(0, tokens // piece, norm_piece, 0)
    output.step(2)
    joint.to_core()
    output.step(3)
    joint.ready()

    projected[...] = dot(normed_ref[...], joint_ref[...])
    own = slice(tokens, 2 * tokens)
    key = projected[:, query_block : query_block + head_dim]
    key_ref[own, :] = (
        key * cosine_ref[...] + pltpu.roll(key, head_dim // 2, 1) * sine_ref[...]
    ).astype(low)
    value_ref[own, :] = projected[:, block + query_block : block + query_block + head_dim].astype(low)

    def pair_copies():
        return [
            remote_copy(
                ref.at[pl.ds(tokens, tokens)],
                ref.at[pl.ds(0, tokens)],
                pair_sem.at[n, 0],
                pair_sem.at[n, 1],
                col=col + 1 - 2 * (col % 2),
            )
            for n, ref in enumerate((key_ref, value_ref))
        ]

    @pl.when(col % 2 == 0)
    def _():
        for copy in pair_copies():
            copy.start()
        key_ref[:tokens, :] = jnp.zeros((tokens, head_dim), low)
        value_ref[:tokens, :] = jnp.zeros((tokens, head_dim), low)

    expert_row_copy(1).start()
    output.from_row()
    cot_pass(1)
    output.to_core()

    @pl.when(col % 2 == 1)
    def _():
        for copy in pair_copies():
            copy.wait_recv()

    heads = 2 * query_block // head_dim
    per_block = heads // 2
    tile = tokens // 2
    window = key_ref.shape[0] - tile

    def head_step(head, carry):
        here = pl.ds(pl.multiple_of(head * head_dim, head_dim), head_dim)
        there = pl.ds(
            pl.multiple_of((head + head // per_block) * head_dim, head_dim), head_dim
        )
        pre = projected[:, there]
        rot = (pre * cosine_ref[...] + pltpu.roll(pre, head_dim // 2, 1) * sine_ref[...]).astype(low)
        rot_ref[:, here] = rot
        for at in range(tokens // tile):
            first = at * tile
            keys = key_ref[first : first + window, :]
            values = value_ref[first : first + window, :]
            scores = dot(rot[first : first + tile], keys, 1, 1) * head_dim ** (-0.5)
            key_place = lax.broadcasted_iota(jnp.int32, scores.shape, 1) + first
            query_place = lax.broadcasted_iota(jnp.int32, scores.shape, 0) + (first + tokens)
            allowed = (key_place <= query_place) & (
                key_place.astype(full) >= start_ref[first : first + tile, :]
            )
            scores = jnp.where(allowed, scores, -1e30)
            exponent = jnp.exp(scores - jnp.max(scores, axis=1, keepdims=True))
            weights = exponent / jnp.sum(exponent, axis=1, keepdims=True)
            attended_ref[first : first + tile, here] = dot(weights.astype(low), values).astype(low)
        return carry

    lax.fori_loop(0, heads, head_step, 0)

    expert_after_row(0)
    output.ready()

    def branch_copy(part):
        return remote_copy(
            branch_stage.at[part],
            branch_arrived.at[part],
            branch_sem.at[part, 0],
            branch_sem.at[part, 1],
            row=other,
        )

    theirs = attended_ref[token_rows(other), :]
    for part in range(2):
        lanes = slice(part * part_width, (part + 1) * part_width)
        branch_stage[part] = dot(theirs, head_output_ref[:, lanes]).astype(low)
        branch_copy(part).start()
    expert_row_copy(2).start()
    cot_pass(2)
    mine = attended_ref[token_rows(row), :]
    branch_own[...] = dot(mine, head_output_ref[...])
    expert_after_row(1)
    expert_after_side(0)
    for part in range(2):
        lanes = slice(part * part_width, (part + 1) * part_width)
        branch_copy(part).wait_recv()
        middle_ref[:, lanes] = (
            inputs_all[token_rows(row), lanes].astype(full)
            + branch_own[:, lanes]
            + branch_arrived[part].astype(full)
        )

    def second_piece(at, carry):
        here = pl.ds(pl.multiple_of(at * piece, piece), piece)
        values = middle_ref[here, :]
        scale = lax.rsqrt(jnp.mean(values * values, axis=1, keepdims=True) + epsilon)
        expert_ref[here, :] = (values * scale * gains_ref[1:2, :]).astype(low)
        return carry

    lax.fori_loop(0, rows // piece, second_piece, 0)
    expert_after_side(1)
    cot_pass(3)

    inputs_copy.wait_send()
    small_copy.wait_send()
    joint.end()
    output.end()
    for which in range(3):
        expert_row_copy(which).wait_send()
        if which == 2:
            expert_row_copy(which).wait_recv()
            continue
        expert_side_copy(which).wait_send()
        for copy in expert_core_copies(which):
            copy.wait()
    cot_row.wait_send()
    for at in range(cols):
        pl.when((at <= col) & (col < last))(lambda: cot_copy(at, True).wait_send())
        pl.when((at >= col) & (col > 0))(lambda: cot_copy(at, False).wait_send())

    @pl.when(col % 2 == 0)
    def _():
        for copy in pair_copies():
            copy.wait_send()

    for part in range(2):
        branch_copy(part).wait_send()


def prologue_call(
    inputs, small, theta, routes, route_gates, cotangent, query_weight, key_value_matrix,
    output_weight, gate_flat, up_flat, down_flat, sequences, experts,
):
    tokens, part_width = inputs.shape
    cols = lax.axis_size("col")
    width, rows = 2 * part_width, tokens // 2
    query_block, keyval_block = query_weight.shape[1], key_value_matrix.shape[1]
    block = query_block + keyval_block
    hidden = down_flat.shape[0]
    vmem = pl.BlockSpec(memory_space=pltpu.VMEM)
    anywhere = pl.BlockSpec(memory_space=pl.ANY)
    dma = pltpu.SemaphoreType.DMA
    shape = jax.ShapeDtypeStruct
    return pl.pallas_call(
        functools.partial(prologue_kernel, sequences=sequences),
        in_specs=[vmem] * 6 + [anywhere] * 6,
        out_specs=[vmem] * 16 + [anywhere] * 3,
        out_shape=[
            shape((tokens, width), low),
            shape((tokens, 1), full),
            shape((2, width), full),
            shape((2 * tokens, head_dim), low),
            shape((2 * tokens, head_dim), low),
            shape((tokens, head_dim), full),
            shape((tokens, head_dim), full),
            shape((tokens, 1), full),
            shape((tokens, 2 * query_block), low),
            shape((tokens, 2 * query_block), low),
            shape((width, 2 * block), low),
            shape((2 * query_block, width), low),
            shape((rows, width), full),
            shape((rows, width), low),
            shape((cols, rows, experts), full),
            shape((cols, rows, width), low),
            shape((hidden, part_width), low),
            shape((hidden, part_width), low),
            shape((hidden, part_width), low),
        ],
        scratch_shapes=[
            pltpu.VMEM((tokens, width), low),
            dma((2,)),
            pltpu.VMEM((2,) + small.shape, full),
            dma((2,)),
            pltpu.VMEM((tokens, 2 * block), full),
            pltpu.VMEM((rows, width), full),
            pltpu.VMEM((2, rows, part_width), low),
            pltpu.VMEM((2, rows, part_width), low),
            dma((2, 2)),
            dma((2, 2)),
            pltpu.VMEM((cols, part_width // 4, block), low),
            dma((2,)),
            dma((cols, 3)),
            dma((2, 2)),
            dma((4, 2)),
            dma((4, 4)),
            pltpu.VMEM((cols, query_block // 4, part_width), low),
            dma((1,)),
            dma((cols, 3)),
            dma((2, 2)),
            dma((4, 2)),
            dma((4, 4)),
            dma((3, 2)),
            dma((3, 2)),
            dma((3, 4)),
            dma((2,)),
            dma((cols,)),
            dma((cols, 2)),
        ],
        compiler_params=pltpu.CompilerParams(
            collective_id=3, has_side_effects=True, vmem_limit_bytes=60 * 2**20
        ),
        cost_estimate=pl.CostEstimate(
            flops=5 * 10**9, bytes_accessed=30 * 10**6, transcendentals=3 * 10**6
        ),
    )(
        inputs, small, theta, routes, route_gates, cotangent, query_weight, key_value_matrix,
        output_weight, gate_flat, up_flat, down_flat,
    )


def finish_kernel(
    middle_ref,
    gains_ref,
    scale_ref,
    start_ref,
    sum_hbm,
    inputs_hbm,
    attended_hbm,
    rot_hbm,
    key_hbm,
    value_hbm,
    cosine_hbm,
    sine_hbm,
    head_output_hbm,
    joint_hbm,
    normed_hbm,
    cot_all_hbm,
    out_part_hbm,
    up_own_hbm,
    up_row_hbm,
    up_other_hbm,
    down_half_hbm,
    out_first_hbm,
    outputs_ref,
    input_grad_ref,
    gain_sums_ref,
    output_total_ref,
    query_total_ref,
    keyval_total_ref,
    up_total_ref,
    down_total_ref,
    further,
    work,
    cot_ref,
    inputs_ref,
    attended_ref,
    rot_ref,
    key_ref,
    value_ref,
    cosine_ref,
    sine_ref,
    head_output_ref,
    joint_ref,
    normed_ref,
    loads,
    branch,
    branch_sem,
    out_stack,
    out_arrived,
    out_send,
    out_recv,
    own_out_sem,
    grad_heads,
    joint_grad,
    key_grad,
    value_grad,
    pair_stage,
    pair_arrived,
    pair_sem,
    normed_arrived,
    normed_sem,
    inner_stage,
    inner_arrived,
    inner_sem,
    sums,
    sums_arrived,
    sums_sem,
    item_mine,
    item_other,
    item_side,
    item_row,
    item_last,
    item_sem,
    item_load_sem,
    wo_parts,
    wo_core,
    wo_row,
    wo_stack,
    wo_arrived,
    wo_side,
    wo_sem,
    wo_send,
    wo_recv,
    wq_parts,
    wq_core,
    wq_row,
    wq_stack,
    wq_arrived,
    wq_side,
    wq_sem,
    wq_side_sem,
    wq_send,
    wq_recv,
    wk_parts,
    wk_core,
    wk_row,
    wk_stack,
    wk_arrived,
    wk_side,
    wk_sem,
    wk_send,
    wk_recv,
):
    row, col, dp = lax.axis_index("row"), lax.axis_index("col"), lax.axis_index("dp")
    cols, dps = lax.axis_size("col"), lax.axis_size("dp")
    core, side, other = dp % 2, (dp // 2) % 2, 1 - row
    core_partner = dp + 1 - 2 * core
    bits = list(range(1, dps.bit_length() - 1))
    sides = len(bits)

    def across(bit):
        on = (dp // (1 << bit)) % 2
        return dp + (1 << bit) * (1 - 2 * on)

    rows, width = middle_ref.shape
    tokens, part_width = inputs_ref.shape
    heads = attended_ref.shape[1] // head_dim
    per_block = heads // 2
    query_lanes, key_lanes = query_total_ref.shape[1], keyval_total_ref.shape[1]
    block_lanes = query_lanes + key_lanes

    def part_lanes(which):
        return pl.ds(pl.multiple_of(which * part_width, 128), part_width)

    size = item_mine.shape[1]
    items = item_mine.shape[0]
    load_pairs = [
        (sum_hbm, work),
        (cot_all_hbm.at[col], cot_ref),
        (out_part_hbm, out_stack),
        (head_output_hbm, head_output_ref),
        (attended_hbm, attended_ref),
        (rot_hbm, rot_ref),
        (key_hbm, key_ref),
        (value_hbm, value_ref),
        (cosine_hbm, cosine_ref),
        (sine_hbm, sine_ref),
        (joint_hbm, joint_ref),
        (normed_hbm, normed_ref),
        (inputs_hbm, inputs_ref),
    ]
    load = [
        pltpu.make_async_copy(source, target, loads.at[n])
        for n, (source, target) in enumerate(load_pairs)
    ]

    def item_loads(at):
        chunk = at % 2
        place = pl.ds(chunk * size, size)
        if at < 2:
            sources = (up_own_hbm.at[place], (up_row_hbm, up_other_hbm)[chunk])
        else:
            sources = [down_half_hbm.at[place, part_lanes(which)] for which in (row, other)]
        return [
            pltpu.make_async_copy(source, target.at[at], item_load_sem.at[at, number])
            for number, (source, target) in enumerate(zip(sources, (item_mine, item_other)))
        ]

    inner_col = (col > 0) & (col < cols - 1)
    first_load = pltpu.make_async_copy(
        out_first_hbm, out_arrived.at[(cols - 1) * (2 - col) % cols], loads.at[13]
    )
    for copy in load[:3]:
        copy.start()
    pl.when(inner_col)(lambda: first_load.start())
    for copy in item_loads(1) + load[3:]:
        copy.start()
    for at in (2, 3, 0):
        for copy in item_loads(at):
            copy.start()

    barrier = pltpu.get_barrier_semaphore()

    def greet(**device):
        pl.semaphore_signal(
            barrier, inc=1, device_id=device, device_id_type=pl.DeviceIdType.MESH
        )

    plane = [
        dict(row=(row + there // cols) % 2, col=(col + there % cols) % cols)
        for there in range(1, 2 * cols)
    ]
    copies = [dict(dp=(dp + apart) % dps) for apart in range(1, dps)]
    for device in plane + copies:
        greet(**device)

    outs = ColSum(out_stack, out_arrived, out_send, out_recv, col, cols, range(cols))
    load[2].wait()
    pl.when(inner_col)(lambda: first_load.wait())
    pl.semaphore_wait(barrier, len(plane) + len(copies))
    outs.step(2, placed=True)

    for copy in load[:2]:
        copy.wait()
    piece = 64
    halves = [slice(h * part_width, (h + 1) * part_width) for h in range(2)]

    def norm_piece(at, mixer_sum):
        place = pl.ds(pl.multiple_of(at * piece, piece), piece)
        middle = middle_ref[place, :]
        second = jnp.concatenate([work[h, place, :] for h in range(2)], axis=1)
        scale = lax.rsqrt(jnp.mean(middle * middle, axis=1, keepdims=True) + epsilon)
        weighted = gains_ref[1:2, :] * second
        inner = jnp.sum(weighted * middle, axis=1, keepdims=True)
        grad = (
            cot_ref[place, :].astype(full)
            + scale * weighted
            - middle * (scale * scale * scale) * (inner / width)
        )
        branch[row, place, :] = grad.astype(low)
        return mixer_sum + jnp.sum(second * middle * scale, axis=0, keepdims=True)

    mixer_sum = lax.fori_loop(0, rows // piece, norm_piece, jnp.zeros((1, width), full))
    quarter_lanes = sums.shape[2]
    parts = width // quarter_lanes
    for n in range(parts):
        sums[0, parts + n : parts + n + 1, :] = mixer_sum[
            :, n * quarter_lanes : (n + 1) * quarter_lanes
        ]
    branch_copy = remote_copy(
        branch.at[row], branch.at[row], branch_sem.at[0], branch_sem.at[1], row=other
    )
    branch_copy.start()

    half_size = size // 2

    def side_rows(which):
        return pl.ds(pl.multiple_of(which * half_size, 16), half_size)

    def item_first_copies(at):
        if at == 0:
            pairs = [(item_mine.at[0], item_side.at[0])]
        else:
            there = side_rows(1 - side)
            pairs = [
                (item_mine.at[at, there], item_side.at[at, side_rows(0)]),
                (item_other.at[at, there], item_side.at[at, side_rows(1)]),
            ]
        return [
            remote_copy(
                source, target, item_sem.at[at, 2 * n], item_sem.at[at, 2 * n + 1], dp=across(1)
            )
            for n, (source, target) in enumerate(pairs)
        ]

    def item_start(at):
        for copy in item_loads(at):
            copy.wait()
        if at == 0:
            item_mine[0] = add_low(item_mine[0], item_other[0])
        for copy in item_first_copies(at):
            copy.start()

    def item_row_copy(at):
        return remote_copy(
            item_other.at[at, side_rows(side)],
            item_row.at[at],
            item_sem.at[at, 4],
            item_sem.at[at, 5],
            row=other,
        )

    def item_to_row(at):
        for copy in item_first_copies(at):
            copy.wait_recv()
        here = side_rows(side)
        item_other[at, here] = add_low(item_other[at, here], item_side[at, side_rows(1)])
        item_row_copy(at).start()
        item_mine[at, here] = add_low(item_mine[at, here], item_side[at, side_rows(0)])

    def item_extent(at):
        return pl.ds(0, size) if at == 0 else side_rows(side)

    def item_further_copy(at, number):
        extent = pl.ds(0, size if at == 0 else half_size)
        return remote_copy(
            item_mine.at[at, item_extent(at)],
            further.at[at, number - 1, extent],
            item_sem.at[at, 4 + 2 * number],
            item_sem.at[at, 5 + 2 * number],
            dp=across(bits[number]),
        )

    def item_further(at):
        extent = pl.ds(0, size if at == 0 else half_size)
        for number in range(1, sides):
            copy = item_further_copy(at, number)
            copy.start()
            copy.wait()
            landed = pltpu.make_async_copy(
                further.at[at, number - 1, extent],
                item_side.at[at, extent],
                item_load_sem.at[at, 0],
            )
            landed.start()
            landed.wait()
            here = item_extent(at)
            item_mine[at, here] = add_low(item_mine[at, here], item_side[at, extent])

    def item_last_copy(at):
        return remote_copy(
            item_mine.at[at, side_rows(side)],
            item_last.at[at],
            item_sem.at[at, 4 + 2 * sides],
            item_sem.at[at, 5 + 2 * sides],
            dp=across(1),
        )

    def item_after_row(at):
        item_row_copy(at).wait_recv()
        here = side_rows(side)
        for copy in item_first_copies(at):
            copy.wait_send()
        item_mine[at, here] = add_low(item_mine[at, here], item_row[at])
        item_further(at)
        item_last_copy(at).start()

    def item_core_copies(at):
        which, chunk = at // 2, at % 2
        total = (up_total_ref, down_total_ref)[which]
        first = core * part_width + chunk * size
        if at == 0:
            pieces = [(item_mine.at[0], pl.ds(pl.multiple_of(first, 16), size))]
        else:
            pieces = [
                (source, pl.ds(pl.multiple_of(first + of_side * half_size, 16), half_size))
                for source, of_side in (
                    (item_mine.at[at, side_rows(side)], side),
                    (item_last.at[at], 1 - side),
                )
            ]
        result = []
        for n, (source, place) in enumerate(pieces):
            base = 6 + 2 * sides + 3 * n
            result.append(
                remote_copy(
                    source,
                    total.at[place],
                    item_sem.at[at, base],
                    item_sem.at[at, base + 1],
                    dp=core_partner,
                )
            )
            result.append(
                pltpu.make_async_copy(source, total.at[place], item_sem.at[at, base + 2])
            )
        return result

    def item_finish(at):
        if at == 0:
            for copy in item_first_copies(0):
                copy.wait()
            item_mine[0] = add_low(item_mine[0], item_side[0])
            item_further(0)
        else:
            item_last_copy(at).wait_recv()
        for copy in item_core_copies(at):
            copy.start()

    def item_end(at):
        if at > 0:
            item_row_copy(at).wait_send()
            item_last_copy(at).wait_send()
        for copy in item_core_copies(at):
            copy.wait()

    item_start(1)
    for copy in load[3:]:
        copy.wait()

    branch_copy.wait_recv()
    item_to_row(1)
    item_start(0)
    outs.step(3)
    branch_all = branch[...].reshape(tokens, width)
    half_lanes = heads * head_dim // 2
    for part in range(2):
        lanes = slice(part * half_lanes, (part + 1) * half_lanes)
        grad_heads[:, lanes] = dot(branch_all, head_output_ref[lanes, :], 1, 1).astype(low)

    wo_size = wo_parts.shape[2]
    for b in range(2):
        lanes = slice(b * half_lanes, (b + 1) * half_lanes)
        value = dot(attended_ref[:, lanes], branch_all, 0, 0).astype(low)
        for part in range(2):
            wo_parts[b, part] = value[part * wo_size : (part + 1) * wo_size, :]

    def wo_core_copy(b):
        return remote_copy(
            wo_parts.at[b, 1 - core],
            wo_core.at[b],
            wo_sem.at[0, b],
            wo_sem.at[1, b],
            dp=core_partner,
        )

    for b in range(2):
        wo_core_copy(b).start()

    key_grad[...] = jnp.zeros_like(key_grad)
    value_grad[...] = jnp.zeros_like(value_grad)
    tile = tokens // 2
    window = key_ref.shape[0] - tile

    def head_step(head, carry):
        here = pl.ds(pl.multiple_of(head * head_dim, head_dim), head_dim)
        there = pl.ds(
            pl.multiple_of((head + head // per_block) * head_dim, head_dim), head_dim
        )
        for at in range(tokens // tile):
            first = at * tile
            rot = rot_ref[first : first + tile, here]
            grad = grad_heads[first : first + tile, here]
            keys = key_ref[first : first + window, :]
            values = value_ref[first : first + window, :]
            scores = dot(rot, keys, 1, 1) * head_dim ** (-0.5)
            place = lax.broadcasted_iota(jnp.int32, scores.shape, 1) + first
            query = lax.broadcasted_iota(jnp.int32, scores.shape, 0) + (first + tokens)
            allowed = (place <= query) & (place.astype(full) >= start_ref[first : first + tile, :])
            scores = jnp.where(allowed, scores, -1e30)
            exponent = jnp.exp(scores - jnp.max(scores, axis=1, keepdims=True))
            probs = exponent / jnp.sum(exponent, axis=1, keepdims=True)
            prob_grad = dot(grad, values, 1, 1)
            inner = jnp.sum(probs * prob_grad, axis=1, keepdims=True)
            score_grad = (probs * (prob_grad - inner) * head_dim ** (-0.5)).astype(low)
            rot_grad = dot(score_grad, keys)
            joint_grad[first : first + tile, there] = (
                rot_grad * cosine_ref[first : first + tile, :]
                - pltpu.roll(rot_grad, head_dim // 2, 1) * sine_ref[first : first + tile, :]
            ).astype(low)
            key_grad[first : first + window, :] += dot(score_grad, rot, 0, 0)
            value_grad[first : first + window, :] += dot(probs.astype(low), grad, 0, 0)
        return carry

    wa_size = part_width // 2
    chunk_rows = wa_size // 2

    class Lanes:
        def __init__(self, parts, core_room, row_room, sems, stretches, chunks):
            self.parts, self.core_room, self.row_room, self.sems = parts, core_room, row_room, sems
            self.stretches, self.chunks = stretches, chunks

        def core_copy(self, r0):
            return remote_copy(
                self.parts.at[r0, 1 - core],
                self.core_room.at[r0],
                self.sems.at[0, r0],
                self.sems.at[1, r0],
                dp=core_partner,
            )

        def dot(self, r0, which):
            first = pl.multiple_of(r0 * part_width + which * wa_size, 128)
            left = normed_ref[:, pl.ds(first, wa_size)]
            right = [joint_grad[:, lanes] for lanes in self.stretches]
            right = right[0] if len(right) == 1 else jnp.concatenate(right, axis=1)
            self.parts[r0, which] = dot(left, right, 0, 0).astype(low)

        def first(self):
            for r0 in (other, row):
                self.dot(r0, 1 - core)
                self.core_copy(r0).start()
            for r0 in (other, row):
                self.dot(r0, core)

        def row_copy(self, chunk):
            count = wa_size // self.chunks
            return remote_copy(
                self.parts.at[other, core, pl.ds(chunk * count, count)],
                self.row_room.at[chunk],
                self.sems.at[2, chunk],
                self.sems.at[3, chunk],
                row=other,
            )

        def to_row(self):
            self.core_copy(other).wait_recv()
            self.parts[other, core] = add_low(self.parts[other, core], self.core_room[other])
            for chunk in range(self.chunks):
                self.row_copy(chunk).start()
            self.core_copy(row).wait_recv()
            self.parts[row, core] = add_low(self.parts[row, core], self.core_room[row])

        def end(self):
            for r0 in range(2):
                self.core_copy(r0).wait_send()
            for chunk in range(self.chunks):
                self.row_copy(chunk).wait_send()

    stretches = [
        slice(b * block_lanes, b * block_lanes + query_lanes) for b in range(2)
    ]
    key_stretch = slice(query_lanes, block_lanes)
    value_stretch = slice(block_lanes + query_lanes, 2 * block_lanes)
    wq = [
        Lanes(
            wq_parts.at[b], wq_core.at[b], wq_row.at[b], wq_sem.at[b], [stretches[b]], 2
        )
        for b in range(2)
    ]
    wk = Lanes(wk_parts, wk_core, wk_row, wk_sem, [key_stretch, value_stretch], 1)

    def wo_row_copy(b):
        return remote_copy(
            wo_parts.at[b, core, :, part_lanes(other)],
            wo_row.at[b],
            wo_sem.at[2, b],
            wo_sem.at[3, b],
            row=other,
        )

    lax.fori_loop(0, 1, head_step, 0)
    for b in range(2):
        wo_core_copy(b).wait_recv()
        wo_parts[b, core] = add_low(wo_parts[b, core], wo_core[b])
        wo_row_copy(b).start()
    lax.fori_loop(1, per_block, head_step, 0)
    item_start(2)
    wq[0].first()
    lax.fori_loop(per_block, per_block + 1, head_step, 0)
    wq[0].to_row()
    lax.fori_loop(per_block + 1, heads, head_step, 0)
    pair_stage[:, :head_dim] = key_grad[:tokens, :].astype(low)
    pair_stage[:, head_dim:] = value_grad[:tokens, :].astype(low)
    odd = col % 2 == 1

    def pair_copy():
        return remote_copy(
            pair_stage, pair_arrived, pair_sem.at[0], pair_sem.at[1], col=col + 1 - 2 * (col % 2)
        )

    pl.when(odd)(lambda: pair_copy().start())
    wq[1].first()
    item_start(3)

    def over_col(lanes, stacks, arrived, send, recv, chunk, blocks):
        return ColSum(
            stacks.at[chunk], arrived.at[chunk], send.at[chunk], recv.at[chunk], col, cols, blocks
        )

    wq_total = [
        [
            over_col(
                wq[b], wq_stack.at[b], wq_arrived.at[b], wq_send.at[b], wq_recv.at[b], c, (b, 2 + b)
            )
            for c in range(2)
        ]
        for b in range(2)
    ]

    def wq_to_col(b):
        for chunk in range(2):
            wq[b].row_copy(chunk).wait_recv()
            place = pl.ds(chunk * chunk_rows, chunk_rows)
            wq_stack[b, chunk, row] = wq_parts[b, row, core, place]
            wq_stack[b, chunk, other] = wq_row[b, chunk]
            wq_total[b][chunk].step(1)

    def wq_step(b, number):
        for chunk in range(2):
            wq_total[b][chunk].step(number)

    wq[1].to_row()
    item_finish(0)
    wo_total = ColSum(wo_stack, wo_arrived, wo_send, wo_recv, col, cols, range(cols))
    for b in range(2):
        wo_row_copy(b).wait_recv()
        wo_stack[2 * row + b] = wo_parts[b, core, :, part_lanes(row)]
        wo_stack[2 * other + b] = wo_row[b]
    wo_total.step(1)
    wq_to_col(0)

    @pl.when(jnp.logical_not(odd))
    def _():
        pair_copy().wait_recv()
        key_grad[tokens:, :] += pair_arrived[:, :head_dim].astype(full)
        value_grad[tokens:, :] += pair_arrived[:, head_dim:].astype(full)

    key_total = key_grad[tokens:, :]
    joint_grad[:, key_stretch] = (
        key_total * cosine_ref[...] - pltpu.roll(key_total, head_dim // 2, 1) * sine_ref[...]
    ).astype(low)
    joint_grad[:, value_stretch] = value_grad[tokens:, :].astype(low)
    wk.first()

    normed_own = work

    def normed_dot(which):
        return dot(joint_grad[...], joint_ref[part_lanes(which), :], 1, 1)

    def normed_sums(which, value):
        product = value * normed_ref[:, part_lanes(which)].astype(full)
        gain = gains_ref[0:1, part_lanes(which)]
        total = jnp.sum(product, axis=0, keepdims=True) / gain
        for n in range(parts // 2):
            sums[0, pl.ds(which * (parts // 2) + n, 1), :] = total[
                :, n * quarter_lanes : (n + 1) * quarter_lanes
            ]
        return jnp.sum(product, axis=1, keepdims=True)

    wk.to_row()
    item_to_row(2)
    value = normed_dot(other)
    grad_heads[...] = value.astype(low)
    normed_copy = remote_copy(
        grad_heads, normed_arrived, normed_sem.at[0], normed_sem.at[1], row=other
    )
    inner = normed_sums(other, value)
    value = normed_dot(row)
    inner += normed_sums(row, value)
    for h in range(2):
        normed_own[h] = value[h * rows : (h + 1) * rows]
    inner_stage[...] = jnp.transpose(jnp.broadcast_to(inner, (tokens, head_dim)))[:8, :]
    inner_copy = remote_copy(
        inner_stage, inner_arrived, inner_sem.at[0], inner_sem.at[1], row=other
    )
    inner_copy.start()

    def sums_copies(stage):
        base = 0 if stage == 0 else len(plane)
        return [
            remote_copy(
                sums.at[stage],
                sums_arrived.at[base + n],
                sums_sem.at[base + n, 0],
                sums_sem.at[base + n, 1],
                **device,
            )
            for n, device in enumerate((plane, copies)[stage])
        ]

    def sums_start(stage):
        for copy in sums_copies(stage):
            copy.start()

    def sums_finish(stage):
        base = 0 if stage == 0 else len(plane)
        total = sums[stage]
        for n, copy in enumerate(sums_copies(stage)):
            copy.wait_recv()
            total += sums_arrived[base + n]
        sums[stage + 1] = total

    sums_start(0)
    wq_to_col(1)
    wq_step(0, 2)
    wo_total.step(2)
    wk_total = ColSum(wk_stack, wk_arrived, wk_send, wk_recv, col, cols, range(cols))
    wk.row_copy(0).wait_recv()
    for b in range(2):
        lanes = slice(b * key_lanes, (b + 1) * key_lanes)
        wk_stack[2 * row + b] = wk_parts[row, core, :, lanes]
        wk_stack[2 * other + b] = wk_row[0, :, lanes]
    wk_total.step(1)
    item_to_row(3)
    wq_step(1, 2)
    wq_step(0, 3)
    wk_total.step(2)
    normed_copy.start()
    sums_finish(0)
    sums_start(1)
    wo_total.step(3)
    wq_step(1, 3)
    wk_total.step(3)
    item_after_row(1)
    item_after_row(2)

    class Owned:
        def __init__(self, side_room, sems, targets):
            self.room, self.sems, self.targets = side_room, sems, targets

        def copy(self, number):
            return remote_copy(
                self.room.at[number % 2],
                self.room.at[2 + number],
                self.sems.at[2 * number],
                self.sems.at[2 * number + 1],
                dp=across(bits[number]),
            )

        def start(self, value):
            self.room[0] = value.astype(low)
            if sides:
                self.copy(0).start()

        def core_copies(self):
            result = []
            base, value = 2 * sides, self.room.at[sides % 2]
            return (
                remote_copy(
                    value,
                    self.targets,
                    self.sems.at[base],
                    self.sems.at[base + 1],
                    dp=core_partner,
                ),
                pltpu.make_async_copy(value, self.targets, self.sems.at[base + 2]),
            )

        def finish(self):
            for number in range(sides):
                self.copy(number).wait()
                self.room[1 - number % 2] = add_low(
                    self.room[number % 2], self.room[2 + number]
                )
                if number + 1 < sides:
                    self.copy(number + 1).start()
            for copy in self.core_copies():
                copy.start()

        def end(self):
            for copy in self.core_copies():
                copy.wait()

    def own_place(chunk, count):
        return pl.ds(pl.multiple_of(core * wa_size + chunk * count, 16), count)

    wk_owned = Owned(wk_side, wk_sem.at[4], keyval_total_ref.at[own_place(0, wa_size)])
    wq_owned = [
        Owned(wq_side.at[c], wq_side_sem.at[c], query_total_ref.at[own_place(c, chunk_rows)])
        for c in range(2)
    ]
    wo_owned = Owned(
        wo_side,
        wo_sem.at[4],
        output_total_ref.at[pl.ds(pl.multiple_of(core * wo_size, 16), wo_size)],
    )
    for b in range(2):
        for c in range(2):
            wq_total[b][c].total(wq_owned[c].start)
    wo_total.total(wo_owned.start)
    wk_total.total(wk_owned.start)

    def own_tokens(value):
        out_stack[col] = (middle_ref[...] + value).astype(low)

    outs.total(own_tokens)

    def outputs_copy():
        place = pl.ds(pl.multiple_of(row * rows, rows), rows)
        return remote_copy(
            out_stack.at[col, :, part_lanes(other)],
            outputs_ref.at[place],
            own_out_sem.at[0],
            own_out_sem.at[1],
            row=other,
        )

    outputs_copy().start()
    outputs_ref[pl.ds(pl.multiple_of(row * rows, rows), rows), :] = out_stack[
        col, :, part_lanes(row)
    ]
    item_after_row(3)
    item_finish(1)
    for c in range(2):
        wq_owned[c].finish()
    wk_owned.finish()
    wo_owned.finish()
    item_finish(2)
    sums_finish(1)
    for n in range(parts // 2):
        place = pl.ds(row * (parts // 2) + n, 1)
        lanes = slice(n * quarter_lanes, (n + 1) * quarter_lanes)
        gain_sums_ref[0:1, lanes] = sums[2, place, :]
        place = pl.ds(parts + row * (parts // 2) + n, 1)
        gain_sums_ref[1:2, lanes] = sums[2, place, :]
    item_finish(3)

    normed_copy.wait_recv()
    inner_copy.wait_recv()
    both = inner_stage[...] + inner_arrived[...]
    inner = jnp.transpose(jnp.concatenate([both] * (head_dim // 8), axis=0))[:, 0:1]
    for h in range(2):
        place = slice(h * rows, (h + 1) * rows)
        scale = scale_ref[place, :]
        normed_grad = normed_own[h] + normed_arrived[place, :].astype(full)
        input_grad_ref[place, :] = (
            branch[h, :, part_lanes(row)].astype(full)
            + scale * (gains_ref[0:1, part_lanes(row)] * normed_grad)
            - inputs_ref[place, :].astype(full) * (scale * scale) * (inner[place, :] / width)
        ).astype(low)

    branch_copy.wait_send()
    pl.when(odd)(lambda: pair_copy().wait_send())
    for b in range(2):
        wo_core_copy(b).wait_send()
        wo_row_copy(b).wait_send()
    for lanes in wq + [wk]:
        lanes.end()
    normed_copy.wait_send()
    inner_copy.wait_send()
    outputs_copy().wait()
    for stage in range(2):
        for copy in sums_copies(stage):
            copy.wait_send()
    outs.end(first=False)
    for total in [wo_total, wk_total] + wq_total[0] + wq_total[1]:
        total.end()
    for owned in wq_owned + [wk_owned, wo_owned]:
        owned.end()
    for at in range(items):
        item_end(at)


def finish_call(
    middle, gains, scale, start, sums, inputs, attended, rot, keys, values, cosine, sine,
    head_output, joint_weight, normed, cot_all, out_part, up_own, up_row, up_other, down_half, out_first,
    query_block, both_block,
):
    rows, width = middle.shape
    tokens, part_width = inputs.shape
    cols, dps = lax.axis_size("col"), lax.axis_size("dp")
    sides = dps.bit_length() - 2
    heads_width = attended.shape[1]
    reach = keys.shape[0]
    vmem = pl.BlockSpec(memory_space=pltpu.VMEM)
    anywhere = pl.BlockSpec(memory_space=pl.ANY)
    dma = pltpu.SemaphoreType.DMA
    hidden = 2 * up_own.shape[0]
    size = part_width // 2
    items = 4
    key_block = both_block - query_block
    wo_size, wa_size = query_block // 2, part_width // 2
    chunk = wa_size // 2
    shape = jax.ShapeDtypeStruct
    sums_count = 2 * cols - 1 + dps - 1
    return pl.pallas_call(
        finish_kernel,
        in_specs=[vmem] * 4 + [anywhere] * 18,
        out_specs=[vmem] * 6 + [anywhere] * 3,
        out_shape=[
            shape((tokens, part_width), low),
            shape((tokens, part_width), low),
            shape((2, part_width), full),
            shape((query_block, part_width), low),
            shape((part_width, query_block), low),
            shape((part_width, key_block), low),
            shape((hidden, part_width), low),
            shape((hidden, part_width), low),
            shape((items, max(sides - 1, 1), size, part_width), low),
        ],
        scratch_shapes=[
            pltpu.VMEM((2, rows, part_width), full),
            pltpu.VMEM((rows, width), low),
            pltpu.VMEM((tokens, part_width), low),
            pltpu.VMEM((tokens, heads_width), low),
            pltpu.VMEM((tokens, heads_width), low),
            pltpu.VMEM((reach, head_dim), low),
            pltpu.VMEM((reach, head_dim), low),
            pltpu.VMEM((tokens, head_dim), full),
            pltpu.VMEM((tokens, head_dim), full),
            pltpu.VMEM((heads_width, width), low),
            pltpu.VMEM((width, 2 * both_block), low),
            pltpu.VMEM((tokens, width), low),
            dma((14,)),
            pltpu.VMEM((2, rows, width), low),
            dma((2,)),
            pltpu.VMEM((cols, rows, width), low),
            pltpu.VMEM((cols + 1, rows, width), low),
            dma((cols,)),
            dma((cols + 1,)),
            dma((2,)),
            pltpu.VMEM((tokens, heads_width), low),
            pltpu.VMEM((tokens, 2 * both_block), low),
            pltpu.VMEM((reach, head_dim), full),
            pltpu.VMEM((reach, head_dim), full),
            pltpu.VMEM((tokens, 2 * head_dim), low),
            pltpu.VMEM((tokens, 2 * head_dim), low),
            dma((2,)),
            pltpu.VMEM((tokens, part_width), low),
            dma((2,)),
            pltpu.VMEM((8, tokens), full),
            pltpu.VMEM((8, tokens), full),
            dma((2,)),
            pltpu.VMEM((3, 8, width // 4), full),
            pltpu.VMEM((sums_count, 8, width // 4), full),
            dma((sums_count, 2)),
            pltpu.VMEM((items, size, part_width), low),
            pltpu.VMEM((items, size, part_width), low),
            pltpu.VMEM((items, size, part_width), low),
            pltpu.VMEM((items, size // 2, part_width), low),
            pltpu.VMEM((items, size // 2, part_width), low),
            dma((items, 12 + 2 * sides)),
            dma((items, 2)),
            pltpu.VMEM((2, 2, wo_size, width), low),
            pltpu.VMEM((2, wo_size, width), low),
            pltpu.VMEM((2, wo_size, part_width), low),
            pltpu.VMEM((cols, wo_size, part_width), low),
            pltpu.VMEM((cols + 1, wo_size, part_width), low),
            pltpu.VMEM((2 + sides, wo_size, part_width), low),
            dma((5, 3 + 2 * sides)),
            dma((cols,)),
            dma((cols + 1,)),
            pltpu.VMEM((2, 2, 2, wa_size, query_block), low),
            pltpu.VMEM((2, 2, wa_size, query_block), low),
            pltpu.VMEM((2, 2, chunk, query_block), low),
            pltpu.VMEM((2, 2, 2, chunk, query_block), low),
            pltpu.VMEM((2, 2, 3, chunk, query_block), low),
            pltpu.VMEM((2, 2 + sides, chunk, query_block), low),
            dma((2, 4, 2)),
            dma((2, 3 + 2 * sides)),
            dma((2, 2, 2)),
            dma((2, 2, 3)),
            pltpu.VMEM((2, 2, wa_size, 2 * key_block), low),
            pltpu.VMEM((2, wa_size, 2 * key_block), low),
            pltpu.VMEM((1, wa_size, 2 * key_block), low),
            pltpu.VMEM((cols, wa_size, key_block), low),
            pltpu.VMEM((cols + 1, wa_size, key_block), low),
            pltpu.VMEM((2 + sides, wa_size, key_block), low),
            dma((5, 3 + 2 * sides)),
            dma((cols,)),
            dma((cols + 1,)),
        ],
        compiler_params=pltpu.CompilerParams(
            collective_id=2, has_side_effects=True, vmem_limit_bytes=63 * 2**20
        ),
        cost_estimate=pl.CostEstimate(
            flops=10 * 10**9, bytes_accessed=40 * 10**6, transcendentals=4 * 10**6
        ),
    )(
        middle, gains, scale, start, sums, inputs, attended, rot, keys, values, cosine, sine,
        head_output, joint_weight, normed, cot_all, out_part, up_own, up_row, up_other, down_half, out_first,
    )


def shards(
    inputs,
    norm_gain,
    query_weight,
    key_value_matrix,
    output_weight,
    mixer_gain,
    gate_weight,
    up_weight,
    down_weight,
    lengths,
    routes,
    route_gates,
    cotangent,
):
    row, col = lax.axis_index("row"), lax.axis_index("col")
    part_width = inputs.shape[1]
    experts, _, units = gate_weight.shape
    hidden_width = experts * units
    query_block, keyval_block = query_weight.shape[1], key_value_matrix.shape[1]
    small = jnp.zeros((8, part_width), full)
    small = small.at[0].set(norm_gain).at[1].set(mixer_gain)
    sequences = lengths.shape[1]
    small = small.at[2, :sequences].set(lengths[0].astype(full))
    theta = rope_base ** (-jnp.arange(0, head_dim, 2, dtype=full) / head_dim)
    theta = jnp.concatenate([theta, theta])[None, :]
    gate_flat = gate_weight.swapaxes(1, 2).reshape(hidden_width, part_width)
    up_flat = up_weight.swapaxes(1, 2).reshape(hidden_width, part_width)
    down_flat = down_weight.reshape(hidden_width, part_width)
    (
        normed,
        first_scale,
        gains,
        keys,
        values,
        cosine,
        sine,
        start,
        attended,
        rot,
        joint_weight,
        head_output,
        middle,
        expert_own,
        tables,
        cot_all,
        gate_other,
        up_other_half,
        down_other,
    ) = prologue_call(
        inputs, small, theta, routes.T, route_gates.T, cotangent, query_weight, key_value_matrix,
        output_weight, gate_flat, up_flat, down_flat, sequences, experts,
    )
    second_grad, out_part, gate_total, up_own, up_row, up_other, down_half, out_first = experts_call(
        expert_own, cot_all, tables, gate_flat, gate_other, up_flat, up_other_half, down_flat, down_other
    )

    both_block = query_block + keyval_block
    (
        outputs,
        input_grad,
        gain_sums,
        output_total,
        query_total,
        keyval_total,
        up_total,
        down_total,
        _,
    ) = finish_call(
        middle, gains, first_scale, start, second_grad, inputs, attended, rot, keys, values,
        cosine, sine, head_output, joint_weight, normed, cot_all, out_part, up_own, up_row,
        up_other, down_half, out_first, query_block, both_block,
    )
    norm_total, mixer_total = gain_sums[0], gain_sums[1]

    def by_expert(flat):
        return flat.astype(full).reshape(experts, units, part_width).swapaxes(1, 2)

    gate_total, up_total = by_expert(gate_total), by_expert(up_total)
    down_total = down_total.reshape(experts, units, part_width).astype(full)
    output_total = output_total.astype(full)
    query_total, keyval_total = query_total.astype(full), keyval_total.astype(full)
    return (
        outputs,
        input_grad,
        norm_total,
        query_total,
        keyval_total,
        output_total,
        mixer_total,
        gate_total,
        up_total,
        down_total,
    )


def solution(mesh):
    return jax.shard_map(
        shards,
        mesh=mesh,
        in_specs=(
            P(("dp", "col"), "row"),
            P("row"),
            P("row", "col"),
            P("row", "col"),
            P("col", "row"),
            P("row"),
            P(None, "row", "col"),
            P(None, "row", "col"),
            P(None, "col", "row"),
            P(("dp", "row"), None),
            P("dp", None),
            P("dp", None),
            P(("dp", "col"), "row"),
        ),
        out_specs=(
            P(("dp", "col"), "row"),
            P(("dp", "col"), "row"),
            P("row"),
            P("row", "col"),
            P("row", "col"),
            P("col", "row"),
            P("row"),
            P(None, "row", "col"),
            P(None, "row", "col"),
            P(None, "col", "row"),
        ),
        check_vma=False,
    )
```

time: 450 us -> 414 us (0.920)
  Pallas kernels: 408 us -> 385 us
  local copies, waits for them, and re-layouts: 28 us -> 6.8 us
  other arithmetic: 4.97 us -> 14.8 us
    pallas_call x2, Pallas kernels: 291 us -> 266 us  [the longest x1 135 us: finish_call(): pl.pallas_call(finish_kernel, in_specs=[vmem] * 4 + [anywhere] * 18, out_...]
    unnamed x26 -> x14, local copies, waits for them, and re-layouts: 13.4 us -> 3.63 us
    convert_element_type x2 -> x0, local copies, waits for them, and re-layouts: 7.64 us -> none  [by_expert(): flat.reshape(part_width, experts, units).transpose(1, 0, 2).astype(full)]
    transpose x0 -> x1, other arithmetic: none -> 4.76 us  [by_expert(): return flat.astype(full).reshape(experts, units, part_width).swapaxes(1, 2)]
where the time goes in v5:
time: 414 us; the launch traced here: 408 us
  Pallas kernels  385 us (93%)
  other arithmetic  14.8 us (4%)
  local copies, waits for them, and re-layouts  6.8 us (2%)
    pallas_call x1, Pallas kernels, finish_call(): pl.pallas_call(finish_kernel, in_specs=[vmem] * 4 + [anywhere] * 18, out_...  135 us
    pallas_call x1, Pallas kernels, experts_call(): pl.pallas_call(experts_kernel, in_specs=[vmem] * 3 + [anywhere] * 6, out_...  131 us
    pallas_call x1, Pallas kernels, prologue_call(): pl.pallas_call(functools.partial(prologue_kernel, sequences=sequences), i...  119 us

profile of v5, /device:TPU:17, one launch (start us, length us, event | category | flops | bytes accessed | tf_op | source)
XLA Modules:
  0.0 408.0 jit_solution(15816534180574875360)
XLA Ops:
  0.6 0.7 convert_element_type.21
  1.3 0.6 maximum_bitcast_fusion.theta_ref
  1.9 0.7 reshape.119
  2.6 0.7 reshape.120
  3.3 0.1 scatter.11
  3.4 0.2 scatter.14.small_ref
  3.6 0.0 copy-start.5
  3.6 0.6 copy-done.5
  4.2 119.4 %shard_map.204 = (bf16[512,1536]{1,0:T(8,128)(2,1)}, f32[512,1]{1,0:T(8,128)}, f32[2,1536]{1,0:T(2,128)}, bf16[1024,128]{1,0:T(8,128)(2,1)}, bf16[1024,128]{1,0:...) custom-call(bf16[512,768]{1,0:T(8,128)(2,1)} %inputs_hbm.1, ...), custom_call_target="tpu_custom_call" | custom-call | flops 5000000000 | bytes 30000000 | tf_op jit(solution)/shard_map/pallas_call | solution.py:1152
  123.6 131.5 %shard_map.205 = (f32[2,256,768]{2,1,0:T(8,128)}, bf16[4,256,1536]{2,1,0:T(8,128)(2,1)}, bf16[1536,768]{1,0:T(8,128)(2,1)}, bf16[768,768]{1,0:T(8,128)(2,1)}, bf...) custom-call(bf16[256,1536]{1,0:T(8,128)(2,1)} %get-tuple-element.85.ow, ...), custom_call_target="tpu_custom_call" | custom-call | flops 43486543872 | bytes 28311552 | tf_op jit(solution)/shard_map/pallas_call | solution.py:544
  255.1 134.6 %shard_map.206 = (bf16[512,768]{1,0:T(8,128)(2,1)}, bf16[512,768]{1,0:T(8,128)(2,1)}, f32[2,768]{1,0:T(2,128)}, bf16[384,768]{1,0:T(8,128)(2,1)}, bf16[768,384]{...) custom-call(f32[256,1536]{1,0:T(8,128)} %get-tuple-element.81.middle, ...), custom_call_target="tpu_custom_call" | custom-call | flops 10000000000 | bytes 40000000 | tf_op jit(solution)/shard_map/pallas_call | solution.py:2045
  389.7 0.0 copy-start.2
  389.7 1.5 slice_reduce_fusion
  391.2 1.7 convert_element_type.23
  392.9 2.2 convert_element_type.22
  395.0 2.2 convert_element_type.24
  397.2 0.0 copy-done.2
  397.2 2.8 convert.7
  400.0 0.0 copy-done
  400.0 1.2 copy-done.1
  401.2 4.8 %convert_bitcast_fusion = (f32[8,768,192]{1,2,0:T(8,128)}, f32[8,768,192]{1,2,0:T(8,128)}) fusion(bf16[8,192,768]{2,1,0:T(8,128)(2,1)S(1)} %bitcast.22, bf16[8,192,768]{2,1,0:T(8,128)(2,1)S(1)} %bitcast.21), kind=kLoop, calls=%fused_computation | loop fusion | flops 2359296 | bytes 14155776 | tf_op jit(solution)/shard_map/transpose | solution.py:2220
  406.0 0.0 copy-done.4
  406.0 0.9 copy.27
  406.9 0.9 copy.28
  (7 shorter events, 0.0 us)
Async XLA Ops:
  3.6 0.6 copy-start.5
  389.7 7.5 %copy-start.2 = (bf16[1536,768]{1,0:T(8,128)(2,1)S(1)}, bf16[1536,768]{1,0:T(8,128)(2,1)}, u32[]{:S(2)}) copy-start(bf16[1536,768]{1,0:T(8,128)(2,1)} %get-tuple-element.115) | copy-start | bytes 7077892
  397.2 2.8 copy-start
  397.2 4.1 copy-start.1
  401.2 4.8 %copy-start.4 = (bf16[512,768]{1,0:T(8,128)(2,1)S(1)}, bf16[512,768]{1,0:T(8,128)(2,1)}, u32[]{:S(2)}) copy-start(bf16[512,768]{1,0:T(8,128)(2,1)} %get-tuple-element.130) | copy-start | bytes 2359300
  401.2 5.6 %copy-start.3 = (bf16[512,768]{1,0:T(8,128)(2,1)S(1)}, bf16[512,768]{1,0:T(8,128)(2,1)}, u32[]{:S(2)}) copy-start(bf16[512,768]{1,0:T(8,128)(2,1)} %get-tuple-element.131) | copy-start | bytes 2359300

commit v6 on v5

--- a/solution.py
+++ b/solution.py
@@ -114,7 +114,7 @@
     up_hbm,
     up_other_hbm,
     down_hbm,
-    down_other_hbm,
+    down_quarter_hbm,
     sum_ref,
     out_part_ref,
     gate_total_ref,
@@ -170,7 +170,7 @@
         return pl.ds(pl.multiple_of(which * half, half), half)
 
     gate_ref, up_ref, down_ref = weights.at[0], weights.at[1], weights.at[2]
-    sources = (gate_hbm, gate_other_hbm, up_hbm, up_other_hbm, down_hbm, down_other_hbm)
+    sources = (gate_hbm, gate_other_hbm, up_hbm, up_other_hbm, down_hbm)
     loads = [
         pltpu.make_async_copy(
             source,
@@ -179,7 +179,7 @@
         )
         for i, source in enumerate(sources)
     ]
-    for copy in loads[:5]:
+    for copy in loads:
         copy.start()
 
     barrier = pltpu.get_barrier_semaphore()
@@ -230,44 +230,47 @@
 
     pl.when(col < last)(lambda: ag_copy(col, True).start())
     pl.when(col > 0)(lambda: ag_copy(col, False).start())
-    quarter_size = down_other_hbm.shape[0] // 4
-
-    def down_quarter(which):
-        return down_other_hbm.at[
-            pl.ds(pl.multiple_of(which * quarter_size, 16), quarter_size)
-        ]
-
-    def down_room(which):
-        first = pl.multiple_of(which * quarter_size, 16)
-        return weights.at[2, pl.ds(first, quarter_size), half_lanes(other)]
-
+    quarter_size = down_hbm.shape[0] // 4
     quarter = dp % 4
-    down_side = remote_copy(
-        down_quarter(quarter), down_room(quarter), down_sem.at[0], down_sem.at[1], dp=across(1)
-    )
-    down_own = pltpu.make_async_copy(down_quarter(quarter), down_room(quarter), weights_sem.at[5])
-
-    def down_core(n):
-        there = down_room(core + 2 * n)
+
+    def down_place(which, piece):
+        first = which * quarter_size + piece * (quarter_size // 2)
+        return pl.ds(pl.multiple_of(first, 16), quarter_size // 2)
+
+    def down_piece(piece):
+        return down_quarter_hbm.at[pl.ds(piece * (quarter_size // 2), quarter_size // 2)]
+
+    def down_side(piece):
         return remote_copy(
-            there, there, down_sem.at[2 + 2 * n], down_sem.at[3 + 2 * n], dp=core_partner
-        )
-
-    down_side.start()
-    down_own.start()
-    for copy in loads[:5]:
+            down_piece(piece),
+            weights.at[2, down_place(quarter, piece), half_lanes(other)],
+            down_sem.at[piece, 2],
+            down_sem.at[piece, 3],
+            dp=across(1),
+        )
+
+    def down_here(piece):
+        there = weights.at[2, down_place(quarter, piece), half_lanes(other)]
+        return pltpu.make_async_copy(down_piece(piece), there, down_sem.at[piece, 0])
+
+    def down_core(piece, n):
+        there = weights.at[2, down_place(core + 2 * n, piece), half_lanes(other)]
+        return remote_copy(
+            there,
+            there,
+            down_sem.at[piece, 4 + 2 * n],
+            down_sem.at[piece, 5 + 2 * n],
+            dp=core_partner,
+        )
+
+    for piece in range(2):
+        down_side(piece).start()
+        down_here(piece).start()
+    for copy in loads[:4]:
         copy.wait()
-    down_own.wait()
-    down_side.wait_recv()
-    for n in range(2):
-        down_core(n).start()
-    for n in range(2):
-        down_core(n).wait()
-    down_side.wait_send()
-
-    def compute(block):
+
+    def products(block):
         tokens = expert_in[block]
-        grads = cot_ref[block]
         table = table_ref[block]
         experts = table.shape[1]
         units = width // experts
@@ -275,7 +278,6 @@
             cols = slice(g * half, (g + 1) * half)
             gate = dot(tokens, gate_ref[cols, :], 1, 1)
             up = dot(tokens, up_ref[cols, :], 1, 1)
-            grad = dot(grads, down_ref[cols, :], 1, 1)
             lane = lax.broadcasted_iota(jnp.int32, gate.shape, 1)
             first = g * experts // 2
             chosen = jnp.broadcast_to(table[:, first : first + 1], gate.shape)
@@ -283,12 +285,18 @@
                 chosen = jnp.where(lane >= e * units, table[:, first + e : first + e + 1], chosen)
             sigmoid = 1.0 / (1.0 + jnp.exp(-gate))
             silu = gate * sigmoid
-            grad = grad * chosen
-            hidden[block, :, cols] = (silu * up * chosen).astype(low)
-            gate_grad[block, :, cols] = (
-                grad * up * (sigmoid * (1.0 + gate * (1.0 - sigmoid)))
-            ).astype(low)
-            up_grad[block, :, cols] = (grad * silu).astype(low)
+            up = up * chosen
+            hidden[block, :, cols] = (silu * up).astype(low)
+            gate_grad[block, :, cols] = (up * (sigmoid * (1.0 + gate * (1.0 - sigmoid)))).astype(low)
+            up_grad[block, :, cols] = (silu * chosen).astype(low)
+
+    def gradients(block):
+        grads = cot_ref[block]
+        for g in range(2):
+            cols = slice(g * half, (g + 1) * half)
+            grad = dot(grads, down_ref[cols, :], 1, 1)
+            gate_grad[block, :, cols] = (grad * gate_grad[block, :, cols].astype(full)).astype(low)
+            up_grad[block, :, cols] = (grad * up_grad[block, :, cols].astype(full)).astype(low)
         gates_now, ups_now = gate_grad[block], up_grad[block]
         for part in range(2):
             cols = slice(part * half, (part + 1) * half)
@@ -298,27 +306,62 @@
             pl.when((col == last) & (block != col))(lambda: rs_copy(block, part, False).start())
         out_part_ref[block] = dot(hidden[block], down_ref[...]).astype(low)
 
-    def step(i, carry):
-        apart = (i + 1) // 2
-        from_left = i % 2 == 1
-
-        @pl.when(from_left & (col - apart >= 0))
+    def block_of(i):
+        return jnp.where(i % 2 == 1, col - (i + 1) // 2, col + (i + 1) // 2)
+
+    def pass_on(apart):
+        @pl.when(col - apart >= 0)
         def _():
-            block = col - apart
-            ag_copy(block, True).wait_recv()
-            pl.when(col < last)(lambda: ag_copy(block, True).start())
-
-        @pl.when(from_left & (col + apart <= last))
+            ag_copy(col - apart, True).wait_recv()
+            pl.when(col < last)(lambda: ag_copy(col - apart, True).start())
+
+        @pl.when(col + apart <= last)
         def _():
-            block = col + apart
-            ag_copy(block, False).wait_recv()
-            pl.when(col > 0)(lambda: ag_copy(block, False).start())
-
-        block = jnp.where(from_left, col - apart, col + apart)
-        pl.when((block >= 0) & (block <= last))(lambda: compute(block))
+            ag_copy(col + apart, False).wait_recv()
+            pl.when(col > 0)(lambda: ag_copy(col + apart, False).start())
+
+    def present(block):
+        return (block >= 0) & (block <= last)
+
+    def near_products(i, carry):
+        pl.when(i == 1)(lambda: pass_on(1))
+        pl.when(present(block_of(i)))(lambda: products(block_of(i)))
         return carry
 
-    lax.fori_loop(0, 2 * last + 1, step, 0)
+    lax.fori_loop(0, 3, near_products, 0)
+    for piece in range(2):
+        down_here(piece).wait()
+        down_side(piece).wait_recv()
+        for n in range(2):
+            down_core(piece, n).start()
+    loads[4].wait()
+    for piece in range(2):
+        for n in range(2):
+            down_core(piece, n).wait_recv()
+
+    def near_gradients(n, carry):
+        i = (n + 1) % 3
+        pl.when(i == 0)(lambda: pass_on(2))
+        pl.when(present(block_of(i)))(lambda: gradients(block_of(i)))
+        return carry
+
+    lax.fori_loop(0, 3, near_gradients, 0)
+
+    def far_blocks(i, carry):
+        pl.when(i == 5)(lambda: pass_on(3))
+
+        @pl.when(present(block_of(i)))
+        def _():
+            products(block_of(i))
+            gradients(block_of(i))
+
+        return carry
+
+    lax.fori_loop(3, 2 * last + 1, far_blocks, 0)
+    for piece in range(2):
+        down_side(piece).wait_send()
+        for n in range(2):
+            down_core(piece, n).wait_send()
 
     greet(ready.at[0], dp=core_partner)
     greet(ready.at[1], row=other)
@@ -330,16 +373,15 @@
             which, pl.ds(down * half, half), pl.ds(right * half, half)
         ]
 
-    def forward(block, right):
-        for part in range(2):
-            rs_wait(block, part)
-            send_stage[block, part] = add_low(send_stage[block, part], arrived[block, part])
-            rs_copy(block, part, right).start()
-
-    def event(number):
+    def forward(block, part, right):
+        rs_wait(block, part)
+        send_stage[block, part] = add_low(send_stage[block, part], arrived[block, part])
+        rs_copy(block, part, right).start()
+
+    def event(number, part):
         blocks = ((2, 1), (3, 0), (0, 3))[number]
-        pl.when(col == 1)(lambda: forward(blocks[0], number < 2))
-        pl.when(col == 2)(lambda: forward(blocks[1], number == 2))
+        pl.when(col == 1)(lambda: forward(blocks[0], part, number < 2))
+        pl.when(col == 2)(lambda: forward(blocks[1], part, number == 2))
 
     def core_copy(at):
         if at < 4:
@@ -430,10 +472,10 @@
         here = chunk_rows(chunk)
         landed = weights.at[0, pl.ds(half + chunk * size, size), pl.ds(0, half)]
         parts[1, here] = add_low(parts[1, here], landed[...])
+        if chunk == 0 and sides:
+            for number in range(sides):
+                pl.semaphore_wait(ready.at[2 + number], 1)
         if sides:
-            if chunk == 0:
-                for number in range(sides):
-                    pl.semaphore_wait(ready.at[2 + number], 1)
             side_copy(chunk, 0).start()
 
     def final_copies(chunk):
@@ -472,28 +514,34 @@
 
     pl.semaphore_wait(ready.at[0], 1)
     core_dot(0)
-    event(0)
-    core_dot(1)
+    event(0, 0)
     core_sum(0)
     pl.semaphore_wait(ready.at[1], 1)
     row_copy(0).start()
+    event(0, 1)
+    core_dot(1)
+    core_sum(1)
     core_dot(2)
-    core_sum(1)
+    event(1, 0)
+    core_dot(3)
     core_sum(2)
     up_rest.start()
-    core_dot(3)
-    event(1)
+    core_sum(3)
+    up_out.start()
+    event(1, 1)
+    event(2, 0)
+    after_row(0)
+    row_copy(1).start()
     pl.when(col == 0)(lambda: out_copy(True).start())
     pl.when(col == last)(lambda: out_copy(False).start())
     down_dot_partner()
-    after_row(0)
-    row_copy(1).start()
-    core_sum(3)
-    up_out.start()
-    event(2)
+    event(2, 1)
     down_dot_own()
     down_sum()
     down_out.start()
+    after_row(1)
+    row_copy(2).start()
+    after_side(0)
 
     for part in range(2):
         sum_ref[part] = send_stage[col, part].astype(full)
@@ -508,9 +556,6 @@
             rs_wait(last + 1, part)
             sum_ref[part] += arrived[last + 1, part].astype(full)
 
-    after_row(1)
-    row_copy(2).start()
-    after_side(0)
     after_side(1)
 
     for block in range(last + 1):
@@ -528,9 +573,8 @@
     for copy in (down_out, up_out, up_rest):
         copy.wait()
     for chunk in range(2):
-        remote, local = final_copies(chunk)
-        remote.wait()
-        local.wait()
+        for copy in final_copies(chunk):
+            copy.wait()
 
 
 def experts_call(own, cot, table, *halves):
@@ -562,8 +606,8 @@
             pltpu.VMEM((blocks + 1, 2, rows, half), low),
             pltpu.VMEM((4, half, half), low),
             pltpu.VMEM((2, half, half), low),
-            dma((6,)),
-            dma((6,)),
+            dma((5,)),
+            dma((2, 8)),
             pltpu.SemaphoreType.REGULAR((2 + max(sides, 1),)),
             dma((blocks,)),
             dma((blocks,)),
@@ -604,25 +648,34 @@
     gate_hbm,
     up_hbm,
     down_hbm,
-    normed_ref,
+    normed_hbm,
     scale_ref,
     gains_ref,
-    key_ref,
-    value_ref,
+    key_hbm,
+    value_hbm,
     cosine_ref,
     sine_ref,
     start_ref,
-    attended_ref,
-    rot_ref,
-    joint_ref,
-    head_output_ref,
+    logsum_ref,
+    attended_hbm,
+    rot_hbm,
+    joint_hbm,
+    head_output_hbm,
     middle_ref,
     expert_ref,
     table_ref,
     cot_all_ref,
     gate_all_ref,
     up_all_ref,
-    down_all_ref,
+    down_quarter_ref,
+    normed_ref,
+    key_ref,
+    value_ref,
+    attended_ref,
+    rot_ref,
+    joint_ref,
+    head_output_ref,
+    store_sem,
     inputs_all,
     inputs_sem,
     small,
@@ -883,17 +936,9 @@
             cot_copy(col + apart, False).wait_recv()
             pl.when(col > 0)(lambda: cot_copy(col + apart, False).start())
 
-    joint.load()
-    output.load()
-    pl.semaphore_wait(barrier, cols + 2)
-    joint.first()
-    small_copy.start()
-    inputs_copy.start()
-    cot_row.start()
-
-    expert_size = down_hbm.shape[0] // 4
-    weights = (gate_hbm, up_hbm, down_hbm)
-    totals = (gate_all_ref, up_all_ref, down_all_ref)
+    expert_size = gate_hbm.shape[0] // 4
+    weights = (gate_hbm, up_hbm)
+    totals = (gate_all_ref, up_all_ref)
 
     def expert_region(which, of_quarter):
         first = pl.multiple_of(of_quarter * expert_size, 16)
@@ -906,6 +951,16 @@
             expert_region(which, quarter),
             expert_row.at[which, 0],
             expert_row.at[which, 1],
+            row=other,
+        )
+
+    def down_row_copy():
+        first = pl.multiple_of(quarter * expert_size, 16)
+        return remote_copy(
+            down_hbm.at[pl.ds(first, expert_size)],
+            down_quarter_ref,
+            expert_row.at[2, 0],
+            expert_row.at[2, 1],
             row=other,
         )
 
@@ -939,6 +994,25 @@
         for copy in expert_core_copies(which):
             copy.start()
 
+    store_pairs = (
+        (normed_ref, normed_hbm),
+        (key_ref, key_hbm),
+        (value_ref, value_hbm),
+        (attended_ref, attended_hbm),
+        (rot_ref, rot_hbm),
+        (joint_ref, joint_hbm),
+        (head_output_ref, head_output_hbm),
+    )
+    stores = [
+        pltpu.make_async_copy(source, target, store_sem.at[n])
+        for n, (source, target) in enumerate(store_pairs)
+    ]
+    joint.load()
+    output.load()
+    pl.semaphore_wait(barrier, cols + 2)
+    joint.first()
+    small_copy.start()
+    cot_row.start()
     cot_all_ref[col, :, part_lanes(row)] = cot_ref[token_rows(row), :]
 
     for at in range(cols):
@@ -949,13 +1023,7 @@
         for k in range(chosen.shape[0]):
             table += jnp.where(chosen[k : k + 1, :] == expert, gates[k : k + 1, :], 0.0)
         table_ref[at] = jnp.transpose(table)
-
     joint.step(1)
-    joint.step(2)
-    joint.step(3)
-    output.first()
-    joint.from_row()
-    cot_first()
 
     small_copy.wait_recv()
     gains_ref[:, :part_width] = small[0, 0:2, :]
@@ -970,12 +1038,18 @@
         begin = jnp.where(place >= total, total, begin)
         total = total + lens[:, n : n + 1]
     start_ref[...] = begin + (1.0 - odd) * tokens
+    cot_first()
+    inputs_copy.start()
     angles = (place - begin) * theta_ref[...]
     cosine_ref[...] = jnp.cos(angles)
     sine = jnp.sin(angles)
     lane = lax.broadcasted_iota(jnp.int32, sine.shape, 1)
     sine_ref[...] = jnp.where(lane < head_dim // 2, -sine, sine)
 
+    joint.step(2)
+    joint.step(3)
+    output.first()
+    joint.from_row()
     output.step(1)
     inputs_copy.wait_recv()
     expert_row_copy(0).start()
@@ -993,23 +1067,24 @@
         return carry
 
     lax.fori_loop(0, tokens // piece, norm_piece, 0)
+    joint.to_core()
     output.step(2)
-    joint.to_core()
-    output.step(3)
+    cot_pass(1)
     joint.ready()
-
-    projected[...] = dot(normed_ref[...], joint_ref[...])
-    own = slice(tokens, 2 * tokens)
-    key = projected[:, query_block : query_block + head_dim]
+    stores[0].start()
+    stores[5].start()
+
+    own = pl.ds(tokens, tokens)
+    key = dot(normed_ref[...], joint_ref[:, query_block:block])
     key_ref[own, :] = (
         key * cosine_ref[...] + pltpu.roll(key, head_dim // 2, 1) * sine_ref[...]
     ).astype(low)
-    value_ref[own, :] = projected[:, block + query_block : block + query_block + head_dim].astype(low)
+    value_ref[own, :] = dot(normed_ref[...], joint_ref[:, block + query_block :]).astype(low)
 
     def pair_copies():
         return [
             remote_copy(
-                ref.at[pl.ds(tokens, tokens)],
+                ref.at[own],
                 ref.at[pl.ds(0, tokens)],
                 pair_sem.at[n, 0],
                 pair_sem.at[n, 1],
@@ -1025,9 +1100,15 @@
         key_ref[:tokens, :] = jnp.zeros((tokens, head_dim), low)
         value_ref[:tokens, :] = jnp.zeros((tokens, head_dim), low)
 
+    for b in range(2):
+        lanes = slice(b * query_block, (b + 1) * query_block)
+        projected[:, lanes] = dot(
+            normed_ref[...], joint_ref[:, b * block : b * block + query_block]
+        )
+    output.step(3)
+    output.from_row()
+    expert_after_row(0)
     expert_row_copy(1).start()
-    output.from_row()
-    cot_pass(1)
     output.to_core()
 
     @pl.when(col % 2 == 1)
@@ -1036,37 +1117,43 @@
             copy.wait_recv()
 
     heads = 2 * query_block // head_dim
-    per_block = heads // 2
-    tile = tokens // 2
+    tile = rows
     window = key_ref.shape[0] - tile
 
-    def head_step(head, carry):
-        here = pl.ds(pl.multiple_of(head * head_dim, head_dim), head_dim)
-        there = pl.ds(
-            pl.multiple_of((head + head // per_block) * head_dim, head_dim), head_dim
-        )
-        pre = projected[:, there]
-        rot = (pre * cosine_ref[...] + pltpu.roll(pre, head_dim // 2, 1) * sine_ref[...]).astype(low)
-        rot_ref[:, here] = rot
-        for at in range(tokens // tile):
-            first = at * tile
-            keys = key_ref[first : first + window, :]
-            values = value_ref[first : first + window, :]
-            scores = dot(rot[first : first + tile], keys, 1, 1) * head_dim ** (-0.5)
+    def attend(which):
+        first = which * tile
+        here = pl.ds(pl.multiple_of(first, 16), tile)
+        reach = pl.ds(pl.multiple_of(first, 16), window)
+
+        def head_step(head, carry):
+            lanes = pl.ds(pl.multiple_of(head * head_dim, head_dim), head_dim)
+            pre = projected[here, lanes]
+            rot = (
+                pre * cosine_ref[here, :] + pltpu.roll(pre, head_dim // 2, 1) * sine_ref[here, :]
+            ).astype(low)
+            rot_ref[here, lanes] = rot
+            scores = dot(rot, key_ref[reach, :], 1, 1) * head_dim ** (-0.5)
             key_place = lax.broadcasted_iota(jnp.int32, scores.shape, 1) + first
             query_place = lax.broadcasted_iota(jnp.int32, scores.shape, 0) + (first + tokens)
             allowed = (key_place <= query_place) & (
-                key_place.astype(full) >= start_ref[first : first + tile, :]
+                key_place.astype(full) >= start_ref[here, :]
             )
             scores = jnp.where(allowed, scores, -1e30)
-            exponent = jnp.exp(scores - jnp.max(scores, axis=1, keepdims=True))
-            weights = exponent / jnp.sum(exponent, axis=1, keepdims=True)
-            attended_ref[first : first + tile, here] = dot(weights.astype(low), values).astype(low)
-        return carry
-
-    lax.fori_loop(0, heads, head_step, 0)
-
-    expert_after_row(0)
+            most = jnp.max(scores, axis=1, keepdims=True)
+            exponent = jnp.exp(scores - most)
+            total = jnp.sum(exponent, axis=1, keepdims=True)
+            weights = exponent / total
+            attended_ref[here, lanes] = dot(weights.astype(low), value_ref[reach, :]).astype(low)
+            lane = lax.broadcasted_iota(jnp.int32, (tile, head_dim), 1)
+            logsum_ref[here, :] = jnp.where(
+                lane == head, most + jnp.log(total), logsum_ref[here, :]
+            )
+            return carry
+
+        lax.fori_loop(0, heads, head_step, 0)
+
+    logsum_ref[...] = jnp.zeros_like(logsum_ref)
+    attend(other)
     output.ready()
 
     def branch_copy(part):
@@ -1083,10 +1170,12 @@
         lanes = slice(part * part_width, (part + 1) * part_width)
         branch_stage[part] = dot(theirs, head_output_ref[:, lanes]).astype(low)
         branch_copy(part).start()
-    expert_row_copy(2).start()
     cot_pass(2)
+    attend(row)
     mine = attended_ref[token_rows(row), :]
     branch_own[...] = dot(mine, head_output_ref[...])
+    for n in (1, 2, 3, 4, 6):
+        stores[n].start()
     expert_after_row(1)
     expert_after_side(0)
     for part in range(2):
@@ -1098,6 +1187,8 @@
             + branch_arrived[part].astype(full)
         )
 
+    down_row_copy().start()
+
     def second_piece(at, carry):
         here = pl.ds(pl.multiple_of(at * piece, piece), piece)
         values = middle_ref[here, :]
@@ -1106,18 +1197,18 @@
         return carry
 
     lax.fori_loop(0, rows // piece, second_piece, 0)
+    cot_pass(3)
     expert_after_side(1)
-    cot_pass(3)
 
     inputs_copy.wait_send()
     small_copy.wait_send()
     joint.end()
     output.end()
-    for which in range(3):
+    for copy in stores:
+        copy.wait()
+    down_row_copy().wait()
+    for which in range(2):
         expert_row_copy(which).wait_send()
-        if which == 2:
-            expert_row_copy(which).wait_recv()
-            continue
         expert_side_copy(which).wait_send()
         for copy in expert_core_copies(which):
             copy.wait()
@@ -1144,7 +1235,7 @@
     width, rows = 2 * part_width, tokens // 2
     query_block, keyval_block = query_weight.shape[1], key_value_matrix.shape[1]
     block = query_block + keyval_block
-    hidden = down_flat.shape[0]
+    hidden = gate_flat.shape[0]
     vmem = pl.BlockSpec(memory_space=pltpu.VMEM)
     anywhere = pl.BlockSpec(memory_space=pl.ANY)
     dma = pltpu.SemaphoreType.DMA
@@ -1152,7 +1243,13 @@
     return pl.pallas_call(
         functools.partial(prologue_kernel, sequences=sequences),
         in_specs=[vmem] * 6 + [anywhere] * 6,
-        out_specs=[vmem] * 16 + [anywhere] * 3,
+        out_specs=[anywhere]
+        + [vmem] * 2
+        + [anywhere] * 2
+        + [vmem] * 4
+        + [anywhere] * 4
+        + [vmem] * 4
+        + [anywhere] * 3,
         out_shape=[
             shape((tokens, width), low),
             shape((tokens, 1), full),
@@ -1162,6 +1259,7 @@
             shape((tokens, head_dim), full),
             shape((tokens, head_dim), full),
             shape((tokens, 1), full),
+            shape((tokens, head_dim), full),
             shape((tokens, 2 * query_block), low),
             shape((tokens, 2 * query_block), low),
             shape((width, 2 * block), low),
@@ -1172,14 +1270,22 @@
             shape((cols, rows, width), low),
             shape((hidden, part_width), low),
             shape((hidden, part_width), low),
-            shape((hidden, part_width), low),
+            shape((hidden // 4, part_width), low),
         ],
         scratch_shapes=[
+            pltpu.VMEM((tokens, width), low),
+            pltpu.VMEM((2 * tokens, head_dim), low),
+            pltpu.VMEM((2 * tokens, head_dim), low),
+            pltpu.VMEM((tokens, 2 * query_block), low),
+            pltpu.VMEM((tokens, 2 * query_block), low),
+            pltpu.VMEM((width, 2 * block), low),
+            pltpu.VMEM((2 * query_block, width), low),
+            dma((7,)),
             pltpu.VMEM((tokens, width), low),
             dma((2,)),
             pltpu.VMEM((2,) + small.shape, full),
             dma((2,)),
-            pltpu.VMEM((tokens, 2 * block), full),
+            pltpu.VMEM((tokens, 2 * query_block), full),
             pltpu.VMEM((rows, width), full),
             pltpu.VMEM((2, rows, part_width), low),
             pltpu.VMEM((2, rows, part_width), low),
@@ -1198,8 +1304,8 @@
             dma((4, 2)),
             dma((4, 4)),
             dma((3, 2)),
-            dma((3, 2)),
-            dma((3, 4)),
+            dma((2, 2)),
+            dma((2, 4)),
             dma((2,)),
             dma((cols,)),
             dma((cols, 2)),
@@ -1221,6 +1327,7 @@
     gains_ref,
     scale_ref,
     start_ref,
+    logsum_ref,
     sum_hbm,
     inputs_hbm,
     attended_hbm,
@@ -1383,7 +1490,7 @@
     pl.when(inner_col)(lambda: first_load.start())
     for copy in item_loads(1) + load[3:]:
         copy.start()
-    for at in (2, 3, 0):
+    for at in (0, 2, 3):
         for copy in item_loads(at):
             copy.start()
 
@@ -1447,7 +1554,7 @@
 
     def item_first_copies(at):
         if at == 0:
-            pairs = [(item_mine.at[0], item_side.at[0])]
+            pairs = [(item_mine.at[at], item_side.at[at])]
         else:
             there = side_rows(1 - side)
             pairs = [
@@ -1566,10 +1673,10 @@
 
     def item_finish(at):
         if at == 0:
-            for copy in item_first_copies(0):
+            for copy in item_first_copies(at):
                 copy.wait()
-            item_mine[0] = add_low(item_mine[0], item_side[0])
-            item_further(0)
+            item_mine[at] = add_low(item_mine[at], item_side[at])
+            item_further(at)
         else:
             item_last_copy(at).wait_recv()
         for copy in item_core_copies(at):
@@ -1636,8 +1743,13 @@
             query = lax.broadcasted_iota(jnp.int32, scores.shape, 0) + (first + tokens)
             allowed = (place <= query) & (place.astype(full) >= start_ref[first : first + tile, :])
             scores = jnp.where(allowed, scores, -1e30)
-            exponent = jnp.exp(scores - jnp.max(scores, axis=1, keepdims=True))
-            probs = exponent / jnp.sum(exponent, axis=1, keepdims=True)
+            lane = lax.broadcasted_iota(jnp.int32, (tile, head_dim), 1)
+            logsum = jnp.sum(
+                jnp.where(lane == head, logsum_ref[first : first + tile, :], 0.0),
+                axis=1,
+                keepdims=True,
+            )
+            probs = jnp.exp(scores - logsum)
             prob_grad = dot(grad, values, 1, 1)
             inner = jnp.sum(probs * prob_grad, axis=1, keepdims=True)
             score_grad = (probs * (prob_grad - inner) * head_dim ** (-0.5)).astype(low)
@@ -2021,7 +2133,7 @@
 
 
 def finish_call(
-    middle, gains, scale, start, sums, inputs, attended, rot, keys, values, cosine, sine,
+    middle, gains, scale, start, logsum, sums, inputs, attended, rot, keys, values, cosine, sine,
     head_output, joint_weight, normed, cot_all, out_part, up_own, up_row, up_other, down_half, out_first,
     query_block, both_block,
 ):
@@ -2044,7 +2156,7 @@
     sums_count = 2 * cols - 1 + dps - 1
     return pl.pallas_call(
         finish_kernel,
-        in_specs=[vmem] * 4 + [anywhere] * 18,
+        in_specs=[vmem] * 5 + [anywhere] * 18,
         out_specs=[vmem] * 6 + [anywhere] * 3,
         out_shape=[
             shape((tokens, part_width), low),
@@ -2136,9 +2248,32 @@
             flops=10 * 10**9, bytes_accessed=40 * 10**6, transcendentals=4 * 10**6
         ),
     )(
-        middle, gains, scale, start, sums, inputs, attended, rot, keys, values, cosine, sine,
+        middle, gains, scale, start, logsum, sums, inputs, attended, rot, keys, values, cosine, sine,
         head_output, joint_weight, normed, cot_all, out_part, up_own, up_row, up_other, down_half, out_first,
     )
+
+
+def results_kernel(*refs):
+    count = len(refs) // 2
+    for source, target in zip(refs[:count], refs[count:]):
+        target[...] = source[...].astype(target.dtype)
+
+
+def results_call(arrays, kinds, steps):
+    specs = [
+        pl.BlockSpec((array.shape[0] // steps, array.shape[1]), lambda i: (i, 0))
+        for array in arrays
+    ]
+    return pl.pallas_call(
+        results_kernel,
+        grid=(steps,),
+        in_specs=specs,
+        out_specs=specs,
+        out_shape=[
+            jax.ShapeDtypeStruct(array.shape, kind) for array, kind in zip(arrays, kinds)
+        ],
+        compiler_params=pltpu.CompilerParams(vmem_limit_bytes=60 * 2**20),
+    )(*arrays)
 
 
 def shards(
@@ -2179,6 +2314,7 @@
         cosine,
         sine,
         start,
+        logsum,
         attended,
         rot,
         joint_weight,
@@ -2189,13 +2325,22 @@
         cot_all,
         gate_other,
         up_other_half,
-        down_other,
+        down_quarter,
     ) = prologue_call(
         inputs, small, theta, routes.T, route_gates.T, cotangent, query_weight, key_value_matrix,
         output_weight, gate_flat, up_flat, down_flat, sequences, experts,
     )
-    second_grad, out_part, gate_total, up_own, up_row, up_other, down_half, out_first = experts_call(
-        expert_own, cot_all, tables, gate_flat, gate_other, up_flat, up_other_half, down_flat, down_other
+    (
+        second_grad,
+        out_part,
+        gate_total,
+        up_own,
+        up_row,
+        up_other,
+        down_half,
+        out_first,
+    ) = experts_call(
+        expert_own, cot_all, tables, gate_flat, gate_other, up_flat, up_other_half, down_flat, down_quarter
     )
 
     both_block = query_block + keyval_block
@@ -2210,19 +2355,30 @@
         down_total,
         _,
     ) = finish_call(
-        middle, gains, first_scale, start, second_grad, inputs, attended, rot, keys, values,
-        cosine, sine, head_output, joint_weight, normed, cot_all, out_part, up_own, up_row,
-        up_other, down_half, out_first, query_block, both_block,
+        middle, gains, first_scale, start, logsum, second_grad, inputs, attended, rot, keys, values,
+        cosine, sine, head_output, joint_weight, normed, cot_all, out_part,
+        up_own, up_row, up_other, down_half, out_first, query_block, both_block,
     )
     norm_total, mixer_total = gain_sums[0], gain_sums[1]
 
+    arrays = [gate_total, up_total, down_total, query_total, keyval_total, output_total]
+    (
+        gate_total,
+        up_total,
+        down_total,
+        query_total,
+        keyval_total,
+        output_total,
+        outputs,
+        input_grad,
+    ) = results_call(arrays + [outputs, input_grad], [full] * 6 + [low] * 2, 8)
+
     def by_expert(flat):
-        return flat.astype(full).reshape(experts, units, part_width).swapaxes(1, 2)
-
-    gate_total, up_total = by_expert(gate_total), by_expert(up_total)
-    down_total = down_total.reshape(experts, units, part_width).astype(full)
-    output_total = output_total.astype(full)
-    query_total, keyval_total = query_total.astype(full), keyval_total.astype(full)
+        return flat.reshape(experts, units, part_width)
+
+    gate_total = by_expert(gate_total).swapaxes(1, 2)
+    up_total = by_expert(up_total).swapaxes(1, 2)
+    down_total = by_expert(down_total)
     return (
         outputs,
         input_grad,

time: 414 us -> 388 us (0.937)
  other arithmetic: 14.8 us -> 1.26 us
  Pallas kernels: 385 us -> 377 us
  local copies, waits for them, and re-layouts: 6.8 us -> 2.17 us
    pallas_call x1, Pallas kernels: 119 us -> 104 us  [prologue_call(): pl.pallas_call(functools.partial(prologue_kernel, sequences=sequences), i...]
    convert_element_type x4 -> x0, other arithmetic: 8.83 us -> none  [the longest x1 2.82 us: shards(): down_total = down_total.reshape(experts, units, part_width).astype(full)]
    pallas_call x1 -> x2, Pallas kernels: 135 us -> 143 us  [the longest x1 132 us: finish_call(): pl.pallas_call(finish_kernel, in_specs=[vmem] * 5 + [anywhere] * 18, out_...]
    transpose x1 -> x0, other arithmetic: 4.76 us -> none  [by_expert(): return flat.astype(full).reshape(experts, units, part_width).swapaxes(1, 2)]
where the time goes in v6:
time: 388 us; the launch traced here: 381 us
  Pallas kernels  377 us (97%)
    pallas_call x1, Pallas kernels, finish_call(): pl.pallas_call(finish_kernel, in_specs=[vmem] * 5 + [anywhere] * 18, out_...  132 us
    pallas_call x1, Pallas kernels, experts_call(): pl.pallas_call(experts_kernel, in_specs=[vmem] * 3 + [anywhere] * 6, out_...  130 us
    pallas_call x1, Pallas kernels, prologue_call(): pl.pallas_call(functools.partial(prologue_kernel, sequences=sequences), i...  104 us
    pallas_call x1, Pallas kernels, results_call(): pl.pallas_call(results_kernel, grid=(steps,), in_specs=specs, out_specs=s...  11.2 us

profile of v6, /device:TPU:17, one launch (start us, length us, event | category | flops | bytes accessed | tf_op | source)
XLA Modules:
  0.0 381.1 jit_solution(1858381438817700688)
XLA Ops:
  0.6 0.7 reshape.117
  1.3 0.7 reshape.118
  2.1 0.7 convert_element_type.4
  2.7 0.1 scatter.14.small_ref
  2.9 0.0 copy-start
  2.9 0.6 maximum_bitcast_fusion.theta_ref
  3.5 0.0 copy-done
  3.5 104.1 %shard_map.204 = (bf16[512,1536]{1,0:T(8,128)(2,1)}, f32[512,1]{1,0:T(8,128)}, f32[2,1536]{1,0:T(2,128)}, bf16[1024,128]{1,0:T(8,128)(2,1)}, bf16[1024,128]{1,0:...) custom-call(bf16[512,768]{1,0:T(8,128)(2,1)} %inputs_hbm.1, ...), custom_call_target="tpu_custom_call" | custom-call | flops 5000000000 | bytes 30000000 | tf_op jit(solution)/shard_map/pallas_call | solution.py:1243
  107.6 129.8 %shard_map.205 = (f32[2,256,768]{2,1,0:T(8,128)}, bf16[4,256,1536]{2,1,0:T(8,128)(2,1)}, bf16[1536,768]{1,0:T(8,128)(2,1)}, bf16[768,768]{1,0:T(8,128)(2,1)}, bf...) custom-call(bf16[256,1536]{1,0:T(8,128)(2,1)} %get-tuple-element.90.ow, ...), custom_call_target="tpu_custom_call" | custom-call | flops 43486543872 | bytes 28311552 | tf_op jit(solution)/shard_map/pallas_call | solution.py:588
  237.4 131.6 %shard_map.206 = (bf16[512,768]{1,0:T(8,128)(2,1)}, bf16[512,768]{1,0:T(8,128)(2,1)}, f32[2,768]{1,0:T(2,128)}, bf16[384,768]{1,0:T(8,128)(2,1)}, bf16[768,384]{...) custom-call(f32[256,1536]{1,0:T(8,128)} %get-tuple-element.97.middle, ...), custom_call_target="tpu_custom_call" | custom-call | flops 10000000000 | bytes 40000000 | tf_op jit(solution)/shard_map/pallas_call | solution.py:2157
  369.0 0.0 copy-start.1
  369.0 11.2 %shard_map.207 = (f32[1536,768]{1,0:T(8,128)}, f32[1536,768]{1,0:T(8,128)}, f32[1536,768]{1,0:T(8,128)}, f32[768,384]{1,0:T(8,128)}, f32[768,128]{1,0:T(8,128)},...) custom-call(bf16[1536,768]{1,0:T(8,128)(2,1)} %get-tuple-element.96.refs_0_, ...), custom_call_target="tpu_custom_call" | custom-call | tf_op jit(solution)/shard_map/pallas_call | solution.py:2267
  380.2 0.0 copy-done.1
  380.3 0.6 slice_reduce_fusion
  (3 shorter events, 0.1 us)
Async XLA Ops:
  2.9 0.6 copy-start
  369.0 11.2 %copy-start.1 = (f32[2,768]{1,0:T(2,128)S(1)}, f32[2,768]{1,0:T(2,128)}, u32[]{:S(2)}) copy-start(f32[2,768]{1,0:T(2,128)} %get-tuple-element.127) | copy-start | bytes 18436
